TPU v7x, 256 devices: a whole 4x4x8 slice. The times are simulated.
256 devices in a mesh: ingest: 64 (over y, z, core), span: 4 (over x).
Axes of the slice: x: 4, y: 4, z: 8, core: 2. Of those that a mesh axis runs over, the one named last changes fastest.
Arguments:
- embeddings: bfloat16 [131072, 1024], P(('ingest', 'span')), may hold values from -6 to 6
- owner: int32 [131072, 1], P(('ingest', 'span')), may hold values from 0 to 63; in each aligned block of 512 rows (0 to 511, 512 to 1023, ...) at most 16 rows name the same one
- cluster: int32 [131072], P(('ingest', 'span')), may hold values from 0 to 63
Outputs:
- max_similarity: float32 [131072], P(('ingest', 'span'))
Inputs may be any that keep to these rules, and one draw needn't show every extreme that they name: Among the rows of one device, at most 16 name the same owner group, and some device has exactly 16 for some group.
All inputs are finite; a program needn't handle non-finite values.
Results may differ from a plain program's by a relative error of at most 0.0013.
Values may be sent and summed in bfloat16 or wider, within the bound.
No kernel may reach another device: no remote copies, remote signals or barrier semaphores. Data moves between devices by JAX's collectives and lax.ppermute only.
A program may use at most 64 MiB of HBM per device.

v0:
```python
import jax
import jax.numpy as jnp
from jax import lax
from jax.sharding import PartitionSpec as P

epsilon = 1e-06


def place_rows(target, groups, capacity):
    onehot = (target[:, None] == jnp.arange(groups, dtype=jnp.int32)[None, :]).astype(jnp.int32)
    within = jnp.sum((jnp.cumsum(onehot, axis=0) - onehot) * onehot, axis=1)
    return target * capacity + within


def shards(embeddings, owner, cluster):
    rows_dev = embeddings.shape[0]
    width = embeddings.shape[1]
    groups = lax.axis_size("ingest")
    capacity = 2 * rows_dev // groups
    values = embeddings.astype(jnp.float32)
    squared = jnp.sum(values * values, axis=1, keepdims=True)
    unit = (values * lax.rsqrt(squared + epsilon)).astype(jnp.bfloat16)
    slot_index = place_rows(owner[:, 0], groups, capacity)
    send_rows = jnp.zeros((groups * capacity, width), jnp.bfloat16).at[slot_index].set(unit)
    send_ids = (
        jnp.full((groups * capacity,), -1.0, jnp.bfloat16)
        .at[slot_index]
        .set(cluster.astype(jnp.bfloat16))
    )
    owned_rows, owned_ids = (
        lax.all_to_all(send_rows, "ingest", split_axis=0, concat_axis=0, tiled=True),
        lax.all_to_all(send_ids, "ingest", split_axis=0, concat_axis=0, tiled=True),
    )
    slots_dev = owned_rows.shape[0]
    span_place = lax.axis_index("span")
    own_position = span_place * slots_dev + jnp.arange(slots_dev, dtype=jnp.int32)
    part_rows = lax.all_gather(owned_rows, "span", axis=0, tiled=True)
    part_ids = lax.all_gather(owned_ids, "span", axis=0, tiled=True)
    count = part_rows.shape[0]
    scores = jnp.einsum("md,kd->mk", owned_rows, part_rows, preferred_element_type=jnp.float32)
    position = jnp.arange(count, dtype=jnp.int32)
    same_cluster = (owned_ids[:, None] == part_ids[None, :]) & (owned_ids[:, None] >= 0)
    same_cluster = same_cluster & (own_position[:, None] != position[None, :])
    masked = jnp.where(same_cluster, scores, jnp.float32(-1.0))
    best_sim = jnp.maximum(jnp.full((slots_dev,), -1.0, jnp.float32), jnp.max(masked, axis=1))
    returned_all = lax.all_to_all(best_sim, "ingest", split_axis=0, concat_axis=0, tiled=True)
    return returned_all[slot_index]


def solution(mesh):
    placed = (P(("ingest", "span"), None), P(("ingest", "span"), None), P(("ingest", "span")))
    return jax.shard_map(
        shards, mesh=mesh, in_specs=placed, out_specs=P(("ingest", "span")), check_vma=False
    )
```

profile of v0, /device:TPU:1, one launch (start us, length us, event | category | flops | bytes accessed | tf_op | source)
XLA Modules:
  0.0 210.2 jit_solution(8547811511106454298)
XLA Ops:
  6.5 0.0 all-gather.2.cloned.1.call-start
  6.5 0.7 fusion.10
  7.2 1.2 reduce-window.6
  8.4 0.2 slice_reduce_fusion
  8.7 0.8 fusion.9
  9.5 0.7 compare_select_fusion
  10.2 1.5 fusion.1
  11.7 0.0 copy-start
  11.7 4.0 %scatter_custom_fusion.1 = bf16[1024,1024]{1,0:T(8,128)(2,1)S(1)} fusion(s32[512]{0:T(512)S(1)} %bitcast.35, bf16[512,1024]{1,0:T(8,128)(2,1)} %param.3, f32[512]{0:T(512)S(1)} %add_rsqrt_fusion, bf16[]{:T(256)} %constant.14.clone.1), kind=kCustom, calls=%fused_computation.10 | custom fusion | flops 1572864 | bytes 3147778 | tf_op jit(solution)/shard_map/scatter | solution.py:24
  15.7 64.3 %all_to_all.31 = bf16[64,16,1024]{2,1,0:T(8,128)(2,1)} all-to-all(bf16[64,16,1024]{2,1,0:T(8,128)(2,1)S(1)} %bitcast.31), channel_id=1, replica_groups=mesh['ingest'=64,'span'=4] {'ingest'}, dimensions={0} | all-to-all | bytes 4194304 | tf_op jit(solution)/shard_map/all_to_all | solution.py:31
  80.0 0.0 all-gather.2.cloned.1.call-update
  80.0 0.0 copy-done
  80.1 3.8 %scatter_custom_fusion = bf16[1024]{0:T(1024)(128)(2,1)S(1)} fusion(s32[512]{0:T(512)S(1)} %bitcast.36, bf16[512]{0:T(512)(128)(2,1)S(1)} %convert_element_type.18, bf16[]{:T(256)} %constant.10.clone.1), kind=kCustom, calls=%fused_computation.28 | custom fusion | bytes 2050 | tf_op jit(solution)/shard_map/scatter | solution.py:28
  83.8 0.7 all_to_all.27
  84.5 5.8 %all-to-all-start = ((bf16[64,16,1]{1,2,0:T(2,128)(2,1)}), bf16[64,16,1]{1,2,0:T(2,128)(2,1)S(1)}, u32[]{:S(2)}, u32[]{:S(2)}) async-start(bf16[64,16,1]{1,2,0:T(2,128)(2,1)} %all_to_all.27), calls=%async_computation | async-start | bytes 65536 | tf_op jit(solution)/shard_map/all_to_all | solution.py:32
  90.4 9.3 %all-to-all-done = bf16[64,16,1]{1,2,0:T(2,128)(2,1)S(1)} async-done(((bf16[64,16,1]{1,2,0:T(2,128)(2,1)}), bf16[64,16,1]{1,2,0:T(2,128)(2,1)S(1)}, u32[]{:S(2)}, u32[]{:S(2)}) %all-to-all-start) | async-done | bytes 2080 | tf_op jit(solution)/shard_map/all_to_all | solution.py:32
  99.6 0.1 reduce.1
  99.7 0.1 eq.48
  99.8 9.7 %all_gather.6 = bf16[4096]{0:T(1024)(128)(2,1)S(1)} all-gather(bf16[1024]{0:T(1024)(128)(2,1)S(1)} %eq.48), channel_id=1, replica_groups=mesh['ingest'=64,'span'=4] {'span'}, dimensions={0}, use_global_device_ids=true | all-gather | bytes 10240 | tf_op jit(solution)/shard_map/all_gather | solution.py:38
  109.5 52.9 %all-gather.2.cloned.1.call-done = bf16[4096,1024]{1,0:T(8,128)(2,1)} async-done(((bf16[1024,1024]{1,0:T(8,128)(2,1)}), bf16[4096,1024]{1,0:T(8,128)(2,1)}) %all-gather.2.cloned.1.call-update) | async-done | bytes 8388624 | tf_op jit(solution)/shard_map/all_gather | solution.py:37
  162.4 15.5 %select_reduce_fusion = f32[1024]{0:T(1024)S(1)} fusion(s32[1024]{0:T(1024)S(1)} %iota_add_fusion, pred[1024]{0:T(1024)(128)(4,1)S(1)} %broadcast_compare_fusion, bf16[1024,1024]{1,0:T(8,128)(2,1)} %bitcast.30, bf16[4096,1024]{1,0:T(8,128)(2,1)} %all-gather.2.cloned.1.call-done, bf16[4096]{0:T(1024)(128)(2,1)S(1)} %all_gather.6, bf16[1024]{0:T(1024)(128)(2,1)S(1)} %eq.48), kind=kOutput, calls=%fused_computation.3 | convolution fusion | flops 8623488000 | bytes 10505216 | tf_op jit(solution)/shard_map/md,kd->mk/dot_general | solution.py:40
  177.9 0.7 max_broadcast_in_dim.14
  178.6 10.7 %all-to-all-start.2 = ((f32[64,16,1]{1,2,0:T(1,128)}), f32[64,16,1]{1,2,0:T(1,128)S(1)}, u32[]{:S(2)}, u32[]{:S(2)}) async-start(f32[64,16,1]{1,2,0:T(1,128)} %bitcast.7), calls=%async_computation.2 | async-start | bytes 65536 | tf_op jit(solution)/shard_map/all_to_all | solution.py:46
  189.3 9.3 %all-to-all-done.2 = f32[64,16,1]{1,2,0:T(1,128)S(1)} async-done(((f32[64,16,1]{1,2,0:T(1,128)}), f32[64,16,1]{1,2,0:T(1,128)S(1)}, u32[]{:S(2)}, u32[]{:S(2)}) %all-to-all-start.2) | async-done | bytes 4128 | tf_op jit(solution)/shard_map/all_to_all | solution.py:46
  198.6 0.5 broadcast.64
  199.1 0.7 reduce.6
  199.8 0.1 all_to_all.26
  199.9 3.4 %gather_fusion = f32[512]{0:T(512)} fusion(f32[1024]{0:T(1024)S(1)} %all_to_all.26, s32[1024]{0:T(1024)S(1)} %pad_clamp_fusion), kind=kCustom, calls=%fused_computation | custom fusion | bytes 6144 | tf_op jit(solution)/shard_map/gather | solution.py:47
  (8 shorter events, 0.1 us)
Async XLA Ops:
  6.5 155.9 %all-gather.2.cloned.1.call-start = ((), (), s32[]{:S(2)}) async-start(), calls=%async_computation.3 | async-start | bytes 10485760 | tf_op jit(solution)/shard_map/all_gather | solution.py:37
  11.7 68.3 %copy-start = (s32[512]{0:T(512)S(1)}, s32[512]{0:T(512)}, u32[]{:S(2)}) copy-start(s32[512]{0:T(512)} %param.5) | copy-start | bytes 6148
  84.5 15.1 %all-to-all-start = ((bf16[64,16,1]{1,2,0:T(2,128)(2,1)}), bf16[64,16,1]{1,2,0:T(2,128)(2,1)S(1)}, u32[]{:S(2)}, u32[]{:S(2)}) async-start(bf16[64,16,1]{1,2,0:T(2,128)(2,1)} %all_to_all.27), calls=%async_computation | async-start | bytes 65536 | tf_op jit(solution)/shard_map/all_to_all | solution.py:32
  178.6 20.0 %all-to-all-start.2 = ((f32[64,16,1]{1,2,0:T(1,128)}), f32[64,16,1]{1,2,0:T(1,128)S(1)}, u32[]{:S(2)}, u32[]{:S(2)}) async-start(f32[64,16,1]{1,2,0:T(1,128)} %bitcast.7), calls=%async_computation.2 | async-start | bytes 65536 | tf_op jit(solution)/shard_map/all_to_all | solution.py:46
Sparse Core Ops, SparseCore 0:
  80.2 82.2 all-gather.1
where the time goes:
time: 211 us; the launch traced here: 210 us
  blocking collectives  74 us (35%)
  waiting for transfers between devices  71.5 us (34%)
  starting transfers between devices  16.5 us (8%)
  matrix products  15.5 us (7%)
  between operations  13.5 us (6%)
  other arithmetic  9.75 us (5%)
  local copies, waits for them, and re-layouts  9.46 us (4%)
    all_to_all x1, blocking collectives, shards(): lax.all_to_all(send_rows, 'ingest', split_axis=0, concat_axis=0, tiled=True)  64.3 us
    all_gather x1, waiting for transfers between devices, shards(): part_rows = lax.all_gather(owned_rows, 'span', axis=0, tiled=True)  52.9 us
    dot_general x1, matrix products, shards(): jnp.einsum('md,kd->mk', owned_rows, part_rows, preferred_element_type=jnp...  15.5 us
    all_to_all x1, starting transfers between devices, shards(): lax.all_to_all(best_sim, 'ingest', split_axis=0, concat_axis=0, tiled=True)  10.7 us
    all_gather x1, blocking collectives, shards(): part_ids = lax.all_gather(owned_ids, 'span', axis=0, tiled=True)  9.65 us
    all_to_all x1, waiting for transfers between devices, shards(): lax.all_to_all(best_sim, 'ingest', split_axis=0, concat_axis=0, tiled=True)  9.27 us
    all_to_all x1, waiting for transfers between devices, shards(): lax.all_to_all(send_ids, 'ingest', split_axis=0, concat_axis=0, tiled=True)  9.26 us
    all_to_all x1, starting transfers between devices, shards(): lax.all_to_all(send_ids, 'ingest', split_axis=0, concat_axis=0, tiled=True)  5.82 us
  transfers between devices with their start and end apart: 3, of which 3 were waited for; matrix products, arithmetic and copies ran while one was open for 2% of the time, Pallas kernels for 0%

commit v1 on v0

v1 whole, which is shorter than its diff:
```python
import functools

import jax
import jax.numpy as jnp
from jax import lax
from jax.experimental import pallas as pl
from jax.experimental.pallas import tpu as pltpu
from jax.sharding import PartitionSpec as P

epsilon = 1e-06
capacity = 16
lanes = 128
cuts = (640, 384)
contract_last = (((1,), (1,)), ((), ()))
contract_first = (((1,), (0,)), ((), ()))


def params():
    return pltpu.CompilerParams(vmem_limit_bytes=40 * 1024 * 1024)


def rank_rows(owner, groups):
    rows = owner.shape[1]
    belongs = lax.broadcasted_iota(jnp.int32, (groups, rows), 0) == owner
    onehot = belongs.astype(jnp.bfloat16)
    earlier = lax.broadcasted_iota(jnp.int32, (rows, rows), 0) < lax.broadcasted_iota(
        jnp.int32, (rows, rows), 1
    )
    before = lax.dot_general(
        onehot, earlier.astype(jnp.bfloat16), contract_first, preferred_element_type=jnp.float32
    )
    within = jnp.sum(jnp.where(belongs, before, 0.0), axis=0, keepdims=True)
    return onehot, within


def place_kernel(groups, emb_ref, owner_ref, cluster_ref, *out_refs):
    *send_refs, ids_ref = out_refs
    owner = owner_ref[...]
    rows = owner.shape[1]
    onehot, within = rank_rows(owner, groups)
    values = emb_ref[...].astype(jnp.float32)
    squared = jnp.sum(values * values, axis=1, keepdims=True)
    unit = (values * lax.rsqrt(squared + epsilon)).astype(jnp.bfloat16)
    slot = owner * capacity + within.astype(jnp.int32)
    spots = groups * capacity
    put = (lax.broadcasted_iota(jnp.int32, (spots, rows), 0) == slot).astype(jnp.bfloat16)
    start = 0
    for ref in send_refs:
        width = ref.shape[1]
        ref[...] = lax.dot_general(
            put,
            unit[:, start : start + width],
            contract_first,
            preferred_element_type=jnp.float32,
        ).astype(jnp.bfloat16)
        start += width
    named = onehot * (cluster_ref[...] + 1).astype(jnp.bfloat16)
    place = lax.broadcasted_iota(jnp.int32, (lanes, rows), 0) == within.astype(jnp.int32)
    ids_ref[...] = (
        lax.dot_general(
            named,
            place.astype(jnp.bfloat16),
            contract_last,
            preferred_element_type=jnp.float32,
        )
        - 1.0
    )


def spread_kernel(ids_ref, out_ref):
    blocks = out_ref.shape[0]
    lane = lax.broadcasted_iota(jnp.int32, (blocks, lanes), 1)
    total = jnp.zeros((blocks, lanes), jnp.float32)
    for i in range(lanes // capacity):
        piece = ids_ref[pl.ds(i, blocks, stride=lanes // capacity), :]
        piece = piece if i == 0 else pltpu.roll(piece, capacity * i, 1)
        total = jnp.where(lane // capacity == i, piece, total)
    out_ref[...] = total


def to_column(row):
    return jnp.transpose(jnp.broadcast_to(row, (lanes, lanes)))


def columns_of(ids, count):
    return jnp.concatenate([to_column(ids[b : b + 1, :]) for b in range(count)], axis=0)


def to_rows(tile):
    blocks = tile.shape[0] // lanes
    return jnp.concatenate(
        [
            jnp.max(jnp.transpose(tile[b * lanes : (b + 1) * lanes, :]), axis=0, keepdims=True)
            for b in range(blocks)
        ],
        axis=0,
    )


wide = 256


def scan_block(lefts, right_of, left_ids, right_ids_ref, at, best, skip_diagonal):
    total = None
    for left, right in zip(lefts, right_of(at)):
        part = lax.dot_general(left, right, contract_last, preferred_element_type=jnp.float32)
        total = part if total is None else total + part
    tops = []
    for half in range(wide // lanes):
        scores = total[:, half * lanes : (half + 1) * lanes]
        ids = right_ids_ref[pl.ds(at * (wide // lanes) + half, 1), :]
        ids = jnp.where(ids < 0, -2.0, ids)
        same = left_ids == ids
        if skip_diagonal:
            row = lax.broadcasted_iota(jnp.int32, scores.shape, 0)
            column = lax.broadcasted_iota(jnp.int32, scores.shape, 1)
            same = same & (row - column != at * wide + half * lanes)
        masked = jnp.where(same, scores, -1.0)
        best = jnp.maximum(best, masked)
        tops.append(jnp.max(masked, axis=0, keepdims=True))
    return best, tops


def own_kernel(parts, *refs):
    own, ids_ref, out_ref, acc = refs[:parts], refs[parts], refs[parts + 1], refs[parts + 2]
    rows = own[0].shape[0]
    columns = columns_of(ids_ref[...], rows // lanes)
    acc[...] = jnp.full(acc.shape, -1.0, jnp.float32)

    def body(at, carry):
        best, _ = scan_block(
            [r[...] for r in own],
            lambda at: [r[pl.ds(at * wide, wide), :] for r in own],
            columns,
            ids_ref,
            at,
            acc[...],
            True,
        )
        acc[...] = best
        return carry

    lax.fori_loop(0, rows // wide, body, 0)
    out_ref[...] = to_rows(acc[...])


def cross_kernel(parts, low_ref, *refs):
    own, after, before = refs[:parts], refs[parts : 2 * parts], refs[2 * parts : 3 * parts]
    ids_ref, after_ids, before_ids, mine_ref, up_ref, down_ref, acc, far, tops, pick = refs[3 * parts :]
    rows = own[0].shape[0]
    half = rows // 2
    low = low_ref[0] == 1
    columns = columns_of(ids_ref[...], rows // lanes)
    acc[...] = jnp.full(acc.shape, -1.0, jnp.float32)
    far[...] = jnp.full(far.shape, -1.0, jnp.float32)
    pick[...] = jnp.where(low, after_ids[...], before_ids[...])
    blocks = rows // lanes
    left_ids = jnp.where(
        low, before_ids[: blocks // 2, :], after_ids[blocks // 2 :, :]
    )
    left_columns = columns_of(left_ids, half // lanes)
    left = [jnp.where(low, b[:half, :], a[half:, :]) for a, b in zip(after, before)]

    def body(at, carry):
        best, found = scan_block(
            [r[...] for r in own],
            lambda at: [r[pl.ds(at * wide, wide), :] for r in after],
            columns,
            after_ids,
            at,
            acc[...],
            False,
        )
        acc[...] = best
        for i, top in enumerate(found):
            up_ref[pl.ds(at * (wide // lanes) + i, 1), :] = top
        spot = pl.ds(at * wide, wide)
        best, found = scan_block(
            left,
            lambda at: [jnp.where(low, a[spot, :], b[spot, :]) for a, b in zip(after, before)],
            left_columns,
            pick,
            at,
            far[...],
            False,
        )
        far[...] = best
        for i, top in enumerate(found):
            tops[pl.ds(at * (wide // lanes) + i, 1), :] = top
        return carry

    lax.fori_loop(0, rows // wide, body, 0)
    mine_ref[...] = to_rows(acc[...])
    side = to_rows(far[...])
    blank = jnp.full(side.shape, -1.0, jnp.float32)
    placed = jnp.where(
        low, jnp.concatenate([side, blank], axis=0), jnp.concatenate([blank, side], axis=0)
    )
    up_ref[...] = jnp.maximum(up_ref[...], jnp.where(low, tops[...], placed))
    down_ref[...] = jnp.where(low, placed, tops[...])


def merge_kernel(a_ref, b_ref, c_ref, d_ref, out_ref):
    best = jnp.maximum(
        jnp.maximum(a_ref[...], b_ref[...]), jnp.maximum(c_ref[...], d_ref[...])
    )
    per = lanes // capacity
    row = lax.broadcasted_iota(jnp.int32, (lanes, lanes), 0)
    lane = lax.broadcasted_iota(jnp.int32, (lanes, lanes), 1)
    for b in range(best.shape[0]):
        tile = jnp.where(row % capacity == lane, to_column(best[b : b + 1, :]), -1.0)
        out_ref[b * per : (b + 1) * per, :] = jnp.max(
            tile.reshape(per, capacity, lanes), axis=1
        )


def fetch_kernel(groups, back_ref, owner_ref, out_ref):
    owner = owner_ref[...]
    rows = owner.shape[1]
    onehot, within = rank_rows(owner, groups)
    rest = back_ref[...]
    found = jnp.zeros((lanes, rows), jnp.float32)
    for _ in range(3):
        piece = rest.astype(jnp.bfloat16)
        rest = rest - piece.astype(jnp.float32)
        found = found + lax.dot_general(
            piece, onehot, (((0,), (0,)), ((), ())), preferred_element_type=jnp.float32
        )
    place = lax.broadcasted_iota(jnp.int32, (lanes, rows), 0) == within.astype(jnp.int32)
    out_ref[...] = jnp.sum(jnp.where(place, found, 0.0), axis=0, keepdims=True)


def shift(values, step):
    count = lax.axis_size("span")
    return lax.ppermute(values, "span", [(i, (i + step) % count) for i in range(count)])


def shards(embeddings, owner, cluster):
    rows = embeddings.shape[0]
    groups = lax.axis_size("ingest")
    spots = groups * capacity
    blocks = spots // lanes
    parts = len(cuts)
    owner = owner.reshape(1, rows)
    cluster = cluster.reshape(1, rows)
    f32 = jnp.float32
    *sends, ids = pl.pallas_call(
        functools.partial(place_kernel, groups),
        out_shape=[jax.ShapeDtypeStruct((spots, w), jnp.bfloat16) for w in cuts]
        + [jax.ShapeDtypeStruct((groups, lanes), f32)],
        compiler_params=params(),
        name="place",
    )(embeddings, owner, cluster)
    own, after, before = [], [], []
    for send in sends:
        got = lax.all_to_all(
            send.reshape(groups, capacity, send.shape[1]),
            "ingest",
            split_axis=0,
            concat_axis=0,
            tiled=True,
        ).reshape(spots, send.shape[1])
        own.append(got)
        before.append(shift(got, 1))
        after.append(shift(got, -1))
    ids, own[-1] = lax.optimization_barrier((ids, own[-1]))
    ids = lax.all_to_all(
        ids.reshape(groups, 1, 1, lanes), "ingest", split_axis=0, concat_axis=0, tiled=True
    ).reshape(groups, lanes)
    ids = pl.pallas_call(
        spread_kernel,
        out_shape=jax.ShapeDtypeStruct((blocks, lanes), f32),
        name="spread",
    )(ids)
    before_ids, after_ids = shift(ids, 1), shift(ids, -1)
    row_shape = jax.ShapeDtypeStruct((blocks, lanes), f32)
    inside = pl.pallas_call(
        functools.partial(own_kernel, parts),
        out_shape=row_shape,
        scratch_shapes=[pltpu.VMEM((spots, lanes), f32)],
        compiler_params=params(),
        name="own",
    )(*own, ids)
    low = (lax.axis_index("span") < lax.axis_size("span") // 2).astype(jnp.int32).reshape(1)
    vmem = pl.BlockSpec(memory_space=pltpu.VMEM)
    mine, up, down = pl.pallas_call(
        functools.partial(cross_kernel, parts),
        out_shape=[row_shape] * 3,
        in_specs=[pl.BlockSpec(memory_space=pltpu.SMEM)] + [vmem] * (3 * parts + 3),
        scratch_shapes=[
            pltpu.VMEM((spots, lanes), f32),
            pltpu.VMEM((spots // 2, lanes), f32),
            pltpu.VMEM((blocks, lanes), f32),
            pltpu.VMEM((blocks, lanes), f32),
        ],
        compiler_params=params(),
        name="cross",
    )(low, *own, *after, *before, ids, after_ids, before_ids)
    from_below, from_above = shift(up, 1), shift(down, -1)
    best = pl.pallas_call(
        merge_kernel,
        out_shape=jax.ShapeDtypeStruct((groups, lanes), f32),
        name="merge",
    )(inside, mine, from_below, from_above)
    back = lax.all_to_all(
        best.reshape(groups, 1, 1, lanes), "ingest", split_axis=0, concat_axis=0, tiled=True
    ).reshape(groups, lanes)
    result = pl.pallas_call(
        functools.partial(fetch_kernel, groups),
        out_shape=jax.ShapeDtypeStruct((1, rows), f32),
        name="fetch",
    )(back, owner)
    return result.reshape(rows)


def solution(mesh):
    placed = (P(("ingest", "span"), None), P(("ingest", "span"), None), P(("ingest", "span")))
    return jax.shard_map(
        shards, mesh=mesh, in_specs=placed, out_specs=P(("ingest", "span")), check_vma=False
    )
```

time: 211 us -> 152 us (0.72)
  waiting for transfers between devices: 71.5 us -> 26 us
  Pallas kernels: 0 us -> 18.7 us
  matrix products: 15.5 us -> 0 us
  between operations: 13.5 us -> 0.1 us
  blocking collectives: 74 us -> 84.5 us
  other arithmetic: 9.75 us -> 0 us
  local copies, waits for them, and re-layouts: 9.46 us -> 4.42 us
    all_gather x1 -> x0, waiting for transfers between devices: 52.9 us -> none  [shards(): part_rows = lax.all_gather(owned_rows, 'span', axis=0, tiled=True)]
    all_to_all x1 -> x3, blocking collectives: 64.3 us -> 84.5 us  [the longest x1 47.1 us: shards(): lax.all_to_all(send.reshape(groups, capacity, send.shape[1]), 'ingest', s...]
    pallas_call x0 -> x6, Pallas kernels: none -> 18.7 us  [the longest x1 7.45 us: shards(): pl.pallas_call(functools.partial(cross_kernel, parts), out_shape=[row_sha...]
    dot_general x1 -> x0, matrix products: 15.5 us -> none  [shards(): jnp.einsum('md,kd->mk', owned_rows, part_rows, preferred_element_type=jnp...]
    ppermute x0 -> x8, starting transfers between devices: none -> 11.8 us  [shift(): lax.ppermute(values, 'span', [(i, (i + step) % count) for i in range(coun...]
    all_to_all x2 -> x1, starting transfers between devices: 16.5 us -> 6.16 us  [shards(): lax.all_to_all(send.reshape(groups, capacity, send.shape[1]), 'ingest', s...]
    all_gather x1 -> x0, blocking collectives: 9.65 us -> none  [shards(): part_ids = lax.all_gather(owned_ids, 'span', axis=0, tiled=True)]
    ppermute x0 -> x8, waiting for transfers between devices: none -> 5.54 us  [shift(): lax.ppermute(values, 'span', [(i, (i + step) % count) for i in range(coun...]
  transfers between devices with their start and end apart: 3 -> 9, of which waited for: 3 -> 3; matrix products, arithmetic and copies ran while one was open for 2% -> 0% of each run, Pallas kernels for 0% -> 3%
where the time goes in v1:
time: 152 us
  blocking collectives  84.5 us (56%)
  waiting for transfers between devices  26 us (17%)
  Pallas kernels  18.7 us (12%)
  starting transfers between devices  17.9 us (12%)
  local copies, waits for them, and re-layouts  4.42 us (3%)
    all_to_all x1, blocking collectives, shards(): lax.all_to_all(send.reshape(groups, capacity, send.shape[1]), 'ingest', s...  47.1 us
    all_to_all x1, blocking collectives, shards(): lax.all_to_all(best.reshape(groups, 1, 1, lanes), 'ingest', split_axis=0,...  21.9 us
    all_to_all x1, waiting for transfers between devices, shards(): lax.all_to_all(send.reshape(groups, capacity, send.shape[1]), 'ingest', s...  20.4 us
    all_to_all x1, blocking collectives, shards(): lax.all_to_all(ids.reshape(groups, 1, 1, lanes), 'ingest', split_axis=0,...  15.5 us
    ppermute x8, starting transfers between devices, shift(): lax.ppermute(values, 'span', [(i, (i + step) % count) for i in range(coun...  11.8 us
    pallas_call x1, Pallas kernels, shards(): pl.pallas_call(functools.partial(cross_kernel, parts), out_shape=[row_sha...  7.45 us
    all_to_all x1, starting transfers between devices, shards(): lax.all_to_all(send.reshape(groups, capacity, send.shape[1]), 'ingest', s...  6.16 us
    ppermute x8, waiting for transfers between devices, shift(): lax.ppermute(values, 'span', [(i, (i + step) % count) for i in range(coun...  5.54 us
  transfers between devices with their start and end apart: 9, of which 3 were waited for; matrix products, arithmetic and copies ran while one was open for 0% of the time, Pallas kernels for 3%

profile of v1, /device:TPU:1, one launch (start us, length us, event | category | flops | bytes accessed | tf_op | source)
XLA Modules:
  0.0 151.7 jit_solution(10077328210455666097)
XLA Ops:
  0.0 1.2 copy-done
  1.2 0.7 copy-done.3
  1.9 0.7 copy-done.5
  2.6 2.8 %place.1 = (bf16[1024,640]{1,0:T(8,128)(2,1)S(1)}, bf16[1024,384]{1,0:T(8,128)(2,1)}, f32[64,128]{1,0:T(8,128)S(1)}) custom-call(bf16[512,1024]{1,0:T(8,128)(2,1)S(1)} %copy-done, s32[1,512]{1,0:T(1,128)S(1)} %bitcast.27, s32[1,512]{1,0:T(1,128)S(1)} %bitcast.28), custom_call_target="tpu_custom_call" | custom-call | tf_op jit(solution)/shard_map/place/pallas_call | solution.py:247
  5.4 47.1 %all_to_all.20 = bf16[64,16,640]{2,1,0:T(8,128)(2,1)S(1)} all-to-all(bf16[64,16,640]{2,1,0:T(8,128)(2,1)S(1)} %bitcast.24), channel_id=1, replica_groups=mesh['ingest'=64,'span'=4] {'ingest'}, dimensions={0} | all-to-all | bytes 2621440 | tf_op jit(solution)/shard_map/all_to_all | solution.py:256
  52.5 6.2 %all-to-all-start.1 = ((bf16[64,16,384]{2,1,0:T(8,128)(2,1)}), bf16[64,16,384]{2,1,0:T(8,128)(2,1)S(1)}, u32[]{:S(2)}, u32[]{:S(2)}) async-start(bf16[64,16,384]{2,1,0:T(8,128)(2,1)} %bitcast.4), calls=%async_computation.1 | async-start | bytes 1572864 | tf_op jit(solution)/shard_map/all_to_all | solution.py:256
  58.7 2.6 %collective-permute-start = (bf16[1024,640]{1,0:T(8,128)(2,1)S(1)}, bf16[1024,640]{1,0:T(8,128)(2,1)S(1)}, u32[]{:S(2)}, u32[]{:S(2)}) collective-permute-start(bf16[1024,640]{1,0:T(8,128)(2,1)S(1)} %bitcast.16), channel_id=1, source_target_pairs={{0,3},{1,0},{2,1},{3,2},{4,7},{5,4},{6,5},{7,6},{8,11},{9,8},{10,9... | collective-permute-start | bytes 3932168 | tf_op jit(solution)/shard_map/ppermute | solution.py:235
  61.3 0.0 collective-permute-start.2
  61.3 20.4 %all-to-all-done.1 = bf16[64,16,384]{2,1,0:T(8,128)(2,1)S(1)} async-done(((bf16[64,16,384]{2,1,0:T(8,128)(2,1)}), bf16[64,16,384]{2,1,0:T(8,128)(2,1)S(1)}, u32[]{:S(2)}, u32[]{:S(2)}) %all-to-all-start.1) | async-done | bytes 786464 | tf_op jit(solution)/shard_map/all_to_all | solution.py:256
  81.7 2.5 %collective-permute-start.1 = (bf16[1024,384]{1,0:T(8,128)(2,1)S(1)}, bf16[1024,384]{1,0:T(8,128)(2,1)}, u32[]{:S(2)}, u32[]{:S(2)}) collective-permute-start(bf16[1024,384]{1,0:T(8,128)(2,1)S(1)} %bitcast.20), channel_id=1, source_target_pairs={{0,3},{1,0},{2,1},{3,2},{4,7},{5,4},{6,5},{7,6},{8,11},{9,8},{10,9... | collective-permute-start | bytes 2359304 | tf_op jit(solution)/shard_map/ppermute | solution.py:235
  84.2 0.0 collective-permute-start.3
  84.2 15.5 %all_to_all.21 = f32[64,1,1,128]{3,2,1,0:T(1,128)} all-to-all(f32[64,1,1,128]{3,2,1,0:T(1,128)S(1)} %bitcast.25), channel_id=1, replica_groups=mesh['ingest'=64,'span'=4] {'ingest'}, dimensions={0} | all-to-all | bytes 65536 | tf_op jit(solution)/shard_map/all_to_all | solution.py:267
  99.7 1.4 spread.1.refs_2_.refs_6_
  101.1 3.0 %collective-permute-start.4 = (f32[8,128]{1,0:T(8,128)}, f32[8,128]{1,0:T(8,128)S(1)}, u32[]{:S(2)}, u32[]{:S(2)}) collective-permute-start(f32[8,128]{1,0:T(8,128)} %spread.1.refs_2_.refs_6_), channel_id=1, source_target_pairs={{0,3},{1,0},{2,1},{3,2},{4,7},{5,4},{6,5},{7,6},{8,11},{9,8},{10,9... | collective-permute-start | bytes 12296 | tf_op jit(solution)/shard_map/ppermute | solution.py:235
  104.1 1.8 %collective-permute-done.4.refs_7_ = f32[8,128]{1,0:T(8,128)S(1)} collective-permute-done((f32[8,128]{1,0:T(8,128)}, f32[8,128]{1,0:T(8,128)S(1)}, u32[]{:S(2)}, u32[]{:S(2)}) %collective-permute-start.4) | collective-permute-done | bytes 4128 | tf_op jit(solution)/shard_map/ppermute | solution.py:235
  105.9 1.0 collective-permute-start.5
  106.9 3.7 %collective-permute-done.5.refs_8_ = f32[8,128]{1,0:T(8,128)S(1)} collective-permute-done((f32[8,128]{1,0:T(8,128)}, f32[8,128]{1,0:T(8,128)S(1)}, u32[]{:S(2)}, u32[]{:S(2)}) %collective-permute-start.5) | collective-permute-done | bytes 4128 | tf_op jit(solution)/shard_map/ppermute | solution.py:235
  110.6 0.0 collective-permute-done.1.refs_3_
  110.6 0.0 collective-permute-done.3.refs_5_
  110.6 0.7 copy-done.1
  111.3 7.4 %cross.1 = (f32[8,128]{1,0:T(8,128)S(1)}, f32[8,128]{1,0:T(8,128)S(1)}, f32[8,128]{1,0:T(8,128)S(1)}) custom-call(s32[1]{0:T(128)} %bitcast.9.low_ref, bf16[1024,640]{1,0:T(8,128)(2,1)S(1)} %bitcast.18, bf16[1024,384]{1,0:T(8,128)(2,1)S(1)} %bitcast.22, bf16[1024,640]{1,0:T(8,128)(2,1)S(1)} %collective-permute-done.refs_2_, ...), custom_call_target="tpu_custom_call" | custom-call | tf_op jit(solution)/shard_map/cross/pallas_call | solution.py:286
  118.8 0.1 collective-permute-start.6
  118.9 2.7 %collective-permute-start.7 = (f32[8,128]{1,0:T(8,128)S(1)}, f32[8,128]{1,0:T(8,128)S(1)}, u32[]{:S(2)}, u32[]{:S(2)}) collective-permute-start(f32[8,128]{1,0:T(8,128)S(1)} %get-tuple-element.20), channel_id=1, source_target_pairs={{0,3},{1,0},{2,1},{3,2},{4,7},{5,4},{6,5},{7,6},{8,11},{9,8},{10,9... | collective-permute-start | bytes 12296 | tf_op jit(solution)/shard_map/ppermute | solution.py:235
  121.5 3.8 %own.1.a_ref = f32[8,128]{1,0:T(8,128)S(1)} custom-call(bf16[1024,640]{1,0:T(8,128)(2,1)S(1)} %bitcast.19, bf16[1024,384]{1,0:T(8,128)(2,1)S(1)} %bitcast.23, f32[8,128]{1,0:T(8,128)S(1)} %copy-done.1), custom_call_target="tpu_custom_call" | custom-call | tf_op jit(solution)/shard_map/own/pallas_call | solution.py:277
  125.4 0.6 copy-done.2
  126.0 0.0 collective-permute-done.6.c_ref
  126.0 0.0 collective-permute-done.7.d_ref
  126.0 0.6 copy-done.6
  126.6 0.0 copy-done.7
  126.6 1.5 merge.1
  128.1 21.9 %all_to_all.22 = f32[64,1,1,128]{3,2,1,0:T(1,128)} all-to-all(f32[64,1,1,128]{3,2,1,0:T(1,128)} %bitcast.29), channel_id=1, replica_groups=mesh['ingest'=64,'span'=4] {'ingest'}, dimensions={0} | all-to-all | bytes 65536 | tf_op jit(solution)/shard_map/all_to_all | solution.py:305
  150.0 1.7 %fetch.1 = f32[1,512]{1,0:T(1,128)} custom-call(f32[64,128]{1,0:T(8,128)} %bitcast.31, s32[1,512]{1,0:T(1,128)} %bitcast.26), custom_call_target="tpu_custom_call" | custom-call | tf_op jit(solution)/shard_map/fetch/pallas_call | solution.py:308
  (11 shorter events, 0.0 us)
Async XLA Ops:
  0.0 1.2 copy-start
  1.2 0.7 copy-start.3
  1.9 0.7 copy-start.5
  52.5 29.2 %all-to-all-start.1 = ((bf16[64,16,384]{2,1,0:T(8,128)(2,1)}), bf16[64,16,384]{2,1,0:T(8,128)(2,1)S(1)}, u32[]{:S(2)}, u32[]{:S(2)}) async-start(bf16[64,16,384]{2,1,0:T(8,128)(2,1)} %bitcast.4), calls=%async_computation.1 | async-start | bytes 1572864 | tf_op jit(solution)/shard_map/all_to_all | solution.py:256
  58.7 51.9 %collective-permute-start = (bf16[1024,640]{1,0:T(8,128)(2,1)S(1)}, bf16[1024,640]{1,0:T(8,128)(2,1)S(1)}, u32[]{:S(2)}, u32[]{:S(2)}) collective-permute-start(bf16[1024,640]{1,0:T(8,128)(2,1)S(1)} %bitcast.16), channel_id=1, source_target_pairs={{0,3},{1,0},{2,1},{3,2},{4,7},{5,4},{6,5},{7,6},{8,11},{9,8},{10,9... | collective-permute-start | bytes 3932168 | tf_op jit(solution)/shard_map/ppermute | solution.py:235
  61.3 49.4 %collective-permute-start.2 = (bf16[1024,640]{1,0:T(8,128)(2,1)S(1)}, bf16[1024,640]{1,0:T(8,128)(2,1)}, u32[]{:S(2)}, u32[]{:S(2)}) collective-permute-start(bf16[1024,640]{1,0:T(8,128)(2,1)S(1)} %bitcast.17), channel_id=1, source_target_pairs={{0,1},{1,2},{2,3},{3,0},{4,5},{5,6},{6,7},{7,4},{8,9},{9,10},{10,1... | collective-permute-start | bytes 3932168 | tf_op jit(solution)/shard_map/ppermute | solution.py:235
  81.7 28.9 %collective-permute-start.1 = (bf16[1024,384]{1,0:T(8,128)(2,1)S(1)}, bf16[1024,384]{1,0:T(8,128)(2,1)}, u32[]{:S(2)}, u32[]{:S(2)}) collective-permute-start(bf16[1024,384]{1,0:T(8,128)(2,1)S(1)} %bitcast.20), channel_id=1, source_target_pairs={{0,3},{1,0},{2,1},{3,2},{4,7},{5,4},{6,5},{7,6},{8,11},{9,8},{10,9... | collective-permute-start | bytes 2359304 | tf_op jit(solution)/shard_map/ppermute | solution.py:235
  84.2 26.5 %collective-permute-start.3 = (bf16[1024,384]{1,0:T(8,128)(2,1)S(1)}, bf16[1024,384]{1,0:T(8,128)(2,1)}, u32[]{:S(2)}, u32[]{:S(2)}) collective-permute-start(bf16[1024,384]{1,0:T(8,128)(2,1)S(1)} %bitcast.21), channel_id=1, source_target_pairs={{0,1},{1,2},{2,3},{3,0},{4,5},{5,6},{6,7},{7,4},{8,9},{9,10},{10,1... | collective-permute-start | bytes 2359304 | tf_op jit(solution)/shard_map/ppermute | solution.py:235
  101.1 4.8 %collective-permute-start.4 = (f32[8,128]{1,0:T(8,128)}, f32[8,128]{1,0:T(8,128)S(1)}, u32[]{:S(2)}, u32[]{:S(2)}) collective-permute-start(f32[8,128]{1,0:T(8,128)} %spread.1.refs_2_.refs_6_), channel_id=1, source_target_pairs={{0,3},{1,0},{2,1},{3,2},{4,7},{5,4},{6,5},{7,6},{8,11},{9,8},{10,9... | collective-permute-start | bytes 12296 | tf_op jit(solution)/shard_map/ppermute | solution.py:235
  105.9 4.7 %collective-permute-start.5 = (f32[8,128]{1,0:T(8,128)}, f32[8,128]{1,0:T(8,128)S(1)}, u32[]{:S(2)}, u32[]{:S(2)}) collective-permute-start(f32[8,128]{1,0:T(8,128)} %spread.1.refs_2_.refs_6_), channel_id=1, source_target_pairs={{0,1},{1,2},{2,3},{3,0},{4,5},{5,6},{6,7},{7,4},{8,9},{9,10},{10,1... | collective-permute-start | bytes 12296 | tf_op jit(solution)/shard_map/ppermute | solution.py:235
  110.6 0.7 copy-start.1
  118.8 6.6 %copy-start.4 = (f32[8,128]{1,0:T(8,128)}, f32[8,128]{1,0:T(8,128)S(1)}, u32[]{:S(2)}) copy-start(f32[8,128]{1,0:T(8,128)S(1)} %get-tuple-element.18.b_ref) | copy-start | bytes 12292
  118.8 7.2 %collective-permute-start.6 = (f32[8,128]{1,0:T(8,128)S(1)}, f32[8,128]{1,0:T(8,128)S(1)}, u32[]{:S(2)}, u32[]{:S(2)}) collective-permute-start(f32[8,128]{1,0:T(8,128)S(1)} %get-tuple-element.19), channel_id=1, source_target_pairs={{0,1},{1,2},{2,3},{3,0},{4,5},{5,6},{6,7},{7,4},{8,9},{9,10},{10,1... | collective-permute-start | bytes 12296 | tf_op jit(solution)/shard_map/ppermute | solution.py:235
  118.9 7.1 %collective-permute-start.7 = (f32[8,128]{1,0:T(8,128)S(1)}, f32[8,128]{1,0:T(8,128)S(1)}, u32[]{:S(2)}, u32[]{:S(2)}) collective-permute-start(f32[8,128]{1,0:T(8,128)S(1)} %get-tuple-element.20), channel_id=1, source_target_pairs={{0,3},{1,0},{2,1},{3,2},{4,7},{5,4},{6,5},{7,6},{8,11},{9,8},{10,9... | collective-permute-start | bytes 12296 | tf_op jit(solution)/shard_map/ppermute | solution.py:235
  125.4 0.6 copy-start.2
  126.0 0.6 copy-start.6
  126.0 0.6 copy-start.7

commit v2 on v0

v2 whole, which is shorter than its diff:
```python
import functools

import jax
import jax.numpy as jnp
from jax import lax
from jax.experimental import pallas as pl
from jax.experimental.pallas import tpu as pltpu
from jax.sharding import PartitionSpec as P

epsilon = 1e-06
capacity = 16
lanes = 128
wide = 256
cores = 2
places = 4
depth = 8
field = cores * capacity
near_slabs = (0, 1, 7, 2, 6)
far_slabs = (3, 5, 4)
contract_last = (((1,), (1,)), ((), ()))
contract_first = (((1,), (0,)), ((), ()))
everyone = ("ingest", "span")


def params():
    return pltpu.CompilerParams(vmem_limit_bytes=40 * 1024 * 1024)


def device(y, z, core, x):
    return ((y * depth + z) * cores + core) * places + x


def pairs(move):
    found = []
    for y in range(places):
        for z in range(depth):
            for core in range(cores):
                for x in range(places):
                    found.append((device(y, z, core, x), device(*move(y, z, core, x))))
    return found


def along_depth(step):
    return pairs(lambda y, z, core, x: (y, (z + step) % depth, core, x))


def other_core():
    return pairs(lambda y, z, core, x: (y, z, 1 - core, x))


def beside(step):
    return pairs(
        lambda y, z, core, x: (y, z, core, (x + step) % places)
        if core == 0
        else ((y + step) % places, z, core, x)
    )


def line_teams():
    spots = range(places)
    return [[device(i, z, 0, x) for i in spots] for z in range(depth) for x in spots] + [
        [device(y, z, 1, i) for i in spots] for z in range(depth) for y in spots
    ]


def plane_teams():
    spots, levels = range(places), range(depth)
    return [[device(i, z, 0, x) for i in spots for z in levels] for x in spots] + [
        [device(y, z, 1, i) for i in spots for z in levels] for y in spots
    ]


def chunks():
    found = []
    for place in range(places):
        for slab in near_slabs:
            found.append((place, slab))
    for place in range(places):
        for slab in far_slabs:
            found.append((place, slab))
    return found


def rank_rows(owner, groups):
    rows = owner.shape[1]
    belongs = lax.broadcasted_iota(jnp.int32, (groups, rows), 0) == owner
    onehot = belongs.astype(jnp.bfloat16)
    earlier = lax.broadcasted_iota(jnp.int32, (rows, rows), 0) < lax.broadcasted_iota(
        jnp.int32, (rows, rows), 1
    )
    before = lax.dot_general(
        onehot, earlier.astype(jnp.bfloat16), contract_first, preferred_element_type=jnp.float32
    )
    return jnp.sum(jnp.where(belongs, before, 0.0), axis=0, keepdims=True).astype(jnp.int32)


def owned_here(owner, core):
    half = owner.shape[1]
    table = lax.broadcasted_iota(jnp.int32, (places * depth, half), 0)
    return (table == owner // cores) & (owner % cores == core)


def place_kernel(groups, spot_ref, *refs):
    embs, owners, clusters = refs[0:2], refs[2:4], refs[4:6]
    slabs, ids_ref, within_ref = refs[6 : 6 + depth], refs[6 + depth], refs[7 + depth]
    core, level = spot_ref[0], spot_ref[1]
    slots, units, named, spots = [], [], [], []
    for side in range(cores):
        owner = owners[side][...]
        within = rank_rows(owner, groups)
        within_ref[side : side + 1, :] = within
        team = owner // cores
        away = (team % depth - level + depth) % depth
        slot = (away * places + team // depth) * field + side * capacity + within
        slots.append(jnp.where(owner % cores == core, slot, -1))
        values = embs[side][...].astype(jnp.float32)
        squared = jnp.sum(values * values, axis=1, keepdims=True)
        units.append((values * lax.rsqrt(squared + epsilon)).astype(jnp.bfloat16))
        here = owned_here(owner, core).astype(jnp.bfloat16)
        named.append(here * (clusters[side][...] + 1).astype(jnp.bfloat16))
        spots.append(within + side * capacity)
    slot = jnp.concatenate(slots, axis=1)
    unit = jnp.concatenate(units, axis=0)
    rows = slot.shape[1]
    room = depth * places * field
    put = (lax.broadcasted_iota(jnp.int32, (room, rows), 0) == slot).astype(jnp.bfloat16)
    each = places * field
    for start in range(0, unit.shape[1], wide):
        placed = lax.dot_general(
            put,
            unit[:, start : start + wide],
            contract_first,
            preferred_element_type=jnp.float32,
        ).astype(jnp.bfloat16)
        for i, ref in enumerate(slabs):
            ref[:, start : start + wide] = placed[i * each : (i + 1) * each, :]
    lane = lax.broadcasted_iota(jnp.int32, (lanes, rows), 0)
    into = (lane == jnp.concatenate(spots, axis=1)).astype(jnp.bfloat16)
    ids_ref[...] = (
        lax.dot_general(
            jnp.concatenate(named, axis=1),
            into,
            contract_last,
            preferred_element_type=jnp.float32,
        )
        - 1.0
    )


def spread_kernel(spot_ref, ids_ref, out_ref):
    level = spot_ref[1]
    lane = lax.broadcasted_iota(jnp.int32, (1, lanes), 1)
    per = lanes // field
    for i, (place, slab) in enumerate(chunks()):
        source = place * depth + (level - slab + depth) % depth
        piece = ids_ref[pl.ds(source, 1), :]
        if i % per == 0:
            total = piece
        else:
            total = jnp.where(lane // field == i % per, pltpu.roll(piece, field * (i % per), 1), total)
        if i % per == per - 1:
            out_ref[i // per : i // per + 1, :] = total


def to_column(row):
    return jnp.transpose(jnp.broadcast_to(row, (lanes, lanes)))


def columns_of(ids):
    return jnp.concatenate([to_column(ids[b : b + 1, :]) for b in range(ids.shape[0])], axis=0)


def to_rows(tile):
    return jnp.concatenate(
        [
            jnp.max(jnp.transpose(tile[b * lanes : (b + 1) * lanes, :]), axis=0, keepdims=True)
            for b in range(tile.shape[0] // lanes)
        ],
        axis=0,
    )


def block_of(refs, start, count):
    found = []
    for ref in refs:
        low, high = max(start, 0), min(start + count, ref.shape[0])
        if low < high:
            found.append(ref[low:high, :])
        start -= ref.shape[0]
    return found[0] if len(found) == 1 else jnp.concatenate(found, axis=0)


def scan_block(lefts, right, left_ids, right_ids, best, skip):
    parts = [
        lax.dot_general(left, right, contract_last, preferred_element_type=jnp.float32)
        for left in lefts
    ]
    total = parts[0] if len(parts) == 1 else jnp.concatenate(parts, axis=0)
    tops = []
    for half in range(wide // lanes):
        scores = total[:, half * lanes : (half + 1) * lanes]
        ids = right_ids[half : half + 1, :]
        same = left_ids == jnp.where(ids < 0, -2.0, ids)
        if skip is not None:
            row = lax.broadcasted_iota(jnp.int32, scores.shape, 0)
            column = lax.broadcasted_iota(jnp.int32, scores.shape, 1)
            same = same & (row - column != skip + half * lanes)
        masked = jnp.where(same, scores, -1.0)
        best = masked if best is None else jnp.maximum(best, masked)
        tops.append(jnp.max(masked, axis=0, keepdims=True))
    return best, tops


def own_kernel(spot_ref, *refs):
    *own, ids_ref, out_ref = refs
    ids = ids_ref[...]
    rows = ids.shape[0] * lanes
    columns = columns_of(ids)
    lefts = [r[...] for r in own]
    best = None
    per = wide // lanes
    for at in range(rows // wide):
        best, _ = scan_block(
            lefts,
            block_of(own, at * wide, wide),
            columns,
            ids[at * per : (at + 1) * per, :],
            best,
            at * wide,
        )
    out_ref[...] = to_rows(best)


def cross_kernel(sets, spot_ref, *refs):
    own, after, before = refs[:sets], refs[sets : 2 * sets], refs[2 * sets : 3 * sets]
    ids_ref, after_ids_ref, before_ids_ref, inside_ref, out_ref = refs[3 * sets :]
    level, low = spot_ref[1], spot_ref[2] == 1
    ids, after_ids, before_ids = ids_ref[...], after_ids_ref[...], before_ids_ref[...]
    blocks = ids.shape[0]
    rows = blocks * lanes
    half = rows // 2
    columns = columns_of(ids)
    right_ids = jnp.where(low, after_ids, before_ids)
    left_ids = jnp.where(low, before_ids[: blocks // 2, :], after_ids[blocks // 2 :, :])
    left_columns = columns_of(left_ids)
    left = jnp.where(low, block_of(before, 0, half), block_of(after, half, half))
    lefts = [r[...] for r in own]
    per = wide // lanes
    best, far, up, side = None, None, [], []
    for at in range(rows // wide):
        near = block_of(after, at * wide, wide)
        right = jnp.where(low, near, block_of(before, at * wide, wide))
        cut = slice(at * per, (at + 1) * per)
        best, tops = scan_block(lefts, near, columns, after_ids[cut, :], best, None)
        up += tops
        far, tops = scan_block([left], right, left_columns, right_ids[cut, :], far, None)
        side += tops
    up, side = jnp.concatenate(up, axis=0), jnp.concatenate(side, axis=0)
    mine = jnp.maximum(to_rows(best), inside_ref[...])
    found = to_rows(far)
    blank = jnp.full(found.shape, -1.0, jnp.float32)
    placed = jnp.where(
        low, jnp.concatenate([found, blank], axis=0), jnp.concatenate([blank, found], axis=0)
    )
    up = jnp.maximum(up, jnp.where(low, side, placed))
    down = jnp.where(low, placed, side)
    lane = lax.broadcasted_iota(jnp.int32, (blocks, lanes), 1)
    count = lanes // field
    for q in range(count):
        turned = [
            values if (i - q) % count == 0 else pltpu.roll(values, field * ((i - q) % count), 1)
            for i, values in enumerate((mine, up, down))
        ]
        joined = jnp.where(
            lane < field, turned[0], jnp.where(lane < 2 * field, turned[1], turned[2])
        )
        for i, (place, slab) in enumerate(chunks()):
            if i % count == q:
                source = place * depth + (level - slab + depth) % depth
                out_ref[pl.ds(source, 1), :] = joined[i // count : i // count + 1, :]


def fetch_kernel(spot_ref, back_ref, below_ref, above_ref, owner_ref, other_ref, within_ref, out_ref):
    core = spot_ref[0]
    table = jnp.maximum(
        back_ref[...],
        jnp.maximum(
            pltpu.roll(below_ref[...], lanes - field, 1),
            pltpu.roll(above_ref[...], lanes - 2 * field, 1),
        ),
    )
    owners = (owner_ref[...], other_ref[...])
    here = [owned_here(owner, core) for owner in owners]
    onehot = jnp.concatenate(here, axis=1).astype(jnp.bfloat16)
    rows = owners[0].shape[1]
    rest = table
    found = jnp.zeros((lanes, cores * rows), jnp.float32)
    for _ in range(3):
        piece = rest.astype(jnp.bfloat16)
        rest = rest - piece.astype(jnp.float32)
        found = found + lax.dot_general(
            piece, onehot, (((0,), (0,)), ((), ())), preferred_element_type=jnp.float32
        )
    lane = lax.broadcasted_iota(jnp.int32, (lanes, rows), 0)
    for side in range(cores):
        place = lane == within_ref[side : side + 1, :] + side * capacity
        part = found[:, side * rows : (side + 1) * rows]
        picked = jnp.sum(jnp.where(place, part, 0.0), axis=0, keepdims=True)
        mine = owners[side] % cores == core
        out_ref[side : side + 1, :] = jnp.where(mine, picked, -1.0)


def send(values, route):
    return lax.ppermute(values, everyone, route)


def trade(values, teams):
    return lax.all_to_all(
        values, everyone, split_axis=0, concat_axis=0, axis_index_groups=teams, tiled=True
    )


def shards(embeddings, owner, cluster):
    rows, width = embeddings.shape
    groups = lax.axis_size("ingest")
    spots = groups * capacity
    blocks = spots // lanes
    each = places * field
    f32 = jnp.float32
    at, x = lax.axis_index("ingest"), lax.axis_index("span")
    core, level, y = at % cores, at // cores % depth, at // (cores * depth)
    low = jnp.where(core == 0, x, y) < places // 2
    spot = jnp.stack([core, level, low.astype(jnp.int32)]).astype(jnp.int32)
    smem, vmem = pl.BlockSpec(memory_space=pltpu.SMEM), pl.BlockSpec(memory_space=pltpu.VMEM)

    def call(kernel, out_shape, name, *args):
        return pl.pallas_call(
            kernel,
            out_shape=out_shape,
            in_specs=[smem] + [vmem] * len(args),
            compiler_params=params(),
            name=name,
        )(spot, *args)

    swap = other_core()
    owner = owner.reshape(1, rows)
    cluster = cluster.reshape(1, rows)
    others = send(owner, swap)
    other_cluster = send(cluster, swap)
    other_rows = send(embeddings, swap)
    *slabs, ids, within = call(
        functools.partial(place_kernel, groups),
        [jax.ShapeDtypeStruct((each, width), jnp.bfloat16)] * depth
        + [
            jax.ShapeDtypeStruct((places * depth, lanes), f32),
            jax.ShapeDtypeStruct((cores, rows), jnp.int32),
        ],
        "place",
        embeddings,
        other_rows,
        owner,
        others,
        cluster,
        other_cluster,
    )
    for slab in near_slabs[1:] + far_slabs:
        slabs[slab] = send(slabs[slab], along_depth(slab))
    teams = plane_teams()
    ids = trade(ids.reshape(places * depth, 1, 1, lanes), teams).reshape(places * depth, lanes)
    ids = call(spread_kernel, jax.ShapeDtypeStruct((blocks, lanes), f32), "spread", ids)
    before_ids, after_ids = send(ids, beside(1)), send(ids, beside(-1))
    own, after, before = [], [], []
    for chosen in (near_slabs, far_slabs):
        group = jnp.concatenate(
            [slabs[s].reshape(places, field, width) for s in chosen], axis=1
        )
        got = trade(group, line_teams()).reshape(len(chosen) * each, width)
        own.append(got)
        before.append(send(got, beside(1)))
        after.append(send(got, beside(-1)))
    inside = call(own_kernel, jax.ShapeDtypeStruct((blocks, lanes), f32), "own", *own, ids)
    best = call(
        functools.partial(cross_kernel, len(own)),
        jax.ShapeDtypeStruct((places * depth, lanes), f32),
        "cross",
        *own,
        *after,
        *before,
        ids,
        after_ids,
        before_ids,
        inside,
    )
    back = trade(best.reshape(places * depth, 1, 1, lanes), teams).reshape(places * depth, lanes)
    below, above = send(back, beside(1)), send(back, beside(-1))
    found = call(
        fetch_kernel,
        jax.ShapeDtypeStruct((cores, rows), f32),
        "fetch",
        back,
        below,
        above,
        owner,
        others,
        within,
    )
    return jnp.maximum(found[0], send(found[1], swap))


def solution(mesh):
    placed = (P(("ingest", "span"), None), P(("ingest", "span"), None), P(("ingest", "span")))
    return jax.shard_map(
        shards, mesh=mesh, in_specs=placed, out_specs=P(("ingest", "span")), check_vma=False
    )
```

time: 211 us -> 148 us (0.70)
  blocking collectives: 74 us -> 42.4 us
  waiting for transfers between devices: 71.5 us -> 42.3 us
  starting transfers between devices: 16.5 us -> 42.3 us
  matrix products: 15.5 us -> 0 us
  between operations: 13.5 us -> 0.13 us
  Pallas kernels: 0 us -> 13.1 us
  other arithmetic: 9.75 us -> 1.59 us
  local copies, waits for them, and re-layouts: 9.46 us -> 6.2 us
    all_gather x1 -> x0, waiting for transfers between devices: 52.9 us -> none  [shards(): part_rows = lax.all_gather(owned_rows, 'span', axis=0, tiled=True)]
    ppermute x0 -> x19, waiting for transfers between devices: none -> 36.4 us  [send(): return lax.ppermute(values, everyone, route)]
    ppermute x0 -> x19, starting transfers between devices: none -> 33.7 us  [send(): return lax.ppermute(values, everyone, route)]
    all_to_all x1 -> x2, blocking collectives: 64.3 us -> 42.4 us  [trade(): lax.all_to_all(values, everyone, split_axis=0, concat_axis=0, axis_index_...]
    dot_general x1 -> x0, matrix products: 15.5 us -> none  [shards(): jnp.einsum('md,kd->mk', owned_rows, part_rows, preferred_element_type=jnp...]
    pallas_call x0 -> x5, Pallas kernels: none -> 13.1 us  [call(): pl.pallas_call(kernel, out_shape=out_shape, in_specs=[smem] + [vmem] * le...]
    all_to_all x2, waiting for transfers between devices: 18.5 us -> 5.87 us  [trade(): lax.all_to_all(values, everyone, split_axis=0, concat_axis=0, axis_index_...]
    all_gather x1 -> x0, blocking collectives: 9.65 us -> none  [shards(): part_ids = lax.all_gather(owned_ids, 'span', axis=0, tiled=True)]
  transfers between devices with their start and end apart: 3 -> 21, of which waited for: 3 -> 11; matrix products, arithmetic and copies ran while one was open for 2% -> 3% of each run, Pallas kernels for 0% -> 2%
where the time goes in v2:
time: 148 us
  blocking collectives  42.4 us (29%)
  starting transfers between devices  42.3 us (29%)
  waiting for transfers between devices  42.3 us (29%)
  Pallas kernels  13.1 us (9%)
  local copies, waits for them, and re-layouts  6.2 us (4%)
  other arithmetic  1.59 us (1%)
    all_to_all x2, blocking collectives, trade(): lax.all_to_all(values, everyone, split_axis=0, concat_axis=0, axis_index_...  42.4 us
    ppermute x19, waiting for transfers between devices, send(): return lax.ppermute(values, everyone, route)  36.4 us
    ppermute x19, starting transfers between devices, send(): return lax.ppermute(values, everyone, route)  33.7 us
    pallas_call x5, Pallas kernels, call(): pl.pallas_call(kernel, out_shape=out_shape, in_specs=[smem] + [vmem] * le...  13.1 us
    all_to_all x2, starting transfers between devices, trade(): lax.all_to_all(values, everyone, split_axis=0, concat_axis=0, axis_index_...  8.59 us
    all_to_all x2, waiting for transfers between devices, trade(): lax.all_to_all(values, everyone, split_axis=0, concat_axis=0, axis_index_...  5.87 us
    unnamed x12, local copies, waits for them, and re-layouts  5.47 us
  transfers between devices with their start and end apart: 21, of which 11 were waited for; matrix products, arithmetic and copies ran while one was open for 3% of the time, Pallas kernels for 2%

profile of v2, /device:TPU:1, one launch (start us, length us, event | category | flops | bytes accessed | tf_op | source)
XLA Modules:
  0.0 147.9 jit_solution(13858299340764941260)
XLA Ops:
  0.0 3.2 %collective-permute-start = (bf16[512,1024]{1,0:T(8,128)(2,1)}, bf16[512,1024]{1,0:T(8,128)(2,1)S(1)}, u32[]{:S(2)}, u32[]{:S(2)}) collective-permute-start(bf16[512,1024]{1,0:T(8,128)(2,1)} %refs_0_.1), channel_id=1, source_target_pairs={{0,4},{1,5},{2,6},{3,7},{4,0},{5,1},{6,2},{7,3},{8,12},{9,13},{10,... | collective-permute-start | bytes 3145736 | tf_op jit(solution)/shard_map/ppermute | solution.py:314
  3.8 1.9 %collective-permute-done.1.refs_3_.other_ref = s32[1,512]{1,0:T(1,128)S(1)} collective-permute-done((s32[1,512]{1,0:T(1,128)}, s32[1,512]{1,0:T(1,128)S(1)}, u32[]{:S(2)}, u32[]{:S(2)}) %collective-permute-start.1) | collective-permute-done | bytes 2080 | tf_op jit(solution)/shard_map/ppermute | solution.py:314
  5.8 1.2 copy-done
  8.3 3.3 %place.1 = (bf16[128,1024]{1,0:T(8,128)(2,1)S(1)}, bf16[128,1024]{1,0:T(8,128)(2,1)S(1)}, bf16[128,1024]{1,0:T(8,128)(2,1)S(1)}, bf16[128,1024]{1,0:T(8,128)(2,1...) custom-call(s32[3]{0:T(128)S(1)} %pad_add_fusion.spot_ref, ...), custom_call_target="tpu_custom_call" | custom-call | tf_op jit(solution)/shard_map/place/pallas_call | solution.py:337
  11.7 3.9 %collective-permute-start.4 = (bf16[128,1024]{1,0:T(8,128)(2,1)S(1)}, bf16[128,1024]{1,0:T(8,128)(2,1)S(1)}, u32[]{:S(2)}, u32[]{:S(2)}) collective-permute-start(bf16[128,1024]{1,0:T(8,128)(2,1)S(1)} %get-tuple-element.17), channel_id=1, source_target_pairs={{0,56},{1,57},{2,58},{3,59},{4,60},{5,61},{6,62},{7,63},{8,0},{9,1... | collective-permute-start | bytes 786440 | tf_op jit(solution)/shard_map/ppermute | solution.py:314
  15.6 3.6 %collective-permute-start.6 = (bf16[128,1024]{1,0:T(8,128)(2,1)S(1)}, bf16[128,1024]{1,0:T(8,128)(2,1)S(1)}, u32[]{:S(2)}, u32[]{:S(2)}) collective-permute-start(bf16[128,1024]{1,0:T(8,128)(2,1)S(1)} %get-tuple-element.19), channel_id=1, source_target_pairs={{0,48},{1,49},{2,50},{3,51},{4,52},{5,53},{6,54},{7,55},{8,56},{9,... | collective-permute-start | bytes 786440 | tf_op jit(solution)/shard_map/ppermute | solution.py:314
  19.9 2.0 %collective-permute-done.3 = bf16[128,1024]{1,0:T(8,128)(2,1)S(1)} collective-permute-done((bf16[128,1024]{1,0:T(8,128)(2,1)S(1)}, bf16[128,1024]{1,0:T(8,128)(2,1)S(1)}, u32[]{:S(2)}, u32[]{:S(2)}) %collective-permute-start.3) | collective-permute-done | bytes 262176 | tf_op jit(solution)/shard_map/ppermute | solution.py:314
  21.9 0.7 constant_dynamic-update-slice_fusion.3
  23.4 5.7 %collective-permute-done.5 = bf16[128,1024]{1,0:T(8,128)(2,1)S(1)} collective-permute-done((bf16[128,1024]{1,0:T(8,128)(2,1)S(1)}, bf16[128,1024]{1,0:T(8,128)(2,1)S(1)}, u32[]{:S(2)}, u32[]{:S(2)}) %collective-permute-start.5) | collective-permute-done | bytes 262176 | tf_op jit(solution)/shard_map/ppermute | solution.py:314
  29.8 2.4 %collective-permute-done.6 = bf16[128,1024]{1,0:T(8,128)(2,1)S(1)} collective-permute-done((bf16[128,1024]{1,0:T(8,128)(2,1)S(1)}, bf16[128,1024]{1,0:T(8,128)(2,1)S(1)}, u32[]{:S(2)}, u32[]{:S(2)}) %collective-permute-start.6) | collective-permute-done | bytes 262176 | tf_op jit(solution)/shard_map/ppermute | solution.py:314
  32.9 4.0 %all-to-all-start = ((bf16[4,160,1024]{2,1,0:T(8,128)(2,1)}), bf16[4,160,1024]{2,1,0:T(8,128)(2,1)S(1)}, u32[]{:S(2)}, u32[]{:S(2)}) async-start(bf16[4,160,1024]{2,1,0:T(8,128)(2,1)} %constant_dynamic-update-slice_fusion), calls=%async_computation | async-start | bytes 2621440 | tf_op jit(solution)/shard_map/all_to_all | solution.py:318
  36.9 2.1 %collective-permute-start.7 = (bf16[128,1024]{1,0:T(8,128)(2,1)S(1)}, bf16[128,1024]{1,0:T(8,128)(2,1)S(1)}, u32[]{:S(2)}, u32[]{:S(2)}) collective-permute-start(bf16[128,1024]{1,0:T(8,128)(2,1)S(1)} %get-tuple-element.20), channel_id=1, source_target_pairs={{0,24},{1,25},{2,26},{3,27},{4,28},{5,29},{6,30},{7,31},{8,32},{9,... | collective-permute-start | bytes 786440 | tf_op jit(solution)/shard_map/ppermute | solution.py:314
  39.0 3.3 %collective-permute-start.8 = (bf16[128,1024]{1,0:T(8,128)(2,1)S(1)}, bf16[128,1024]{1,0:T(8,128)(2,1)S(1)}, u32[]{:S(2)}, u32[]{:S(2)}) collective-permute-start(bf16[128,1024]{1,0:T(8,128)(2,1)S(1)} %get-tuple-element.21), channel_id=1, source_target_pairs={{0,40},{1,41},{2,42},{3,43},{4,44},{5,45},{6,46},{7,47},{8,48},{9,... | collective-permute-start | bytes 786440 | tf_op jit(solution)/shard_map/ppermute | solution.py:314
  42.3 3.4 %collective-permute-start.9 = (bf16[128,1024]{1,0:T(8,128)(2,1)S(1)}, bf16[128,1024]{1,0:T(8,128)(2,1)S(1)}, u32[]{:S(2)}, u32[]{:S(2)}) collective-permute-start(bf16[128,1024]{1,0:T(8,128)(2,1)S(1)} %get-tuple-element.22), channel_id=1, source_target_pairs={{0,32},{1,33},{2,34},{3,35},{4,36},{5,37},{6,38},{7,39},{8,40},{9,... | collective-permute-start | bytes 786440 | tf_op jit(solution)/shard_map/ppermute | solution.py:314
  45.7 13.9 %collective-permute-done.7 = bf16[128,1024]{1,0:T(8,128)(2,1)S(1)} collective-permute-done((bf16[128,1024]{1,0:T(8,128)(2,1)S(1)}, bf16[128,1024]{1,0:T(8,128)(2,1)S(1)}, u32[]{:S(2)}, u32[]{:S(2)}) %collective-permute-start.7) | collective-permute-done | bytes 262176 | tf_op jit(solution)/shard_map/ppermute | solution.py:314
  59.6 2.8 %collective-permute-done.9 = bf16[128,1024]{1,0:T(8,128)(2,1)S(1)} collective-permute-done((bf16[128,1024]{1,0:T(8,128)(2,1)S(1)}, bf16[128,1024]{1,0:T(8,128)(2,1)S(1)}, u32[]{:S(2)}, u32[]{:S(2)}) %collective-permute-start.9) | collective-permute-done | bytes 262176 | tf_op jit(solution)/shard_map/ppermute | solution.py:314
  62.4 0.9 pad_maximum_fusion
  63.3 4.6 %all-to-all-start.1 = ((bf16[4,96,1024]{2,1,0:T(8,128)(2,1)}), bf16[4,96,1024]{2,1,0:T(8,128)(2,1)S(1)}, u32[]{:S(2)}, u32[]{:S(2)}) async-start(bf16[4,96,1024]{2,1,0:T(8,128)(2,1)} %pad_maximum_fusion), calls=%async_computation.1 | async-start | bytes 1572864 | tf_op jit(solution)/shard_map/all_to_all | solution.py:318
  68.5 2.0 %collective-permute-start.10 = (bf16[640,1024]{1,0:T(8,128)(2,1)S(1)}, bf16[640,1024]{1,0:T(8,128)(2,1)}, u32[]{:S(2)}, u32[]{:S(2)}) collective-permute-start(bf16[640,1024]{1,0:T(8,128)(2,1)S(1)} %bitcast.26), channel_id=1, source_target_pairs={{0,3},{1,0},{2,1},{3,2},{4,196},{5,197},{6,198},{7,199},{8,11},{9,... | collective-permute-start | bytes 3932168 | tf_op jit(solution)/shard_map/ppermute | solution.py:314
  70.6 5.9 %all-to-all-done.1 = bf16[4,96,1024]{2,1,0:T(8,128)(2,1)S(1)} async-done(((bf16[4,96,1024]{2,1,0:T(8,128)(2,1)}), bf16[4,96,1024]{2,1,0:T(8,128)(2,1)S(1)}, u32[]{:S(2)}, u32[]{:S(2)}) %all-to-all-start.1) | async-done | bytes 786464 | tf_op jit(solution)/shard_map/all_to_all | solution.py:318
  76.9 2.2 %collective-permute-start.11 = (bf16[384,1024]{1,0:T(8,128)(2,1)S(1)}, bf16[384,1024]{1,0:T(8,128)(2,1)S(1)}, u32[]{:S(2)}, u32[]{:S(2)}) collective-permute-start(bf16[384,1024]{1,0:T(8,128)(2,1)S(1)} %bitcast.30), channel_id=1, source_target_pairs={{0,3},{1,0},{2,1},{3,2},{4,196},{5,197},{6,198},{7,199},{8,11},{9,... | collective-permute-start | bytes 2359304 | tf_op jit(solution)/shard_map/ppermute | solution.py:314
  79.1 26.2 %all_to_all.20 = f32[32,1,1,128]{3,2,1,0:T(1,128)S(1)} all-to-all(f32[32,1,1,128]{3,2,1,0:T(1,128)S(1)} %bitcast.39), channel_id=1, replica_groups={{0,8,16,24,32,40,48,56,64,72,80,88,96,104,112,120,128,136,144,152,160,1..., dimensions={0} | all-to-all | bytes 32768 | tf_op jit(solution)/shard_map/all_to_all | solution.py:318
  106.0 3.9 %collective-permute-done.15.refs_8_ = f32[8,128]{1,0:T(8,128)S(1)} collective-permute-done((f32[8,128]{1,0:T(8,128)S(1)}, f32[8,128]{1,0:T(8,128)S(1)}, u32[]{:S(2)}, u32[]{:S(2)}) %collective-permute-start.15) | collective-permute-done | bytes 4128 | tf_op jit(solution)/shard_map/ppermute | solution.py:314
  110.0 3.0 %own.1.refs_9_ = f32[8,128]{1,0:T(8,128)S(1)} custom-call(s32[3]{0:T(128)S(1)} %pad_add_fusion.spot_ref, bf16[640,1024]{1,0:T(8,128)(2,1)S(1)} %bitcast.27, bf16[384,1024]{1,0:T(8,128)(2,1)S(1)} %bitcast.31, f32[8,128]{1,0:T(8,128)S(1)} %spread.1.refs_2_.refs_6_), custom_call_target="tpu_custom_call" | custom-call | tf_op jit(solution)/shard_map/own/pallas_call | solution.py:337
  113.1 5.1 %cross.1 = f32[32,128]{1,0:T(8,128)S(1)} custom-call(s32[3]{0:T(128)S(1)} %pad_add_fusion.spot_ref, bf16[640,1024]{1,0:T(8,128)(2,1)S(1)} %bitcast.28, bf16[384,1024]{1,0:T(8,128)(2,1)S(1)} %bitcast.32, bf16[640,1024]{1,0:T(8,128)(2,1)} %collective-permute-done.10.refs_2_, bf16[384,1024]{1,0:T(8,128)(2,1)S(1)} %collective-permute-done.11.refs_3_, ...), custom_call_target="tpu_custom_call" | custom-call | tf_op jit(solution)/shard_map/cross/pallas_call | solution.py:337
  118.2 16.2 %all_to_all.21 = f32[32,1,1,128]{3,2,1,0:T(1,128)S(1)} all-to-all(f32[32,1,1,128]{3,2,1,0:T(1,128)S(1)} %bitcast.34), channel_id=1, replica_groups={{0,8,16,24,32,40,48,56,64,72,80,88,96,104,112,120,128,136,144,152,160,1..., dimensions={0} | all-to-all | bytes 32768 | tf_op jit(solution)/shard_map/all_to_all | solution.py:318
  135.0 0.9 collective-permute-start.16
  135.9 1.4 collective-permute-done.17.above_ref
  137.3 1.5 %collective-permute-done.16.below_ref = f32[32,128]{1,0:T(8,128)S(1)} collective-permute-done((f32[32,128]{1,0:T(8,128)S(1)}, f32[32,128]{1,0:T(8,128)S(1)}, u32[]{:S(2)}, u32[]{:S(2)}) %collective-permute-start.16) | collective-permute-done | bytes 16416 | tf_op jit(solution)/shard_map/ppermute | solution.py:314
  138.8 1.0 fetch.1
  139.8 6.7 %collective-permute-start.18 = (f32[512]{0:T(512)S(1)}, f32[512]{0:T(512)S(1)}, u32[]{:S(2)}, u32[]{:S(2)}) collective-permute-start(f32[512]{0:T(512)S(1)} %bitcast.53), channel_id=1, source_target_pairs={{0,4},{1,5},{2,6},{3,7},{4,0},{5,1},{6,2},{7,3},{8,12},{9,13},{10,... | collective-permute-start | bytes 6152 | tf_op jit(solution)/shard_map/ppermute | solution.py:314
  146.5 0.8 collective-permute-done.18
  (34 shorter events, 7.9 us)
Async XLA Ops:
  0.0 5.7 %collective-permute-start = (bf16[512,1024]{1,0:T(8,128)(2,1)}, bf16[512,1024]{1,0:T(8,128)(2,1)S(1)}, u32[]{:S(2)}, u32[]{:S(2)}) collective-permute-start(bf16[512,1024]{1,0:T(8,128)(2,1)} %refs_0_.1), channel_id=1, source_target_pairs={{0,4},{1,5},{2,6},{3,7},{4,0},{5,1},{6,2},{7,3},{8,12},{9,13},{10,... | collective-permute-start | bytes 3145736 | tf_op jit(solution)/shard_map/ppermute | solution.py:314
  3.2 2.5 %collective-permute-start.1 = (s32[1,512]{1,0:T(1,128)}, s32[1,512]{1,0:T(1,128)S(1)}, u32[]{:S(2)}, u32[]{:S(2)}) collective-permute-start(s32[1,512]{1,0:T(1,128)} %bitcast.40), channel_id=1, source_target_pairs={{0,4},{1,5},{2,6},{3,7},{4,0},{5,1},{6,2},{7,3},{8,12},{9,13},{10,... | collective-permute-start | bytes 6152 | tf_op jit(solution)/shard_map/ppermute | solution.py:314
  3.2 2.5 %collective-permute-start.2 = (s32[1,512]{1,0:T(1,128)}, s32[1,512]{1,0:T(1,128)S(1)}, u32[]{:S(2)}, u32[]{:S(2)}) collective-permute-start(s32[1,512]{1,0:T(1,128)} %bitcast.43), channel_id=1, source_target_pairs={{0,4},{1,5},{2,6},{3,7},{4,0},{5,1},{6,2},{7,3},{8,12},{9,13},{10,... | collective-permute-start | bytes 6152 | tf_op jit(solution)/shard_map/ppermute | solution.py:314
  5.7 1.2 copy-start
  7.0 0.7 copy-start.1
  7.7 0.7 copy-start.3
  11.6 10.3 %collective-permute-start.3 = (bf16[128,1024]{1,0:T(8,128)(2,1)S(1)}, bf16[128,1024]{1,0:T(8,128)(2,1)S(1)}, u32[]{:S(2)}, u32[]{:S(2)}) collective-permute-start(bf16[128,1024]{1,0:T(8,128)(2,1)S(1)} %get-tuple-element.16), channel_id=1, source_target_pairs={{0,8},{1,9},{2,10},{3,11},{4,12},{5,13},{6,14},{7,15},{8,16},{9,17... | collective-permute-start | bytes 786440 | tf_op jit(solution)/shard_map/ppermute | solution.py:314
  11.7 10.9 %collective-permute-start.4 = (bf16[128,1024]{1,0:T(8,128)(2,1)S(1)}, bf16[128,1024]{1,0:T(8,128)(2,1)S(1)}, u32[]{:S(2)}, u32[]{:S(2)}) collective-permute-start(bf16[128,1024]{1,0:T(8,128)(2,1)S(1)} %get-tuple-element.17), channel_id=1, source_target_pairs={{0,56},{1,57},{2,58},{3,59},{4,60},{5,61},{6,62},{7,63},{8,0},{9,1... | collective-permute-start | bytes 786440 | tf_op jit(solution)/shard_map/ppermute | solution.py:314
  15.6 13.5 %collective-permute-start.5 = (bf16[128,1024]{1,0:T(8,128)(2,1)S(1)}, bf16[128,1024]{1,0:T(8,128)(2,1)S(1)}, u32[]{:S(2)}, u32[]{:S(2)}) collective-permute-start(bf16[128,1024]{1,0:T(8,128)(2,1)S(1)} %get-tuple-element.18), channel_id=1, source_target_pairs={{0,16},{1,17},{2,18},{3,19},{4,20},{5,21},{6,22},{7,23},{8,24},{9,... | collective-permute-start | bytes 786440 | tf_op jit(solution)/shard_map/ppermute | solution.py:314
  15.6 16.6 %collective-permute-start.6 = (bf16[128,1024]{1,0:T(8,128)(2,1)S(1)}, bf16[128,1024]{1,0:T(8,128)(2,1)S(1)}, u32[]{:S(2)}, u32[]{:S(2)}) collective-permute-start(bf16[128,1024]{1,0:T(8,128)(2,1)S(1)} %get-tuple-element.19), channel_id=1, source_target_pairs={{0,48},{1,49},{2,50},{3,51},{4,52},{5,53},{6,54},{7,55},{8,56},{9,... | collective-permute-start | bytes 786440 | tf_op jit(solution)/shard_map/ppermute | solution.py:314
  32.9 30.4 %all-to-all-start = ((bf16[4,160,1024]{2,1,0:T(8,128)(2,1)}), bf16[4,160,1024]{2,1,0:T(8,128)(2,1)S(1)}, u32[]{:S(2)}, u32[]{:S(2)}) async-start(bf16[4,160,1024]{2,1,0:T(8,128)(2,1)} %constant_dynamic-update-slice_fusion), calls=%async_computation | async-start | bytes 2621440 | tf_op jit(solution)/shard_map/all_to_all | solution.py:318
  36.9 22.7 %collective-permute-start.7 = (bf16[128,1024]{1,0:T(8,128)(2,1)S(1)}, bf16[128,1024]{1,0:T(8,128)(2,1)S(1)}, u32[]{:S(2)}, u32[]{:S(2)}) collective-permute-start(bf16[128,1024]{1,0:T(8,128)(2,1)S(1)} %get-tuple-element.20), channel_id=1, source_target_pairs={{0,24},{1,25},{2,26},{3,27},{4,28},{5,29},{6,30},{7,31},{8,32},{9,... | collective-permute-start | bytes 786440 | tf_op jit(solution)/shard_map/ppermute | solution.py:314
  39.0 20.6 %collective-permute-start.8 = (bf16[128,1024]{1,0:T(8,128)(2,1)S(1)}, bf16[128,1024]{1,0:T(8,128)(2,1)S(1)}, u32[]{:S(2)}, u32[]{:S(2)}) collective-permute-start(bf16[128,1024]{1,0:T(8,128)(2,1)S(1)} %get-tuple-element.21), channel_id=1, source_target_pairs={{0,40},{1,41},{2,42},{3,43},{4,44},{5,45},{6,46},{7,47},{8,48},{9,... | collective-permute-start | bytes 786440 | tf_op jit(solution)/shard_map/ppermute | solution.py:314
  42.3 20.1 %collective-permute-start.9 = (bf16[128,1024]{1,0:T(8,128)(2,1)S(1)}, bf16[128,1024]{1,0:T(8,128)(2,1)S(1)}, u32[]{:S(2)}, u32[]{:S(2)}) collective-permute-start(bf16[128,1024]{1,0:T(8,128)(2,1)S(1)} %get-tuple-element.22), channel_id=1, source_target_pairs={{0,32},{1,33},{2,34},{3,35},{4,36},{5,37},{6,38},{7,39},{8,40},{9,... | collective-permute-start | bytes 786440 | tf_op jit(solution)/shard_map/ppermute | solution.py:314
  63.3 13.1 %all-to-all-start.1 = ((bf16[4,96,1024]{2,1,0:T(8,128)(2,1)}), bf16[4,96,1024]{2,1,0:T(8,128)(2,1)S(1)}, u32[]{:S(2)}, u32[]{:S(2)}) async-start(bf16[4,96,1024]{2,1,0:T(8,128)(2,1)} %pad_maximum_fusion), calls=%async_computation.1 | async-start | bytes 1572864 | tf_op jit(solution)/shard_map/all_to_all | solution.py:318
  67.9 45.2 %collective-permute-start.12 = (bf16[640,1024]{1,0:T(8,128)(2,1)S(1)}, bf16[640,1024]{1,0:T(8,128)(2,1)S(1)}, u32[]{:S(2)}, u32[]{:S(2)}) collective-permute-start(bf16[640,1024]{1,0:T(8,128)(2,1)S(1)} %bitcast.25), channel_id=1, source_target_pairs={{0,1},{1,2},{2,3},{3,0},{4,68},{5,69},{6,70},{7,71},{8,9},{9,10},{... | collective-permute-start | bytes 3932168 | tf_op jit(solution)/shard_map/ppermute | solution.py:314
  68.5 44.5 %collective-permute-start.10 = (bf16[640,1024]{1,0:T(8,128)(2,1)S(1)}, bf16[640,1024]{1,0:T(8,128)(2,1)}, u32[]{:S(2)}, u32[]{:S(2)}) collective-permute-start(bf16[640,1024]{1,0:T(8,128)(2,1)S(1)} %bitcast.26), channel_id=1, source_target_pairs={{0,3},{1,0},{2,1},{3,2},{4,196},{5,197},{6,198},{7,199},{8,11},{9,... | collective-permute-start | bytes 3932168 | tf_op jit(solution)/shard_map/ppermute | solution.py:314
  76.4 36.6 %collective-permute-start.13 = (bf16[384,1024]{1,0:T(8,128)(2,1)S(1)}, bf16[384,1024]{1,0:T(8,128)(2,1)S(1)}, u32[]{:S(2)}, u32[]{:S(2)}) collective-permute-start(bf16[384,1024]{1,0:T(8,128)(2,1)S(1)} %bitcast.29), channel_id=1, source_target_pairs={{0,1},{1,2},{2,3},{3,0},{4,68},{5,69},{6,70},{7,71},{8,9},{9,10},{... | collective-permute-start | bytes 2359304 | tf_op jit(solution)/shard_map/ppermute | solution.py:314
  76.9 36.1 %collective-permute-start.11 = (bf16[384,1024]{1,0:T(8,128)(2,1)S(1)}, bf16[384,1024]{1,0:T(8,128)(2,1)S(1)}, u32[]{:S(2)}, u32[]{:S(2)}) collective-permute-start(bf16[384,1024]{1,0:T(8,128)(2,1)S(1)} %bitcast.30), channel_id=1, source_target_pairs={{0,3},{1,0},{2,1},{3,2},{4,196},{5,197},{6,198},{7,199},{8,11},{9,... | collective-permute-start | bytes 2359304 | tf_op jit(solution)/shard_map/ppermute | solution.py:314
  105.9 4.0 %collective-permute-start.15 = (f32[8,128]{1,0:T(8,128)S(1)}, f32[8,128]{1,0:T(8,128)S(1)}, u32[]{:S(2)}, u32[]{:S(2)}) collective-permute-start(f32[8,128]{1,0:T(8,128)S(1)} %spread.1.refs_2_.refs_6_), channel_id=1, source_target_pairs={{0,1},{1,2},{2,3},{3,0},{4,68},{5,69},{6,70},{7,71},{8,9},{9,10},{... | collective-permute-start | bytes 12296 | tf_op jit(solution)/shard_map/ppermute | solution.py:314
  110.0 3.1 %collective-permute-start.14 = (f32[8,128]{1,0:T(8,128)S(1)}, f32[8,128]{1,0:T(8,128)S(1)}, u32[]{:S(2)}, u32[]{:S(2)}) collective-permute-start(f32[8,128]{1,0:T(8,128)S(1)} %spread.1.refs_2_.refs_6_), channel_id=1, source_target_pairs={{0,3},{1,0},{2,1},{3,2},{4,196},{5,197},{6,198},{7,199},{8,11},{9,... | collective-permute-start | bytes 12296 | tf_op jit(solution)/shard_map/ppermute | solution.py:314
  113.0 25.8 %copy-start.2 = (s32[512,1]{0,1:T(1,128)S(1)}, s32[512,1]{0,1:T(1,128)}, u32[]{:S(2)}) copy-start(s32[512,1]{0,1:T(1,128)} %param.4) | copy-start | bytes 6148
  134.4 2.9 %collective-permute-start.17 = (f32[32,128]{1,0:T(8,128)S(1)}, f32[32,128]{1,0:T(8,128)S(1)}, u32[]{:S(2)}, u32[]{:S(2)}) collective-permute-start(f32[32,128]{1,0:T(8,128)S(1)} %bitcast.36), channel_id=1, source_target_pairs={{0,3},{1,0},{2,1},{3,2},{4,196},{5,197},{6,198},{7,199},{8,11},{9,... | collective-permute-start | bytes 49160 | tf_op jit(solution)/shard_map/ppermute | solution.py:314
  135.0 3.8 %collective-permute-start.16 = (f32[32,128]{1,0:T(8,128)S(1)}, f32[32,128]{1,0:T(8,128)S(1)}, u32[]{:S(2)}, u32[]{:S(2)}) collective-permute-start(f32[32,128]{1,0:T(8,128)S(1)} %bitcast.37), channel_id=1, source_target_pairs={{0,1},{1,2},{2,3},{3,0},{4,68},{5,69},{6,70},{7,71},{8,9},{9,10},{... | collective-permute-start | bytes 49160 | tf_op jit(solution)/shard_map/ppermute | solution.py:314
  139.8 7.5 %collective-permute-start.18 = (f32[512]{0:T(512)S(1)}, f32[512]{0:T(512)S(1)}, u32[]{:S(2)}, u32[]{:S(2)}) collective-permute-start(f32[512]{0:T(512)S(1)} %bitcast.53), channel_id=1, source_target_pairs={{0,4},{1,5},{2,6},{3,7},{4,0},{5,1},{6,2},{7,3},{8,12},{9,13},{10,... | collective-permute-start | bytes 6152 | tf_op jit(solution)/shard_map/ppermute | solution.py:314

commit v3 on v2

v3 whole, which is shorter than its diff:
```python
import functools

import jax
import jax.numpy as jnp
from jax import lax
from jax.experimental import pallas as pl
from jax.experimental.pallas import tpu as pltpu
from jax.sharding import PartitionSpec as P

epsilon = 1e-06
capacity = 16
lanes = 128
wide = 256
cores = 2
places = 4
depth = 8
field = cores * capacity
cuts = (1024,)
contract_last = (((1,), (1,)), ((), ()))
contract_first = (((1,), (0,)), ((), ()))
everyone = ("ingest", "span")


def params():
    return pltpu.CompilerParams(vmem_limit_bytes=40 * 1024 * 1024)


def device(y, z, core, x):
    return ((y * depth + z) * cores + core) * places + x


def pairs(move):
    found = []
    for y in range(places):
        for z in range(depth):
            for core in range(cores):
                for x in range(places):
                    found.append((device(y, z, core, x), device(*move(y, z, core, x))))
    return found


def other_core():
    return pairs(lambda y, z, core, x: (y, z, 1 - core, x))


def beside(step, swapped=False):
    def move(y, z, core, x):
        found = 1 - core if swapped else core
        if core == 0:
            return (y, z, found, (x + step) % places)
        return ((y + step) % places, z, found, x)

    return pairs(move)


def plane_teams():
    spots, levels = range(places), range(depth)
    return [[device(i, z, 0, x) for i in spots for z in levels] for x in spots] + [
        [device(y, z, 1, i) for i in spots for z in levels] for y in spots
    ]


def rank_rows(owner, groups):
    rows = owner.shape[1]
    belongs = lax.broadcasted_iota(jnp.int32, (groups, rows), 0) == owner
    onehot = belongs.astype(jnp.bfloat16)
    earlier = lax.broadcasted_iota(jnp.int32, (rows, rows), 0) < lax.broadcasted_iota(
        jnp.int32, (rows, rows), 1
    )
    before = lax.dot_general(
        onehot, earlier.astype(jnp.bfloat16), contract_first, preferred_element_type=jnp.float32
    )
    return jnp.sum(jnp.where(belongs, before, 0.0), axis=0, keepdims=True).astype(jnp.int32)


def owned_here(owner, core):
    half = owner.shape[1]
    table = lax.broadcasted_iota(jnp.int32, (places * depth, half), 0)
    return (table == owner // cores) & (owner % cores == core)


def place_kernel(groups, spot_ref, *refs):
    embs, owners, clusters = refs[0:2], refs[2:4], refs[4:6]
    *sends, ids_ref, within_ref = refs[6:]
    core = spot_ref[0]
    slots, units, named, spots = [], [], [], []
    for side in range(cores):
        owner = owners[side][...]
        within = rank_rows(owner, groups)
        if side == 0:
            within_ref[...] = within
        slot = owner // cores * field + side * capacity + within
        slots.append(jnp.where(owner % cores == core, slot, -1))
        values = embs[side][...].astype(jnp.float32)
        squared = jnp.sum(values * values, axis=1, keepdims=True)
        units.append((values * lax.rsqrt(squared + epsilon)).astype(jnp.bfloat16))
        here = owned_here(owner, core).astype(jnp.bfloat16)
        named.append(here * (clusters[side][...] + 1).astype(jnp.bfloat16))
        spots.append(within + side * capacity)
    slot = jnp.concatenate(slots, axis=1)
    unit = jnp.concatenate(units, axis=0)
    rows = slot.shape[1]
    room = sends[0].shape[0]
    put = (lax.broadcasted_iota(jnp.int32, (room, rows), 0) == slot).astype(jnp.bfloat16)
    base = 0
    for ref in sends:
        for start in range(0, ref.shape[1], wide):
            ref[:, start : start + wide] = lax.dot_general(
                put,
                unit[:, base + start : base + start + wide],
                contract_first,
                preferred_element_type=jnp.float32,
            ).astype(jnp.bfloat16)
        base += ref.shape[1]
    lane = lax.broadcasted_iota(jnp.int32, (lanes, rows), 0)
    into = (lane == jnp.concatenate(spots, axis=1)).astype(jnp.bfloat16)
    ids_ref[...] = (
        lax.dot_general(
            jnp.concatenate(named, axis=1),
            into,
            contract_last,
            preferred_element_type=jnp.float32,
        )
        - 1.0
    )


def spread_kernel(ids_ref, out_ref):
    blocks, count = out_ref.shape[0], lanes // field
    lane = lax.broadcasted_iota(jnp.int32, (blocks, lanes), 1)
    total = ids_ref[pl.ds(0, blocks, stride=count), :]
    for q in range(1, count):
        piece = pltpu.roll(ids_ref[pl.ds(q, blocks, stride=count), :], field * q, 1)
        total = jnp.where(lane // field == q, piece, total)
    out_ref[...] = total


def to_column(row):
    return jnp.transpose(jnp.broadcast_to(row, (lanes, lanes)))


def columns_of(ids):
    return jnp.concatenate([to_column(ids[b : b + 1, :]) for b in range(ids.shape[0])], axis=0)


def to_rows(tile):
    return jnp.concatenate(
        [
            jnp.max(jnp.transpose(tile[b * lanes : (b + 1) * lanes, :]), axis=0, keepdims=True)
            for b in range(tile.shape[0] // lanes)
        ],
        axis=0,
    )


def scan_block(lefts, rights, left_ids, right_ids, best, skip):
    total = None
    for left, right in zip(lefts, rights):
        part = lax.dot_general(left, right, contract_last, preferred_element_type=jnp.float32)
        total = part if total is None else total + part
    tops = []
    for half in range(wide // lanes):
        scores = total[:, half * lanes : (half + 1) * lanes]
        ids = right_ids[half : half + 1, :]
        same = left_ids == jnp.where(ids < 0, -2.0, ids)
        if skip is not None:
            row = lax.broadcasted_iota(jnp.int32, scores.shape, 0)
            column = lax.broadcasted_iota(jnp.int32, scores.shape, 1)
            same = same & (row - column != skip + half * lanes)
        masked = jnp.where(same, scores, -1.0)
        best = masked if best is None else jnp.maximum(best, masked)
        tops.append(jnp.max(masked, axis=0, keepdims=True))
    return best, tops


def own_kernel(*refs):
    *own, ids_ref, out_ref = refs
    ids = ids_ref[...]
    rows = ids.shape[0] * lanes
    columns = columns_of(ids)
    lefts = [r[...] for r in own]
    best = None
    per = wide // lanes
    for at in range(rows // wide):
        best, _ = scan_block(
            lefts,
            [r[at * wide : (at + 1) * wide, :] for r in own],
            columns,
            ids[at * per : (at + 1) * per, :],
            best,
            at * wide,
        )
    out_ref[...] = to_rows(best)


def cross_kernel(parts, spot_ref, *refs):
    own, after, before = refs[:parts], refs[parts : 2 * parts], refs[2 * parts : 3 * parts]
    ids_ref, after_ids_ref, before_ids_ref, inside_ref, out_ref = refs[3 * parts :]
    low = spot_ref[1] == 1
    ids, after_ids, before_ids = ids_ref[...], after_ids_ref[...], before_ids_ref[...]
    blocks = ids.shape[0]
    rows = blocks * lanes
    half = rows // 2
    columns = columns_of(ids)
    right_ids = jnp.where(low, after_ids, before_ids)
    left_ids = jnp.where(low, before_ids[: blocks // 2, :], after_ids[blocks // 2 :, :])
    left_columns = columns_of(left_ids)
    left = [jnp.where(low, b[:half, :], a[half:, :]) for a, b in zip(after, before)]
    lefts = [r[...] for r in own]
    per = wide // lanes
    best, far, up, side = None, None, [], []
    for at in range(rows // wide):
        spot = slice(at * wide, (at + 1) * wide)
        near = [a[spot, :] for a in after]
        right = [jnp.where(low, a, b[spot, :]) for a, b in zip(near, before)]
        cut = slice(at * per, (at + 1) * per)
        best, tops = scan_block(lefts, near, columns, after_ids[cut, :], best, None)
        up += tops
        far, tops = scan_block(left, right, left_columns, right_ids[cut, :], far, None)
        side += tops
    up, side = jnp.concatenate(up, axis=0), jnp.concatenate(side, axis=0)
    mine = jnp.maximum(to_rows(best), inside_ref[...])
    found = to_rows(far)
    blank = jnp.full(found.shape, -1.0, jnp.float32)
    placed = jnp.where(
        low, jnp.concatenate([found, blank], axis=0), jnp.concatenate([blank, found], axis=0)
    )
    up = jnp.maximum(up, jnp.where(low, side, placed))
    down = jnp.where(low, placed, side)
    lane = lax.broadcasted_iota(jnp.int32, (blocks, lanes), 1)
    count = lanes // field
    for q in range(count):
        turned = [
            values if (i - q) % count == 0 else pltpu.roll(values, field * ((i - q) % count), 1)
            for i, values in enumerate((mine, up, down))
        ]
        joined = jnp.where(
            lane < field, turned[0], jnp.where(lane < 2 * field, turned[1], turned[2])
        )
        out_ref[pl.ds(q, blocks, stride=count), :] = joined


def fetch_kernel(spot_ref, *refs):
    *tables, owner_ref, within_ref, out_ref = refs
    core = spot_ref[0]
    joined = []
    for side in range(cores):
        own, below, above = tables[3 * side : 3 * side + 3]
        joined.append(
            jnp.maximum(
                own[...],
                jnp.maximum(
                    pltpu.roll(below[...], lanes - field, 1),
                    pltpu.roll(above[...], lanes - 2 * field, 1),
                ),
            )
        )
    spread = lax.broadcasted_iota(jnp.int32, joined[0].shape, 1)
    rest = jnp.where(spread < capacity, joined[0], joined[1])
    owner = owner_ref[...]
    rows = owner.shape[1]
    team = lax.broadcasted_iota(jnp.int32, (places * depth, rows), 0)
    onehot = (team == owner // cores).astype(jnp.bfloat16)
    found = jnp.zeros((lanes, rows), jnp.float32)
    for _ in range(3):
        piece = rest.astype(jnp.bfloat16)
        rest = rest - piece.astype(jnp.float32)
        found = found + lax.dot_general(
            piece, onehot, (((0,), (0,)), ((), ())), preferred_element_type=jnp.float32
        )
    lane = lax.broadcasted_iota(jnp.int32, (lanes, rows), 0)
    within = within_ref[...] + jnp.where(owner % cores == core, 0, capacity)
    out_ref[...] = jnp.sum(jnp.where(lane == within, found, 0.0), axis=0, keepdims=True)


def send(values, route):
    return lax.ppermute(values, everyone, route)


def trade(values, teams):
    return lax.all_to_all(
        values, everyone, split_axis=0, concat_axis=0, axis_index_groups=teams, tiled=True
    )


def shards(embeddings, owner, cluster):
    rows, width = embeddings.shape
    groups = lax.axis_size("ingest")
    spots = groups * capacity
    blocks = spots // lanes
    each = places * depth
    f32 = jnp.float32
    at, x = lax.axis_index("ingest"), lax.axis_index("span")
    core, y = at % cores, at // (cores * depth)
    low = jnp.where(core == 0, x, y) < places // 2
    spot = jnp.stack([core, low.astype(jnp.int32)]).astype(jnp.int32)
    smem, vmem = pl.BlockSpec(memory_space=pltpu.SMEM), pl.BlockSpec(memory_space=pltpu.VMEM)

    def call(kernel, out_shape, name, *args):
        return pl.pallas_call(
            kernel,
            out_shape=out_shape,
            in_specs=[smem if a is spot else vmem for a in args],
            compiler_params=params(),
            name=name,
        )(*args)

    swap = other_core()
    owner = owner.reshape(1, rows)
    cluster = cluster.reshape(1, rows)
    others = send(owner, swap)
    other_cluster = send(cluster, swap)
    other_rows = send(embeddings, swap)
    *parts, ids, within = call(
        functools.partial(place_kernel, groups),
        [jax.ShapeDtypeStruct((spots, w), jnp.bfloat16) for w in cuts]
        + [
            jax.ShapeDtypeStruct((each, lanes), f32),
            jax.ShapeDtypeStruct((1, rows), jnp.int32),
        ],
        "place",
        spot,
        embeddings,
        other_rows,
        owner,
        others,
        cluster,
        other_cluster,
    )
    teams = plane_teams()
    own, after, before = [], [], []
    for part in parts:
        got = trade(part.reshape(each, field, part.shape[1]), teams).reshape(part.shape)
        own.append(got)
        before.append(send(got, beside(1)))
        after.append(send(got, beside(-1)))
    ids, own[-1] = lax.optimization_barrier((ids, own[-1]))
    ids = trade(ids.reshape(each, 1, 1, lanes), teams).reshape(each, lanes)
    ids = call(spread_kernel, jax.ShapeDtypeStruct((blocks, lanes), f32), "spread", ids)
    before_ids, after_ids = send(ids, beside(1)), send(ids, beside(-1))
    inside = call(own_kernel, jax.ShapeDtypeStruct((blocks, lanes), f32), "own", *own, ids)
    best = call(
        functools.partial(cross_kernel, len(own)),
        jax.ShapeDtypeStruct((each, lanes), f32),
        "cross",
        spot,
        *own,
        *after,
        *before,
        ids,
        after_ids,
        before_ids,
        inside,
    )
    back = trade(best.reshape(each, 1, 1, lanes), teams).reshape(each, lanes)
    tables = [back] + [send(back, beside(step)) for step in (1, -1)]
    tables += [send(back, swap)] + [send(back, beside(step, True)) for step in (1, -1)]
    result = call(
        fetch_kernel, jax.ShapeDtypeStruct((1, rows), f32), "fetch", spot, *tables, owner, within
    )
    return result.reshape(rows)


def solution(mesh):
    placed = (P(("ingest", "span"), None), P(("ingest", "span"), None), P(("ingest", "span")))
    return jax.shard_map(
        shards, mesh=mesh, in_specs=placed, out_specs=P(("ingest", "span")), check_vma=False
    )
```

time: 148 us -> 128 us (0.86)
  blocking collectives: 42.4 us -> 89.4 us
  waiting for transfers between devices: 42.3 us -> 6.86 us
  starting transfers between devices: 42.3 us -> 17.1 us
  local copies, waits for them, and re-layouts: 6.2 us -> 2.59 us
  other arithmetic: 1.59 us -> 0.07 us
    all_to_all x2 -> x3, blocking collectives: 42.4 us -> 89.4 us  [trade(): lax.all_to_all(values, everyone, split_axis=0, concat_axis=0, axis_index_...]
    ppermute x19 -> x12, waiting for transfers between devices: 36.4 us -> 6.86 us  [send(): return lax.ppermute(values, everyone, route)]
    ppermute x19 -> x12, starting transfers between devices: 33.7 us -> 17.1 us  [send(): return lax.ppermute(values, everyone, route)]
    all_to_all x2 -> x0, starting transfers between devices: 8.59 us -> none  [trade(): lax.all_to_all(values, everyone, split_axis=0, concat_axis=0, axis_index_...]
    all_to_all x2 -> x0, waiting for transfers between devices: 5.87 us -> none  [trade(): lax.all_to_all(values, everyone, split_axis=0, concat_axis=0, axis_index_...]
    unnamed x12 -> x8, local copies, waits for them, and re-layouts: 5.47 us -> 2.59 us
  transfers between devices with their start and end apart: 21 -> 12, of which waited for: 11 -> 4; matrix products, arithmetic and copies ran while one was open for 3% -> 0% of each run, Pallas kernels for 2% -> 2%
where the time goes in v3:
time: 128 us
  blocking collectives  89.4 us (70%)
  starting transfers between devices  17.1 us (13%)
  Pallas kernels  11.7 us (9%)
  waiting for transfers between devices  6.86 us (5%)
  local copies, waits for them, and re-layouts  2.59 us (2%)
    all_to_all x3, blocking collectives, trade(): lax.all_to_all(values, everyone, split_axis=0, concat_axis=0, axis_index_...  89.4 us
    ppermute x12, starting transfers between devices, send(): return lax.ppermute(values, everyone, route)  17.1 us
    pallas_call x5, Pallas kernels, call(): pl.pallas_call(kernel, out_shape=out_shape, in_specs=[smem if a is spot e...  11.7 us
    ppermute x12, waiting for transfers between devices, send(): return lax.ppermute(values, everyone, route)  6.86 us
    unnamed x8, local copies, waits for them, and re-layouts  2.59 us
  transfers between devices with their start and end apart: 12, of which 4 were waited for; matrix products, arithmetic and copies ran while one was open for 0% of the time, Pallas kernels for 2%

profile of v3, /device:TPU:1, one launch (start us, length us, event | category | flops | bytes accessed | tf_op | source)
XLA Modules:
  0.0 127.7 jit_solution(6378388620938628049)
XLA Ops:
  0.0 3.2 %collective-permute-start = (bf16[512,1024]{1,0:T(8,128)(2,1)}, bf16[512,1024]{1,0:T(8,128)(2,1)S(1)}, u32[]{:S(2)}, u32[]{:S(2)}) collective-permute-start(bf16[512,1024]{1,0:T(8,128)(2,1)} %refs_0_.1), channel_id=1, source_target_pairs={{0,4},{1,5},{2,6},{3,7},{4,0},{5,1},{6,2},{7,3},{8,12},{9,13},{10,... | collective-permute-start | bytes 3145736 | tf_op jit(solution)/shard_map/ppermute | solution.py:277
  3.2 0.5 collective-permute-start.2
  3.8 0.1 pad_add_fusion.spot_ref
  3.8 1.9 %collective-permute-done.1.refs_3_ = s32[1,512]{1,0:T(1,128)S(1)} collective-permute-done((s32[1,512]{1,0:T(1,128)}, s32[1,512]{1,0:T(1,128)S(1)}, u32[]{:S(2)}, u32[]{:S(2)}) %collective-permute-start.1) | collective-permute-done | bytes 2080 | tf_op jit(solution)/shard_map/ppermute | solution.py:277
  5.7 0.0 collective-permute-done.2.refs_5_
  5.8 1.2 copy-done
  7.0 0.7 copy-done.1
  7.7 0.7 copy-done.3
  8.3 3.3 %place.1 = (bf16[1024,1024]{1,0:T(8,128)(2,1)S(1)}, f32[32,128]{1,0:T(8,128)S(1)}, s32[1,512]{1,0:T(1,128)S(1)}) custom-call(s32[2]{0:T(128)S(1)} %pad_add_fusion.spot_ref, bf16[512,1024]{1,0:T(8,128)(2,1)S(1)} %copy-done, bf16[512,1024]{1,0:T(8,128)(2,1)S(1)} %collective-permute-done.refs_1_, s32[1,512]{1,0:T(1,128)S(1)} %bitcast.30, ...), custom_call_target="tpu_custom_call" | custom-call | tf_op jit(solution)/shard_map/place/pallas_call | solution.py:300
  11.6 56.7 %all_to_all.15 = bf16[32,32,1024]{2,1,0:T(8,128)(2,1)S(1)} all-to-all(bf16[32,32,1024]{2,1,0:T(8,128)(2,1)S(1)} %bitcast.19), channel_id=1, replica_groups={{0,8,16,24,32,40,48,56,64,72,80,88,96,104,112,120,128,136,144,152,160,1..., dimensions={0} | all-to-all | bytes 4194304 | tf_op jit(solution)/shard_map/all_to_all | solution.py:281
  68.3 1.2 collective-permute-start.4
  69.6 1.7 %collective-permute-start.3 = (bf16[1024,1024]{1,0:T(8,128)(2,1)S(1)}, bf16[1024,1024]{1,0:T(8,128)(2,1)S(1)}, u32[]{:S(2)}, u32[]{:S(2)}) collective-permute-start(bf16[1024,1024]{1,0:T(8,128)(2,1)S(1)} %bitcast.16), channel_id=1, source_target_pairs={{0,3},{1,0},{2,1},{3,2},{4,196},{5,197},{6,198},{7,199},{8,11},{9,... | collective-permute-start | bytes 6291464 | tf_op jit(solution)/shard_map/ppermute | solution.py:277
  71.3 16.4 %all_to_all.16 = f32[32,1,1,128]{3,2,1,0:T(1,128)S(1)} all-to-all(f32[32,1,1,128]{3,2,1,0:T(1,128)S(1)} %bitcast.28), channel_id=1, replica_groups={{0,8,16,24,32,40,48,56,64,72,80,88,96,104,112,120,128,136,144,152,160,1..., dimensions={0} | all-to-all | bytes 32768 | tf_op jit(solution)/shard_map/all_to_all | solution.py:281
  87.6 0.1 spread.1.refs_1_.refs_3_
  87.7 0.0 collective-permute-start.6
  87.7 2.7 %collective-permute-start.5 = (f32[8,128]{1,0:T(8,128)S(1)}, f32[8,128]{1,0:T(8,128)S(1)}, u32[]{:S(2)}, u32[]{:S(2)}) collective-permute-start(f32[8,128]{1,0:T(8,128)S(1)} %spread.1.refs_1_.refs_3_), channel_id=1, source_target_pairs={{0,3},{1,0},{2,1},{3,2},{4,196},{5,197},{6,198},{7,199},{8,11},{9,... | collective-permute-start | bytes 12296 | tf_op jit(solution)/shard_map/ppermute | solution.py:277
  90.4 2.5 %own.1.refs_6_ = f32[8,128]{1,0:T(8,128)S(1)} custom-call(bf16[1024,1024]{1,0:T(8,128)(2,1)S(1)} %bitcast.17, f32[8,128]{1,0:T(8,128)S(1)} %spread.1.refs_1_.refs_3_), custom_call_target="tpu_custom_call" | custom-call | tf_op jit(solution)/shard_map/own/pallas_call | solution.py:300
  92.9 0.0 copy-start.2
  92.9 2.2 %collective-permute-done.6.refs_5_ = f32[8,128]{1,0:T(8,128)S(1)} collective-permute-done((f32[8,128]{1,0:T(8,128)S(1)}, f32[8,128]{1,0:T(8,128)S(1)}, u32[]{:S(2)}, u32[]{:S(2)}) %collective-permute-start.6) | collective-permute-done | bytes 4128 | tf_op jit(solution)/shard_map/ppermute | solution.py:277
  95.1 0.0 collective-permute-done.5.refs_4_
  95.1 0.0 collective-permute-done.4.refs_2_
  95.1 0.0 collective-permute-done.3.refs_1_
  95.1 4.3 %cross.1 = f32[32,128]{1,0:T(8,128)S(1)} custom-call(s32[2]{0:T(128)S(1)} %pad_add_fusion.spot_ref, bf16[1024,1024]{1,0:T(8,128)(2,1)S(1)} %bitcast.18, bf16[1024,1024]{1,0:T(8,128)(2,1)S(1)} %collective-permute-done.3.refs_1_, bf16[1024,1024]{1,0:T(8,128)(2,1)S(1)} %collective-permute-done.4.refs_2_, f32[8,128]{1,0:T(8,128)S(1)} %spread.1.refs_1_.refs_3_, ...), custom_call_target="tpu_custom_call" | custom-call | tf_op jit(solution)/shard_map/cross/pallas_call | solution.py:300
  99.5 16.3 %all_to_all.17 = f32[32,1,1,128]{3,2,1,0:T(1,128)S(1)} all-to-all(f32[32,1,1,128]{3,2,1,0:T(1,128)S(1)} %bitcast.20), channel_id=1, replica_groups={{0,8,16,24,32,40,48,56,64,72,80,88,96,104,112,120,128,136,144,152,160,1..., dimensions={0} | all-to-all | bytes 32768 | tf_op jit(solution)/shard_map/all_to_all | solution.py:281
  115.8 4.7 %collective-permute-start.11 = (f32[32,128]{1,0:T(8,128)S(1)}, f32[32,128]{1,0:T(8,128)S(1)}, u32[]{:S(2)}, u32[]{:S(2)}) collective-permute-start(f32[32,128]{1,0:T(8,128)S(1)} %bitcast.21), channel_id=1, source_target_pairs={{0,7},{1,4},{2,5},{3,6},{4,192},{5,193},{6,194},{7,195},{8,15},{9,... | collective-permute-start | bytes 49160 | tf_op jit(solution)/shard_map/ppermute | solution.py:277
  120.5 0.0 collective-permute-start.10
  120.5 1.6 %collective-permute-start.9 = (f32[32,128]{1,0:T(8,128)S(1)}, f32[32,128]{1,0:T(8,128)S(1)}, u32[]{:S(2)}, u32[]{:S(2)}) collective-permute-start(f32[32,128]{1,0:T(8,128)S(1)} %bitcast.23), channel_id=1, source_target_pairs={{0,4},{1,5},{2,6},{3,7},{4,0},{5,1},{6,2},{7,3},{8,12},{9,13},{10,... | collective-permute-start | bytes 49160 | tf_op jit(solution)/shard_map/ppermute | solution.py:277
  122.1 0.4 collective-permute-start.8
  122.4 1.1 collective-permute-start.7
  123.5 1.3 %collective-permute-done.10.refs_4_ = f32[32,128]{1,0:T(8,128)S(1)} collective-permute-done((f32[32,128]{1,0:T(8,128)S(1)}, f32[32,128]{1,0:T(8,128)S(1)}, u32[]{:S(2)}, u32[]{:S(2)}) %collective-permute-start.10) | collective-permute-done | bytes 16416 | tf_op jit(solution)/shard_map/ppermute | solution.py:277
  124.8 1.4 %collective-permute-done.7.refs_1_ = f32[32,128]{1,0:T(8,128)S(1)} collective-permute-done((f32[32,128]{1,0:T(8,128)S(1)}, f32[32,128]{1,0:T(8,128)S(1)}, u32[]{:S(2)}, u32[]{:S(2)}) %collective-permute-start.7) | collective-permute-done | bytes 16416 | tf_op jit(solution)/shard_map/ppermute | solution.py:277
  126.2 1.5 %fetch.1 = f32[1,512]{1,0:T(1,128)} custom-call(s32[2]{0:T(128)S(1)} %pad_add_fusion.spot_ref, f32[32,128]{1,0:T(8,128)S(1)} %bitcast.26, f32[32,128]{1,0:T(8,128)S(1)} %collective-permute-done.7.refs_1_, f32[32,128]{1,0:T(8,128)S(1)} %collective-permute-done.8.refs_2_, f32[32,128]{1,0:T(8,128)S(1)} %collective-permute-done.9.refs_3_, ...), custom_call_target="tpu_custom_call" | custom-call | tf_op jit(solution)/shard_map/fetch/pallas_call | solution.py:300
  (9 shorter events, 0.0 us)
Async XLA Ops:
  0.0 5.7 %collective-permute-start = (bf16[512,1024]{1,0:T(8,128)(2,1)}, bf16[512,1024]{1,0:T(8,128)(2,1)S(1)}, u32[]{:S(2)}, u32[]{:S(2)}) collective-permute-start(bf16[512,1024]{1,0:T(8,128)(2,1)} %refs_0_.1), channel_id=1, source_target_pairs={{0,4},{1,5},{2,6},{3,7},{4,0},{5,1},{6,2},{7,3},{8,12},{9,13},{10,... | collective-permute-start | bytes 3145736 | tf_op jit(solution)/shard_map/ppermute | solution.py:277
  3.2 2.5 %collective-permute-start.1 = (s32[1,512]{1,0:T(1,128)}, s32[1,512]{1,0:T(1,128)S(1)}, u32[]{:S(2)}, u32[]{:S(2)}) collective-permute-start(s32[1,512]{1,0:T(1,128)} %bitcast.29), channel_id=1, source_target_pairs={{0,4},{1,5},{2,6},{3,7},{4,0},{5,1},{6,2},{7,3},{8,12},{9,13},{10,... | collective-permute-start | bytes 6152 | tf_op jit(solution)/shard_map/ppermute | solution.py:277
  3.2 2.5 %collective-permute-start.2 = (s32[1,512]{1,0:T(1,128)}, s32[1,512]{1,0:T(1,128)S(1)}, u32[]{:S(2)}, u32[]{:S(2)}) collective-permute-start(s32[1,512]{1,0:T(1,128)} %bitcast.32), channel_id=1, source_target_pairs={{0,4},{1,5},{2,6},{3,7},{4,0},{5,1},{6,2},{7,3},{8,12},{9,13},{10,... | collective-permute-start | bytes 6152 | tf_op jit(solution)/shard_map/ppermute | solution.py:277
  5.7 1.2 copy-start
  7.0 0.7 copy-start.1
  7.7 0.7 copy-start.3
  68.3 26.8 %collective-permute-start.4 = (bf16[1024,1024]{1,0:T(8,128)(2,1)S(1)}, bf16[1024,1024]{1,0:T(8,128)(2,1)S(1)}, u32[]{:S(2)}, u32[]{:S(2)}) collective-permute-start(bf16[1024,1024]{1,0:T(8,128)(2,1)S(1)} %bitcast.15), channel_id=1, source_target_pairs={{0,1},{1,2},{2,3},{3,0},{4,68},{5,69},{6,70},{7,71},{8,9},{9,10},{... | collective-permute-start | bytes 6291464 | tf_op jit(solution)/shard_map/ppermute | solution.py:277
  69.6 25.6 %collective-permute-start.3 = (bf16[1024,1024]{1,0:T(8,128)(2,1)S(1)}, bf16[1024,1024]{1,0:T(8,128)(2,1)S(1)}, u32[]{:S(2)}, u32[]{:S(2)}) collective-permute-start(bf16[1024,1024]{1,0:T(8,128)(2,1)S(1)} %bitcast.16), channel_id=1, source_target_pairs={{0,3},{1,0},{2,1},{3,2},{4,196},{5,197},{6,198},{7,199},{8,11},{9,... | collective-permute-start | bytes 6291464 | tf_op jit(solution)/shard_map/ppermute | solution.py:277
  87.7 7.4 %collective-permute-start.6 = (f32[8,128]{1,0:T(8,128)S(1)}, f32[8,128]{1,0:T(8,128)S(1)}, u32[]{:S(2)}, u32[]{:S(2)}) collective-permute-start(f32[8,128]{1,0:T(8,128)S(1)} %spread.1.refs_1_.refs_3_), channel_id=1, source_target_pairs={{0,1},{1,2},{2,3},{3,0},{4,68},{5,69},{6,70},{7,71},{8,9},{9,10},{... | collective-permute-start | bytes 12296 | tf_op jit(solution)/shard_map/ppermute | solution.py:277
  87.7 7.4 %collective-permute-start.5 = (f32[8,128]{1,0:T(8,128)S(1)}, f32[8,128]{1,0:T(8,128)S(1)}, u32[]{:S(2)}, u32[]{:S(2)}) collective-permute-start(f32[8,128]{1,0:T(8,128)S(1)} %spread.1.refs_1_.refs_3_), channel_id=1, source_target_pairs={{0,3},{1,0},{2,1},{3,2},{4,196},{5,197},{6,198},{7,199},{8,11},{9,... | collective-permute-start | bytes 12296 | tf_op jit(solution)/shard_map/ppermute | solution.py:277
  92.9 33.4 %copy-start.2 = (s32[512,1]{0,1:T(1,128)S(1)}, s32[512,1]{0,1:T(1,128)}, u32[]{:S(2)}) copy-start(s32[512,1]{0,1:T(1,128)} %param.4) | copy-start | bytes 6148
  115.8 7.8 %collective-permute-start.11 = (f32[32,128]{1,0:T(8,128)S(1)}, f32[32,128]{1,0:T(8,128)S(1)}, u32[]{:S(2)}, u32[]{:S(2)}) collective-permute-start(f32[32,128]{1,0:T(8,128)S(1)} %bitcast.21), channel_id=1, source_target_pairs={{0,7},{1,4},{2,5},{3,6},{4,192},{5,193},{6,194},{7,195},{8,15},{9,... | collective-permute-start | bytes 49160 | tf_op jit(solution)/shard_map/ppermute | solution.py:277
  120.5 4.4 %collective-permute-start.10 = (f32[32,128]{1,0:T(8,128)S(1)}, f32[32,128]{1,0:T(8,128)S(1)}, u32[]{:S(2)}, u32[]{:S(2)}) collective-permute-start(f32[32,128]{1,0:T(8,128)S(1)} %bitcast.22), channel_id=1, source_target_pairs={{0,5},{1,6},{2,7},{3,4},{4,64},{5,65},{6,66},{7,67},{8,13},{9,14},... | collective-permute-start | bytes 49160 | tf_op jit(solution)/shard_map/ppermute | solution.py:277
  120.5 4.4 %collective-permute-start.9 = (f32[32,128]{1,0:T(8,128)S(1)}, f32[32,128]{1,0:T(8,128)S(1)}, u32[]{:S(2)}, u32[]{:S(2)}) collective-permute-start(f32[32,128]{1,0:T(8,128)S(1)} %bitcast.23), channel_id=1, source_target_pairs={{0,4},{1,5},{2,6},{3,7},{4,0},{5,1},{6,2},{7,3},{8,12},{9,13},{10,... | collective-permute-start | bytes 49160 | tf_op jit(solution)/shard_map/ppermute | solution.py:277
  122.1 2.8 %collective-permute-start.8 = (f32[32,128]{1,0:T(8,128)S(1)}, f32[32,128]{1,0:T(8,128)S(1)}, u32[]{:S(2)}, u32[]{:S(2)}) collective-permute-start(f32[32,128]{1,0:T(8,128)S(1)} %bitcast.24), channel_id=1, source_target_pairs={{0,3},{1,0},{2,1},{3,2},{4,196},{5,197},{6,198},{7,199},{8,11},{9,... | collective-permute-start | bytes 49160 | tf_op jit(solution)/shard_map/ppermute | solution.py:277
  122.4 3.8 %collective-permute-start.7 = (f32[32,128]{1,0:T(8,128)S(1)}, f32[32,128]{1,0:T(8,128)S(1)}, u32[]{:S(2)}, u32[]{:S(2)}) collective-permute-start(f32[32,128]{1,0:T(8,128)S(1)} %bitcast.25), channel_id=1, source_target_pairs={{0,1},{1,2},{2,3},{3,0},{4,68},{5,69},{6,70},{7,71},{8,9},{9,10},{... | collective-permute-start | bytes 49160 | tf_op jit(solution)/shard_map/ppermute | solution.py:277

commit v4 on v3

v4 whole, which is shorter than its diff:
```python
import functools

import jax
import jax.numpy as jnp
from jax import lax
from jax.experimental import pallas as pl
from jax.experimental.pallas import tpu as pltpu
from jax.sharding import PartitionSpec as P

epsilon = 1e-06
capacity = 16
lanes = 128
wide = 256
cores = 2
places = 4
depth = 8
field = cores * capacity
tail = 128
note = 8
labels = 64
contract_last = (((1,), (1,)), ((), ()))
contract_first = (((1,), (0,)), ((), ()))
everyone = ("ingest", "span")


def params():
    return pltpu.CompilerParams(vmem_limit_bytes=40 * 1024 * 1024)


def device(y, z, core, x):
    return ((y * depth + z) * cores + core) * places + x


def pairs(move):
    found = []
    for y in range(places):
        for z in range(depth):
            for core in range(cores):
                for x in range(places):
                    found.append((device(y, z, core, x), device(*move(y, z, core, x))))
    return found


def other_core():
    return pairs(lambda y, z, core, x: (y, z, 1 - core, x))


def beside(step):
    return pairs(
        lambda y, z, core, x: (y, z, core, (x + step) % places)
        if core == 0
        else ((y + step) % places, z, core, x)
    )


def plane_teams():
    spots, levels = range(places), range(depth)
    return [[device(i, z, 0, x) for i in spots for z in levels] for x in spots] + [
        [device(y, z, 1, i) for i in spots for z in levels] for y in spots
    ]


def rank_rows(owner, groups):
    rows = owner.shape[1]
    belongs = lax.broadcasted_iota(jnp.int32, (groups, rows), 0) == owner
    onehot = belongs.astype(jnp.bfloat16)
    earlier = lax.broadcasted_iota(jnp.int32, (rows, rows), 0) < lax.broadcasted_iota(
        jnp.int32, (rows, rows), 1
    )
    before = lax.dot_general(
        onehot, earlier.astype(jnp.bfloat16), contract_first, preferred_element_type=jnp.float32
    )
    return jnp.sum(jnp.where(belongs, before, 0.0), axis=0, keepdims=True).astype(jnp.int32)


def put_rows(groups, side, spot_ref, emb_ref, name_ref):
    core = spot_ref[0]
    owner = name_ref[...] // labels
    rows = owner.shape[1]
    within = rank_rows(owner, groups)
    slot = jnp.where(owner % cores == core, owner // cores * capacity + within, -1)
    room = groups // cores * capacity
    put = (lax.broadcasted_iota(jnp.int32, (room, rows), 0) == slot).astype(jnp.bfloat16)
    values = emb_ref[...].astype(jnp.float32)
    squared = jnp.sum(values * values, axis=1, keepdims=True)
    unit = (values * lax.rsqrt(squared + epsilon)).astype(jnp.bfloat16)

    def placed(start, width):
        return lax.dot_general(
            put,
            unit[:, start : start + width],
            contract_first,
            preferred_element_type=jnp.float32,
        ).astype(jnp.bfloat16)

    team = lax.broadcasted_iota(jnp.int32, (groups // cores, rows), 0)
    here = (team == owner // cores) & (owner % cores == core)
    named = here.astype(jnp.bfloat16) * (name_ref[...] % labels + 1).astype(jnp.bfloat16)
    lane = lax.broadcasted_iota(jnp.int32, (lanes, rows), 0)
    into = (lane == within + side * capacity).astype(jnp.bfloat16)
    ids = lax.dot_general(named, into, contract_last, preferred_element_type=jnp.float32)
    return placed, ids, within


def place_kernel(groups, spot_ref, emb_ref, name_ref, main_ref, tail_ref, ids_ref, within_ref):
    placed, ids, within = put_rows(groups, 0, spot_ref, emb_ref, name_ref)
    width = main_ref.shape[1]
    for start in range(0, width, wide):
        size = min(wide, width - start)
        main_ref[:, start : start + size] = placed(start, size)
    tail_ref[...] = placed(width, tail)
    ids_ref[...] = ids
    within_ref[...] = within


def pair_kernel(
    groups, spot_ref, emb_ref, name_ref, first_ref, last_ref, ids_ref, main_ref, tail_ref
):
    placed, ids, _ = put_rows(groups, 1, spot_ref, emb_ref, name_ref)
    teams, _, width = main_ref.shape
    main_ref[:, :capacity, :] = first_ref[...].reshape(teams, capacity, width)
    tail_ref[:, :capacity, :] = last_ref[...].reshape(teams, capacity, tail)
    for start in range(0, width, wide):
        size = min(wide, width - start)
        main_ref[:, capacity:field, start : start + size] = placed(start, size).reshape(
            teams, capacity, size
        )
    tail_ref[:, capacity:field, :] = placed(width, tail).reshape(teams, capacity, tail)
    ids = (ids + ids_ref[...] - 1.0).astype(jnp.bfloat16)
    tail_ref[:, field:, :] = jnp.broadcast_to(ids[:, None, :], (teams, note, lanes))


def read_ids(ref, hold):
    count = lanes // field
    blocks = ref.shape[0] // count
    hold[...] = jnp.max(ref[:, field:, :].astype(jnp.float32), axis=1)
    lane = lax.broadcasted_iota(jnp.int32, (blocks, lanes), 1)
    total = hold[pl.ds(0, blocks, stride=count), :]
    for q in range(1, count):
        piece = pltpu.roll(hold[pl.ds(q, blocks, stride=count), :], field * q, 1)
        total = jnp.where(lane // field == q, piece, total)
    return total


def features(main, last, start, count):
    rest = last[start // field : (start + count) // field, :field, :].reshape(count, tail)
    return jnp.concatenate([main[start : start + count, :], rest], axis=1)


def to_column(row):
    return jnp.transpose(jnp.broadcast_to(row, (lanes, lanes)))


def columns_of(ids):
    return jnp.concatenate([to_column(ids[b : b + 1, :]) for b in range(ids.shape[0])], axis=0)


def to_rows(tile):
    return jnp.concatenate(
        [
            jnp.max(jnp.transpose(tile[b * lanes : (b + 1) * lanes, :]), axis=0, keepdims=True)
            for b in range(tile.shape[0] // lanes)
        ],
        axis=0,
    )


def scan_block(left, right, left_ids, right_ids, best, skip):
    total = lax.dot_general(left, right, contract_last, preferred_element_type=jnp.float32)
    tops = []
    for half in range(wide // lanes):
        scores = total[:, half * lanes : (half + 1) * lanes]
        ids = right_ids[half : half + 1, :]
        same = left_ids == jnp.where(ids < 0, -2.0, ids)
        if skip is not None:
            row = lax.broadcasted_iota(jnp.int32, scores.shape, 0)
            column = lax.broadcasted_iota(jnp.int32, scores.shape, 1)
            same = same & (row - column != skip + half * lanes)
        masked = jnp.where(same, scores, -1.0)
        best = masked if best is None else jnp.maximum(best, masked)
        tops.append(jnp.max(masked, axis=0, keepdims=True))
    return best, tops


def own_kernel(main, last, out_ref, ids_ref, hold):
    ids = read_ids(last, hold)
    ids_ref[...] = ids
    rows = main.shape[0]
    columns = columns_of(ids)
    left = features(main, last, 0, rows)
    best = None
    per = wide // lanes
    for at in range(rows // wide):
        best, _ = scan_block(
            left,
            features(main, last, at * wide, wide),
            columns,
            ids[at * per : (at + 1) * per, :],
            best,
            at * wide,
        )
    out_ref[...] = to_rows(best)


def cross_kernel(
    spot_ref,
    main,
    last,
    after,
    after_last,
    before,
    before_last,
    inside_ref,
    ids_ref,
    out_ref,
    hold,
    table,
):
    low = spot_ref[1] == 1
    ids, after_ids, before_ids = (
        ids_ref[...],
        read_ids(after_last, hold.at[0]),
        read_ids(before_last, hold.at[1]),
    )
    blocks = ids.shape[0]
    rows = blocks * lanes
    half = rows // 2
    columns = columns_of(ids)
    right_ids = jnp.where(low, after_ids, before_ids)
    left_ids = jnp.where(low, before_ids[: blocks // 2, :], after_ids[blocks // 2 :, :])
    left_columns = columns_of(left_ids)
    side_left = jnp.where(
        low,
        features(before, before_last, 0, half),
        features(after, after_last, half, half),
    )
    left = features(main, last, 0, rows)
    per = wide // lanes
    best, far, up, side = None, None, [], []
    for at in range(rows // wide):
        near = features(after, after_last, at * wide, wide)
        right = jnp.where(low, near, features(before, before_last, at * wide, wide))
        cut = slice(at * per, (at + 1) * per)
        best, tops = scan_block(left, near, columns, after_ids[cut, :], best, None)
        up += tops
        far, tops = scan_block(side_left, right, left_columns, right_ids[cut, :], far, None)
        side += tops
    up, side = jnp.concatenate(up, axis=0), jnp.concatenate(side, axis=0)
    mine = jnp.maximum(to_rows(best), inside_ref[...])
    found = to_rows(far)
    blank = jnp.full(found.shape, -1.0, jnp.float32)
    placed = jnp.where(
        low, jnp.concatenate([found, blank], axis=0), jnp.concatenate([blank, found], axis=0)
    )
    up = jnp.maximum(up, jnp.where(low, side, placed))
    down = jnp.where(low, placed, side)
    count = lanes // field
    steps = (0, 1, places - 1)
    for step, values in enumerate((mine, up, down)):
        for q in range(count):
            turned = values if q == 0 else pltpu.roll(values, lanes - field * q, 1)
            table[step, pl.ds(q, blocks, stride=count), :] = turned
    core, x, y = spot_ref[0], spot_ref[2], spot_ref[3]
    each = places * depth
    across = cores * places

    def found(step, other):
        values = table[step]
        return jnp.where(other == core, values, pltpu.roll(values, lanes - capacity, 1))

    @pl.when(core == 0)
    def _():
        for step, move in enumerate(steps):
            for other in range(cores):
                start = other * places + lax.rem(x + move, places)
                out_ref[pl.ds(start, each, stride=across), :] = found(step, other)

    @pl.when(core == 1)
    def _():
        for step, move in enumerate(steps):
            row = lax.rem(y + move, places) * (depth * across)
            for other in range(cores):
                values = found(step, other)
                for place in range(places):
                    start = row + other * places + place
                    out_ref[pl.ds(start, depth, stride=across), :] = values[
                        place * depth : (place + 1) * depth, :
                    ]


def fetch_kernel(spot_ref, back_ref, name_ref, within_ref, out_ref):
    x, y = spot_ref[2], spot_ref[3]
    each = places * depth
    across = cores * places
    even, odd = None, []
    for move in (0, 1, places - 1):
        rows = back_ref[pl.ds(lax.rem(x + move, places), each, stride=across), :]
        even = rows if even is None else jnp.maximum(even, rows)
    for place in range(places):
        total = None
        for move in (0, 1, places - 1):
            start = lax.rem(y + move, places) * (depth * across) + places + place
            rows = back_ref[pl.ds(start, depth, stride=across), :]
            total = rows if total is None else jnp.maximum(total, rows)
        odd.append(total)
    odd = pltpu.roll(jnp.concatenate(odd, axis=0), capacity, 1)
    rest = jnp.where(lax.broadcasted_iota(jnp.int32, even.shape, 1) < capacity, even, odd)
    rest = jnp.where(lax.broadcasted_iota(jnp.int32, even.shape, 1) < field, rest, 0.0)
    owner = name_ref[...] // labels
    rows = owner.shape[1]
    team = lax.broadcasted_iota(jnp.int32, (places * depth, rows), 0)
    onehot = (team == owner // cores).astype(jnp.bfloat16)
    found = jnp.zeros((lanes, rows), jnp.float32)
    for _ in range(3):
        piece = rest.astype(jnp.bfloat16)
        rest = rest - piece.astype(jnp.float32)
        found = found + lax.dot_general(
            piece, onehot, (((0,), (0,)), ((), ())), preferred_element_type=jnp.float32
        )
    lane = lax.broadcasted_iota(jnp.int32, (lanes, rows), 0)
    within = within_ref[...] + owner % cores * capacity
    out_ref[...] = jnp.sum(jnp.where(lane == within, found, 0.0), axis=0, keepdims=True)


def send(values, route):
    return lax.ppermute(values, everyone, route)


def trade(values, teams):
    return lax.all_to_all(
        values, everyone, split_axis=0, concat_axis=0, axis_index_groups=teams, tiled=True
    )


def shards(embeddings, owner, cluster):
    rows, width = embeddings.shape
    groups = lax.axis_size("ingest")
    spots = groups * capacity
    blocks = spots // lanes
    each = places * depth
    f32 = jnp.float32
    at, x = lax.axis_index("ingest"), lax.axis_index("span")
    core, y = at % cores, at // (cores * depth)
    low = jnp.where(core == 0, x, y) < places // 2
    spot = jnp.stack([core, low.astype(jnp.int32), x, y]).astype(jnp.int32)
    smem, vmem = pl.BlockSpec(memory_space=pltpu.SMEM), pl.BlockSpec(memory_space=pltpu.VMEM)

    def call(kernel, out_shape, name, *args, scratch=()):
        return pl.pallas_call(
            kernel,
            out_shape=out_shape,
            in_specs=[smem if a is spot else vmem for a in args],
            scratch_shapes=scratch,
            compiler_params=params(),
            name=name,
        )(*args)

    def array(*shape, dtype=jnp.bfloat16):
        return jax.ShapeDtypeStruct(shape, dtype)

    swap = other_core()
    names = owner.reshape(1, rows) * labels + cluster.reshape(1, rows)
    other_rows = send(embeddings, swap)
    other_names = send(names, swap)
    first, last, ids, within = call(
        functools.partial(place_kernel, groups),
        [
            array(spots // cores, width - tail),
            array(spots // cores, tail),
            array(each, lanes, dtype=f32),
            array(1, rows, dtype=jnp.int32),
        ],
        "place",
        spot,
        embeddings,
        names,
    )
    parts = call(
        functools.partial(pair_kernel, groups),
        [array(each, field, width - tail), array(each, field + note, tail)],
        "pair",
        spot,
        other_rows,
        other_names,
        first,
        last,
        ids,
    )
    teams = plane_teams()
    own, after, before = [], [], []
    for part in parts:
        got = trade(part, teams)
        if not own:
            got = got.reshape(spots, width - tail)
        own.append(got)
        before.append(send(got, beside(1)))
        after.append(send(got, beside(-1)))
    inside, ids = call(
        own_kernel,
        [array(blocks, lanes, dtype=f32)] * 2,
        "own",
        *own,
        scratch=[pltpu.VMEM((each, lanes), f32)],
    )
    count = groups * places
    best = call(
        cross_kernel,
        array(count, lanes, dtype=f32),
        "cross",
        spot,
        *own,
        *after,
        *before,
        inside,
        ids,
        scratch=[pltpu.VMEM((2, each, lanes), f32), pltpu.VMEM((3, each, lanes), f32)],
    )
    back = lax.all_to_all(
        best.reshape(count, 1, 1, lanes), everyone, split_axis=0, concat_axis=0, tiled=True
    ).reshape(count, lanes)
    result = call(fetch_kernel, array(1, rows, dtype=f32), "fetch", spot, back, names, within)
    return result.reshape(rows)


def solution(mesh):
    placed = (P(("ingest", "span"), None), P(("ingest", "span"), None), P(("ingest", "span")))
    return jax.shard_map(
        shards, mesh=mesh, in_specs=placed, out_specs=P(("ingest", "span")), check_vma=False
    )
```

time: 128 us -> 122 us (0.953)
  starting transfers between devices: 17.1 us -> 8.78 us
  blocking collectives: 89.4 us -> 95.5 us
  waiting for transfers between devices: 6.86 us -> 2.56 us
  other arithmetic: 0.07 us -> 1.44 us
  local copies, waits for them, and re-layouts: 2.59 us -> 1.23 us
    all_to_all x0 -> x1, blocking collectives: none -> 26.4 us  [shards(): lax.all_to_all(best.reshape(count, 1, 1, lanes), everyone, split_axis=0,...]
    all_to_all x3 -> x2, blocking collectives: 89.4 us -> 69 us  [trade(): lax.all_to_all(values, everyone, split_axis=0, concat_axis=0, axis_index_...]
    ppermute x12 -> x6, starting transfers between devices: 17.1 us -> 8.78 us  [send(): return lax.ppermute(values, everyone, route)]
    ppermute x12 -> x6, waiting for transfers between devices: 6.86 us -> 2.56 us  [send(): return lax.ppermute(values, everyone, route)]
    unnamed x8 -> x2, local copies, waits for them, and re-layouts: 2.59 us -> 1.23 us
  transfers between devices with their start and end apart: 12 -> 6, of which waited for: 4 -> 1; matrix products, arithmetic and copies ran while one was open for 0% -> 1% of each run, Pallas kernels for 2% -> 3%
where the time goes in v4:
time: 122 us; the launch traced here: 121 us
  blocking collectives  95.5 us (78%)
  Pallas kernels  11.9 us (10%)
  starting transfers between devices  8.78 us (7%)
  waiting for transfers between devices  2.56 us (2%)
  other arithmetic  1.44 us (1%)
  local copies, waits for them, and re-layouts  1.23 us (1%)
    all_to_all x2, blocking collectives, trade(): lax.all_to_all(values, everyone, split_axis=0, concat_axis=0, axis_index_...  69 us
    all_to_all x1, blocking collectives, shards(): lax.all_to_all(best.reshape(count, 1, 1, lanes), everyone, split_axis=0,...  26.4 us
    pallas_call x5, Pallas kernels, call(): pl.pallas_call(kernel, out_shape=out_shape, in_specs=[smem if a is spot e...  11.9 us
    ppermute x6, starting transfers between devices, send(): return lax.ppermute(values, everyone, route)  8.78 us
    ppermute x6, waiting for transfers between devices, send(): return lax.ppermute(values, everyone, route)  2.56 us
  transfers between devices with their start and end apart: 6, of which 1 were waited for; matrix products, arithmetic and copies ran while one was open for 1% of the time, Pallas kernels for 3%

profile of v4, /device:TPU:1, one launch (start us, length us, event | category | flops | bytes accessed | tf_op | source)
XLA Modules:
  0.0 121.4 jit_solution(354443428234372684)
XLA Ops:
  0.0 3.2 %collective-permute-start = (bf16[512,1024]{1,0:T(8,128)(2,1)}, bf16[512,1024]{1,0:T(8,128)(2,1)S(1)}, u32[]{:S(2)}, u32[]{:S(2)}) collective-permute-start(bf16[512,1024]{1,0:T(8,128)(2,1)} %emb_ref.1), channel_id=1, source_target_pairs={{0,4},{1,5},{2,6},{3,7},{4,0},{5,1},{6,2},{7,3},{8,12},{9,13},{10,... | collective-permute-start | bytes 3145736 | tf_op jit(solution)/shard_map/ppermute | solution.py:326
  3.2 0.7 broadcast_multiply_fusion
  3.9 0.7 add.11
  4.6 0.0 collective-permute-start.1
  4.6 0.1 pad_add_fusion.spot_ref
  4.7 0.0 copy-start
  4.7 1.2 %copy-done = bf16[512,1024]{1,0:T(8,128)(2,1)S(1)} copy-done((bf16[512,1024]{1,0:T(8,128)(2,1)S(1)}, bf16[512,1024]{1,0:T(8,128)(2,1)}, u32[]{:S(2)}) %copy-start) | copy-done | bytes 1048600
  5.9 1.7 %place.1 = (bf16[512,896]{1,0:T(8,128)(2,1)S(1)}, bf16[512,128]{1,0:T(8,128)(2,1)S(1)}, f32[32,128]{1,0:T(8,128)S(1)}, s32[1,512]{1,0:T(1,128)S(1)}) custom-call(s32[4]{0:T(128)S(1)} %pad_add_fusion.spot_ref, bf16[512,1024]{1,0:T(8,128)(2,1)S(1)} %copy-done, s32[1,512]{1,0:T(1,128)S(1)} %bitcast.19), custom_call_target="tpu_custom_call" | custom-call | tf_op jit(solution)/shard_map/place/pallas_call | solution.py:349
  7.6 0.0 collective-permute-done.1.name_ref
  7.6 0.0 collective-permute-done.emb_ref
  7.7 1.8 %pair.1 = (bf16[32,32,896]{2,1,0:T(8,128)(2,1)S(1)}, bf16[32,40,128]{2,1,0:T(8,128)(2,1)S(1)}) custom-call(s32[4]{0:T(128)S(1)} %pad_add_fusion.spot_ref, bf16[512,1024]{1,0:T(8,128)(2,1)S(1)} %collective-permute-done.emb_ref, s32[1,512]{1,0:T(1,128)S(1)} %collective-permute-done.1.name_ref, bf16[512,896]{1,0:T(8,128)(2,1)S(1)} %get-tuple-element.13.first_ref, ...), custom_call_target="tpu_custom_call" | custom-call | tf_op jit(solution)/shard_map/pair/pallas_call | solution.py:349
  9.4 50.3 %all_to_all.15 = bf16[32,32,896]{2,1,0:T(8,128)(2,1)S(1)} all-to-all(bf16[32,32,896]{2,1,0:T(8,128)(2,1)S(1)} %get-tuple-element.16), channel_id=1, replica_groups={{0,8,16,24,32,40,48,56,64,72,80,88,96,104,112,120,128,136,144,152,160,1..., dimensions={0} | all-to-all | bytes 3670016 | tf_op jit(solution)/shard_map/all_to_all | solution.py:330
  59.8 1.3 %collective-permute-start.4 = (bf16[1024,896]{1,0:T(8,128)(2,1)S(1)}, bf16[1024,896]{1,0:T(8,128)(2,1)S(1)}, u32[]{:S(2)}, u32[]{:S(2)}) collective-permute-start(bf16[1024,896]{1,0:T(8,128)(2,1)S(1)} %bitcast.12), channel_id=1, source_target_pairs={{0,1},{1,2},{2,3},{3,0},{4,68},{5,69},{6,70},{7,71},{8,9},{9,10},{... | collective-permute-start | bytes 5505032 | tf_op jit(solution)/shard_map/ppermute | solution.py:326
  61.1 1.5 %collective-permute-start.2 = (bf16[1024,896]{1,0:T(8,128)(2,1)S(1)}, bf16[1024,896]{1,0:T(8,128)(2,1)S(1)}, u32[]{:S(2)}, u32[]{:S(2)}) collective-permute-start(bf16[1024,896]{1,0:T(8,128)(2,1)S(1)} %bitcast.13), channel_id=1, source_target_pairs={{0,3},{1,0},{2,1},{3,2},{4,196},{5,197},{6,198},{7,199},{8,11},{9,... | collective-permute-start | bytes 5505032 | tf_op jit(solution)/shard_map/ppermute | solution.py:326
  62.6 18.7 %all_to_all.16.last = bf16[32,40,128]{2,1,0:T(8,128)(2,1)S(1)} all-to-all(bf16[32,40,128]{2,1,0:T(8,128)(2,1)S(1)} %get-tuple-element.17), channel_id=1, replica_groups={{0,8,16,24,32,40,48,56,64,72,80,88,96,104,112,120,128,136,144,152,160,1..., dimensions={0} | all-to-all | bytes 655360 | tf_op jit(solution)/shard_map/all_to_all | solution.py:330
  81.3 0.0 collective-permute-start.5
  81.3 2.7 %collective-permute-start.3 = (bf16[32,40,128]{2,1,0:T(8,128)(2,1)S(1)}, bf16[32,40,128]{2,1,0:T(8,128)(2,1)S(1)}, u32[]{:S(2)}, u32[]{:S(2)}) collective-permute-start(bf16[32,40,128]{2,1,0:T(8,128)(2,1)S(1)} %all_to_all.16.last), channel_id=1, source_target_pairs={{0,3},{1,0},{2,1},{3,2},{4,196},{5,197},{6,198},{7,199},{8,11},{9,... | collective-permute-start | bytes 983048 | tf_op jit(solution)/shard_map/ppermute | solution.py:326
  84.0 2.5 %own.1 = (f32[8,128]{1,0:T(8,128)S(1)}, f32[8,128]{1,0:T(8,128)S(1)}) custom-call(bf16[1024,896]{1,0:T(8,128)(2,1)S(1)} %bitcast.14, bf16[32,40,128]{2,1,0:T(8,128)(2,1)S(1)} %all_to_all.16.last), custom_call_target="tpu_custom_call" | custom-call | tf_op jit(solution)/shard_map/own/pallas_call | solution.py:349
  86.5 2.5 %collective-permute-done.5.before_last = bf16[32,40,128]{2,1,0:T(8,128)(2,1)S(1)} collective-permute-done((bf16[32,40,128]{2,1,0:T(8,128)(2,1)S(1)}, bf16[32,40,128]{2,1,0:T(8,128)(2,1)S(1)}, u32[]{:S(2)}, u32[]{:S(2)}) %collective-permute-start.5) | collective-permute-done | bytes 327712 | tf_op jit(solution)/shard_map/ppermute | solution.py:326
  89.0 0.0 collective-permute-done.3.after_last
  89.0 0.0 collective-permute-done.4.before
  89.0 0.0 collective-permute-done.2.after
  89.0 4.5 %cross.1 = f32[256,128]{1,0:T(8,128)S(1)} custom-call(s32[4]{0:T(128)S(1)} %pad_add_fusion.spot_ref, bf16[1024,896]{1,0:T(8,128)(2,1)S(1)} %bitcast.15, bf16[32,40,128]{2,1,0:T(8,128)(2,1)S(1)} %all_to_all.16.last, bf16[1024,896]{1,0:T(8,128)(2,1)S(1)} %collective-permute-done.2.after, bf16[32,40,128]{2,1,0:T(8,128)(2,1)S(1)} %collective-permute-done.3.after_last, ...), custom_call_target="tpu_custom_call" | custom-call | tf_op jit(solution)/shard_map/cross/pallas_call | solution.py:349
  93.5 26.4 %all_to_all.17 = f32[256,1,1,128]{3,2,1,0:T(1,128)S(1)} all-to-all(f32[256,1,1,128]{3,2,1,0:T(1,128)S(1)} %bitcast.17), channel_id=1, replica_groups=mesh['ingest'=64,'span'=4] {'ingest','span'}, dimensions={0} | all-to-all | bytes 262144 | tf_op jit(solution)/shard_map/all_to_all | solution.py:418
  119.9 1.5 %fetch.1 = f32[1,512]{1,0:T(1,128)} custom-call(s32[4]{0:T(128)S(1)} %pad_add_fusion.spot_ref, f32[256,128]{1,0:T(8,128)S(1)} %bitcast.16, s32[1,512]{1,0:T(1,128)S(1)} %bitcast.20, s32[1,512]{1,0:T(1,128)S(1)} %get-tuple-element.20.within_ref), custom_call_target="tpu_custom_call" | custom-call | tf_op jit(solution)/shard_map/fetch/pallas_call | solution.py:349
Async XLA Ops:
  0.0 7.6 %collective-permute-start = (bf16[512,1024]{1,0:T(8,128)(2,1)}, bf16[512,1024]{1,0:T(8,128)(2,1)S(1)}, u32[]{:S(2)}, u32[]{:S(2)}) collective-permute-start(bf16[512,1024]{1,0:T(8,128)(2,1)} %emb_ref.1), channel_id=1, source_target_pairs={{0,4},{1,5},{2,6},{3,7},{4,0},{5,1},{6,2},{7,3},{8,12},{9,13},{10,... | collective-permute-start | bytes 3145736 | tf_op jit(solution)/shard_map/ppermute | solution.py:326
  4.6 3.0 %collective-permute-start.1 = (s32[1,512]{1,0:T(1,128)S(1)}, s32[1,512]{1,0:T(1,128)S(1)}, u32[]{:S(2)}, u32[]{:S(2)}) collective-permute-start(s32[1,512]{1,0:T(1,128)S(1)} %bitcast.18), channel_id=1, source_target_pairs={{0,4},{1,5},{2,6},{3,7},{4,0},{5,1},{6,2},{7,3},{8,12},{9,13},{10,... | collective-permute-start | bytes 6152 | tf_op jit(solution)/shard_map/ppermute | solution.py:326
  4.7 1.2 %copy-start = (bf16[512,1024]{1,0:T(8,128)(2,1)S(1)}, bf16[512,1024]{1,0:T(8,128)(2,1)}, u32[]{:S(2)}) copy-start(bf16[512,1024]{1,0:T(8,128)(2,1)} %emb_ref.1) | copy-start | bytes 3145732
  59.8 29.3 %collective-permute-start.4 = (bf16[1024,896]{1,0:T(8,128)(2,1)S(1)}, bf16[1024,896]{1,0:T(8,128)(2,1)S(1)}, u32[]{:S(2)}, u32[]{:S(2)}) collective-permute-start(bf16[1024,896]{1,0:T(8,128)(2,1)S(1)} %bitcast.12), channel_id=1, source_target_pairs={{0,1},{1,2},{2,3},{3,0},{4,68},{5,69},{6,70},{7,71},{8,9},{9,10},{... | collective-permute-start | bytes 5505032 | tf_op jit(solution)/shard_map/ppermute | solution.py:326
  61.1 28.0 %collective-permute-start.2 = (bf16[1024,896]{1,0:T(8,128)(2,1)S(1)}, bf16[1024,896]{1,0:T(8,128)(2,1)S(1)}, u32[]{:S(2)}, u32[]{:S(2)}) collective-permute-start(bf16[1024,896]{1,0:T(8,128)(2,1)S(1)} %bitcast.13), channel_id=1, source_target_pairs={{0,3},{1,0},{2,1},{3,2},{4,196},{5,197},{6,198},{7,199},{8,11},{9,... | collective-permute-start | bytes 5505032 | tf_op jit(solution)/shard_map/ppermute | solution.py:326
  81.3 7.7 %collective-permute-start.5 = (bf16[32,40,128]{2,1,0:T(8,128)(2,1)S(1)}, bf16[32,40,128]{2,1,0:T(8,128)(2,1)S(1)}, u32[]{:S(2)}, u32[]{:S(2)}) collective-permute-start(bf16[32,40,128]{2,1,0:T(8,128)(2,1)S(1)} %all_to_all.16.last), channel_id=1, source_target_pairs={{0,1},{1,2},{2,3},{3,0},{4,68},{5,69},{6,70},{7,71},{8,9},{9,10},{... | collective-permute-start | bytes 983048 | tf_op jit(solution)/shard_map/ppermute | solution.py:326
  81.3 7.7 %collective-permute-start.3 = (bf16[32,40,128]{2,1,0:T(8,128)(2,1)S(1)}, bf16[32,40,128]{2,1,0:T(8,128)(2,1)S(1)}, u32[]{:S(2)}, u32[]{:S(2)}) collective-permute-start(bf16[32,40,128]{2,1,0:T(8,128)(2,1)S(1)} %all_to_all.16.last), channel_id=1, source_target_pairs={{0,3},{1,0},{2,1},{3,2},{4,196},{5,197},{6,198},{7,199},{8,11},{9,... | collective-permute-start | bytes 983048 | tf_op jit(solution)/shard_map/ppermute | solution.py:326

commit v5 on v4

--- a/solution.py
+++ b/solution.py
@@ -165,8 +165,11 @@
     )
 
 
-def scan_block(left, right, left_ids, right_ids, best, skip):
-    total = lax.dot_general(left, right, contract_last, preferred_element_type=jnp.float32)
+def product(left, right):
+    return lax.dot_general(left, right, contract_last, preferred_element_type=jnp.float32)
+
+
+def scan_block(total, left_ids, right_ids, best, skip):
     tops = []
     for half in range(wide // lanes):
         scores = total[:, half * lanes : (half + 1) * lanes]
@@ -192,8 +195,7 @@
     per = wide // lanes
     for at in range(rows // wide):
         best, _ = scan_block(
-            left,
-            features(main, last, at * wide, wide),
+            product(left, features(main, last, at * wide, wide)),
             columns,
             ids[at * per : (at + 1) * per, :],
             best,
@@ -202,14 +204,25 @@
     out_ref[...] = to_rows(best)
 
 
+def start_kernel(spot_ref, main, after, before, near_ref, side_ref):
+    low = spot_ref[1] == 1
+    rows = main.shape[0]
+    left = main[...]
+    side_left = jnp.where(low, before[: rows // 2, :], after[rows // 2 :, :])
+    for at in range(0, rows, wide):
+        near = after[at : at + wide, :]
+        near_ref[:, at : at + wide] = product(left, near)
+        right = jnp.where(low, near, before[at : at + wide, :])
+        side_ref[:, at : at + wide] = product(side_left, right)
+
+
 def cross_kernel(
     spot_ref,
-    main,
     last,
-    after,
     after_last,
-    before,
     before_last,
+    near_ref,
+    side_ref,
     inside_ref,
     ids_ref,
     out_ref,
@@ -229,21 +242,24 @@
     right_ids = jnp.where(low, after_ids, before_ids)
     left_ids = jnp.where(low, before_ids[: blocks // 2, :], after_ids[blocks // 2 :, :])
     left_columns = columns_of(left_ids)
-    side_left = jnp.where(
-        low,
-        features(before, before_last, 0, half),
-        features(after, after_last, half, half),
-    )
-    left = features(main, last, 0, rows)
+
+    def final(ref):
+        return ref[:, :field, :].reshape(rows, tail)
+
+    left, after, before = final(last), final(after_last), final(before_last)
+    side_left = jnp.where(low, before[:half, :], after[half:, :])
     per = wide // lanes
     best, far, up, side = None, None, [], []
     for at in range(rows // wide):
-        near = features(after, after_last, at * wide, wide)
-        right = jnp.where(low, near, features(before, before_last, at * wide, wide))
+        span = slice(at * wide, (at + 1) * wide)
+        near = after[span, :]
+        right = jnp.where(low, near, before[span, :])
         cut = slice(at * per, (at + 1) * per)
-        best, tops = scan_block(left, near, columns, after_ids[cut, :], best, None)
+        best, tops = scan_block(
+            near_ref[:, span] + product(left, near), columns, after_ids[cut, :], best, None)
         up += tops
-        far, tops = scan_block(side_left, right, left_columns, right_ids[cut, :], far, None)
+        far, tops = scan_block(
+            side_ref[:, span] + product(side_left, right), left_columns, right_ids[cut, :], far, None)
         side += tops
     up, side = jnp.concatenate(up, axis=0), jnp.concatenate(side, axis=0)
     mine = jnp.maximum(to_rows(best), inside_ref[...])
@@ -359,7 +375,8 @@
         return jax.ShapeDtypeStruct(shape, dtype)
 
     swap = other_core()
-    names = owner.reshape(1, rows) * labels + cluster.reshape(1, rows)
+    cluster = lax.optimization_barrier(cluster.reshape(rows, 1))
+    names = (owner * labels + cluster).reshape(1, rows)
     other_rows = send(embeddings, swap)
     other_names = send(names, swap)
     first, last, ids, within = call(
@@ -403,14 +420,25 @@
         scratch=[pltpu.VMEM((each, lanes), f32)],
     )
     count = groups * places
+    near, side = call(
+        start_kernel,
+        [array(spots, spots, dtype=f32), array(spots // 2, spots, dtype=f32)],
+        "start",
+        spot,
+        own[0],
+        after[0],
+        before[0],
+    )
     best = call(
         cross_kernel,
         array(count, lanes, dtype=f32),
         "cross",
         spot,
-        *own,
-        *after,
-        *before,
+        own[1],
+        after[1],
+        before[1],
+        near,
+        side,
         inside,
         ids,
         scratch=[pltpu.VMEM((2, each, lanes), f32), pltpu.VMEM((3, each, lanes), f32)],

time: 122 us -> 120 us (0.984)
  blocking collectives: 95.5 us -> 93 us
  Pallas kernels: 11.9 us -> 14 us
  waiting for transfers between devices: 2.56 us -> 1.16 us
    all_to_all x1, blocking collectives: 26.4 us -> 24.1 us  [shards(): lax.all_to_all(best.reshape(count, 1, 1, lanes), everyone, split_axis=0,...]
    pallas_call x5 -> x6, Pallas kernels: 11.9 us -> 14 us  [call(): pl.pallas_call(kernel, out_shape=out_shape, in_specs=[smem if a is spot e...]
    ppermute x6, waiting for transfers between devices: 2.56 us -> 1.16 us  [send(): return lax.ppermute(values, everyone, route)]
  transfers between devices with their start and end apart: 6 -> 6, of which waited for: 1 -> 1; matrix products, arithmetic and copies ran while one was open for 1% -> 1% of each run, Pallas kernels for 3% -> 7%
where the time goes in v5:
time: 120 us
  blocking collectives  93 us (78%)
  Pallas kernels  14 us (12%)
  starting transfers between devices  9.19 us (8%)
  local copies, waits for them, and re-layouts  1.23 us (1%)
    all_to_all x2, blocking collectives, trade(): lax.all_to_all(values, everyone, split_axis=0, concat_axis=0, axis_index_...  68.9 us
    all_to_all x1, blocking collectives, shards(): lax.all_to_all(best.reshape(count, 1, 1, lanes), everyone, split_axis=0,...  24.1 us
    pallas_call x6, Pallas kernels, call(): pl.pallas_call(kernel, out_shape=out_shape, in_specs=[smem if a is spot e...  14 us
    ppermute x6, starting transfers between devices, send(): return lax.ppermute(values, everyone, route)  9.19 us
  transfers between devices with their start and end apart: 6, of which 1 were waited for; matrix products, arithmetic and copies ran while one was open for 1% of the time, Pallas kernels for 7%

profile of v5, /device:TPU:1, one launch (start us, length us, event | category | flops | bytes accessed | tf_op | source)
XLA Modules:
  0.0 119.5 jit_solution(5176155233109357945)
XLA Ops:
  0.0 3.2 %collective-permute-start = (bf16[512,1024]{1,0:T(8,128)(2,1)}, bf16[512,1024]{1,0:T(8,128)(2,1)S(1)}, u32[]{:S(2)}, u32[]{:S(2)}) collective-permute-start(bf16[512,1024]{1,0:T(8,128)(2,1)} %emb_ref.1), channel_id=1, source_target_pairs={{0,4},{1,5},{2,6},{3,7},{4,0},{5,1},{6,2},{7,3},{8,12},{9,13},{10,... | collective-permute-start | bytes 3145736 | tf_op jit(solution)/shard_map/ppermute | solution.py:342
  3.2 0.7 add_bitcast_fusion.name_ref
  3.9 0.0 collective-permute-start.1
  4.0 0.1 pad_add_fusion.spot_ref
  4.0 0.0 copy-start
  4.1 1.2 %copy-done = bf16[512,1024]{1,0:T(8,128)(2,1)S(1)} copy-done((bf16[512,1024]{1,0:T(8,128)(2,1)S(1)}, bf16[512,1024]{1,0:T(8,128)(2,1)}, u32[]{:S(2)}) %copy-start) | copy-done | bytes 1048600
  5.3 1.7 %place.1 = (bf16[512,896]{1,0:T(8,128)(2,1)S(1)}, bf16[512,128]{1,0:T(8,128)(2,1)S(1)}, f32[32,128]{1,0:T(8,128)S(1)}, s32[1,512]{1,0:T(1,128)S(1)}) custom-call(s32[4]{0:T(128)S(1)} %pad_add_fusion.spot_ref, bf16[512,1024]{1,0:T(8,128)(2,1)S(1)} %copy-done, s32[1,512]{1,0:T(1,128)S(1)} %add_bitcast_fusion.name_ref), custom_call_target="tpu_custom_call" | custom-call | tf_op jit(solution)/shard_map/place/pallas_call | solution.py:365
  7.0 0.0 collective-permute-done.1.name_ref
  7.0 0.0 collective-permute-done.emb_ref
  7.0 1.8 %pair.1 = (bf16[32,32,896]{2,1,0:T(8,128)(2,1)S(1)}, bf16[32,40,128]{2,1,0:T(8,128)(2,1)S(1)}) custom-call(s32[4]{0:T(128)S(1)} %pad_add_fusion.spot_ref, bf16[512,1024]{1,0:T(8,128)(2,1)S(1)} %collective-permute-done.emb_ref, s32[1,512]{1,0:T(1,128)S(1)} %collective-permute-done.1.name_ref, bf16[512,896]{1,0:T(8,128)(2,1)S(1)} %get-tuple-element.15.first_ref, ...), custom_call_target="tpu_custom_call" | custom-call | tf_op jit(solution)/shard_map/pair/pallas_call | solution.py:365
  8.8 50.3 %all_to_all.15 = bf16[32,32,896]{2,1,0:T(8,128)(2,1)S(1)} all-to-all(bf16[32,32,896]{2,1,0:T(8,128)(2,1)S(1)} %get-tuple-element.19), channel_id=1, replica_groups={{0,8,16,24,32,40,48,56,64,72,80,88,96,104,112,120,128,136,144,152,160,1..., dimensions={0} | all-to-all | bytes 3670016 | tf_op jit(solution)/shard_map/all_to_all | solution.py:346
  59.1 2.9 %collective-permute-start.4 = (bf16[1024,896]{1,0:T(8,128)(2,1)S(1)}, bf16[1024,896]{1,0:T(8,128)(2,1)S(1)}, u32[]{:S(2)}, u32[]{:S(2)}) collective-permute-start(bf16[1024,896]{1,0:T(8,128)(2,1)S(1)} %bitcast.13), channel_id=1, source_target_pairs={{0,3},{1,0},{2,1},{3,2},{4,196},{5,197},{6,198},{7,199},{8,11},{9,... | collective-permute-start | bytes 5505032 | tf_op jit(solution)/shard_map/ppermute | solution.py:342
  62.0 0.0 collective-permute-start.5
  62.0 18.6 %all_to_all.16.last = bf16[32,40,128]{2,1,0:T(8,128)(2,1)S(1)} all-to-all(bf16[32,40,128]{2,1,0:T(8,128)(2,1)S(1)} %get-tuple-element.18), channel_id=1, replica_groups={{0,8,16,24,32,40,48,56,64,72,80,88,96,104,112,120,128,136,144,152,160,1..., dimensions={0} | all-to-all | bytes 655360 | tf_op jit(solution)/shard_map/all_to_all | solution.py:346
  80.6 3.1 %collective-permute-start.2 = (bf16[32,40,128]{2,1,0:T(8,128)(2,1)S(1)}, bf16[32,40,128]{2,1,0:T(8,128)(2,1)S(1)}, u32[]{:S(2)}, u32[]{:S(2)}) collective-permute-start(bf16[32,40,128]{2,1,0:T(8,128)(2,1)S(1)} %all_to_all.16.last), channel_id=1, source_target_pairs={{0,3},{1,0},{2,1},{3,2},{4,196},{5,197},{6,198},{7,199},{8,11},{9,... | collective-permute-start | bytes 983048 | tf_op jit(solution)/shard_map/ppermute | solution.py:342
  83.7 0.0 collective-permute-start.3
  83.7 2.5 %own.1 = (f32[8,128]{1,0:T(8,128)S(1)}, f32[8,128]{1,0:T(8,128)S(1)}) custom-call(bf16[1024,896]{1,0:T(8,128)(2,1)S(1)} %bitcast.15, bf16[32,40,128]{2,1,0:T(8,128)(2,1)S(1)} %all_to_all.16.last), custom_call_target="tpu_custom_call" | custom-call | tf_op jit(solution)/shard_map/own/pallas_call | solution.py:365
  86.2 0.0 collective-permute-done.4.after
  86.2 1.1 collective-permute-done.5.before
  87.3 4.1 %start.1 = (f32[1024,1024]{1,0:T(8,128)S(1)}, f32[512,1024]{1,0:T(8,128)S(1)}) custom-call(s32[4]{0:T(128)S(1)} %pad_add_fusion.spot_ref, bf16[1024,896]{1,0:T(8,128)(2,1)S(1)} %bitcast.16, bf16[1024,896]{1,0:T(8,128)(2,1)S(1)} %collective-permute-done.4.after, bf16[1024,896]{1,0:T(8,128)(2,1)S(1)} %collective-permute-done.5.before), custom_call_target="tpu_custom_call" | custom-call | tf_op jit(solution)/shard_map/start/pallas_call | solution.py:365
  91.4 0.0 collective-permute-done.2.after_last
  91.4 0.0 collective-permute-done.3.before_last
  91.4 2.5 %cross.1 = f32[256,128]{1,0:T(8,128)S(1)} custom-call(s32[4]{0:T(128)S(1)} %pad_add_fusion.spot_ref, bf16[32,40,128]{2,1,0:T(8,128)(2,1)S(1)} %all_to_all.16.last, bf16[32,40,128]{2,1,0:T(8,128)(2,1)S(1)} %collective-permute-done.2.after_last, bf16[32,40,128]{2,1,0:T(8,128)(2,1)S(1)} %collective-permute-done.3.before_last, ...), custom_call_target="tpu_custom_call" | custom-call | tf_op jit(solution)/shard_map/cross/pallas_call | solution.py:365
  93.9 24.1 %all_to_all.17 = f32[256,1,1,128]{3,2,1,0:T(1,128)S(1)} all-to-all(f32[256,1,1,128]{3,2,1,0:T(1,128)S(1)} %bitcast.17), channel_id=1, replica_groups=mesh['ingest'=64,'span'=4] {'ingest','span'}, dimensions={0} | all-to-all | bytes 262144 | tf_op jit(solution)/shard_map/all_to_all | solution.py:446
  118.0 1.5 %fetch.1 = f32[1,512]{1,0:T(1,128)} custom-call(s32[4]{0:T(128)S(1)} %pad_add_fusion.spot_ref, f32[256,128]{1,0:T(8,128)S(1)} %bitcast.18, s32[1,512]{1,0:T(1,128)S(1)} %add_bitcast_fusion.name_ref, s32[1,512]{1,0:T(1,128)S(1)} %get-tuple-element.24.within_ref), custom_call_target="tpu_custom_call" | custom-call | tf_op jit(solution)/shard_map/fetch/pallas_call | solution.py:365
Async XLA Ops:
  0.0 7.0 %collective-permute-start = (bf16[512,1024]{1,0:T(8,128)(2,1)}, bf16[512,1024]{1,0:T(8,128)(2,1)S(1)}, u32[]{:S(2)}, u32[]{:S(2)}) collective-permute-start(bf16[512,1024]{1,0:T(8,128)(2,1)} %emb_ref.1), channel_id=1, source_target_pairs={{0,4},{1,5},{2,6},{3,7},{4,0},{5,1},{6,2},{7,3},{8,12},{9,13},{10,... | collective-permute-start | bytes 3145736 | tf_op jit(solution)/shard_map/ppermute | solution.py:342
  3.9 3.0 %collective-permute-start.1 = (s32[1,512]{1,0:T(1,128)S(1)}, s32[1,512]{1,0:T(1,128)S(1)}, u32[]{:S(2)}, u32[]{:S(2)}) collective-permute-start(s32[1,512]{1,0:T(1,128)S(1)} %add_bitcast_fusion.name_ref), channel_id=1, source_target_pairs={{0,4},{1,5},{2,6},{3,7},{4,0},{5,1},{6,2},{7,3},{8,12},{9,13},{10,... | collective-permute-start | bytes 6152 | tf_op jit(solution)/shard_map/ppermute | solution.py:342
  4.0 1.2 %copy-start = (bf16[512,1024]{1,0:T(8,128)(2,1)S(1)}, bf16[512,1024]{1,0:T(8,128)(2,1)}, u32[]{:S(2)}) copy-start(bf16[512,1024]{1,0:T(8,128)(2,1)} %emb_ref.1) | copy-start | bytes 3145732
  59.1 27.0 %collective-permute-start.4 = (bf16[1024,896]{1,0:T(8,128)(2,1)S(1)}, bf16[1024,896]{1,0:T(8,128)(2,1)S(1)}, u32[]{:S(2)}, u32[]{:S(2)}) collective-permute-start(bf16[1024,896]{1,0:T(8,128)(2,1)S(1)} %bitcast.13), channel_id=1, source_target_pairs={{0,3},{1,0},{2,1},{3,2},{4,196},{5,197},{6,198},{7,199},{8,11},{9,... | collective-permute-start | bytes 5505032 | tf_op jit(solution)/shard_map/ppermute | solution.py:342
  62.0 25.3 %collective-permute-start.5 = (bf16[1024,896]{1,0:T(8,128)(2,1)S(1)}, bf16[1024,896]{1,0:T(8,128)(2,1)S(1)}, u32[]{:S(2)}, u32[]{:S(2)}) collective-permute-start(bf16[1024,896]{1,0:T(8,128)(2,1)S(1)} %bitcast.14), channel_id=1, source_target_pairs={{0,1},{1,2},{2,3},{3,0},{4,68},{5,69},{6,70},{7,71},{8,9},{9,10},{... | collective-permute-start | bytes 5505032 | tf_op jit(solution)/shard_map/ppermute | solution.py:342
  80.6 10.8 %collective-permute-start.2 = (bf16[32,40,128]{2,1,0:T(8,128)(2,1)S(1)}, bf16[32,40,128]{2,1,0:T(8,128)(2,1)S(1)}, u32[]{:S(2)}, u32[]{:S(2)}) collective-permute-start(bf16[32,40,128]{2,1,0:T(8,128)(2,1)S(1)} %all_to_all.16.last), channel_id=1, source_target_pairs={{0,3},{1,0},{2,1},{3,2},{4,196},{5,197},{6,198},{7,199},{8,11},{9,... | collective-permute-start | bytes 983048 | tf_op jit(solution)/shard_map/ppermute | solution.py:342
  83.7 7.7 %collective-permute-start.3 = (bf16[32,40,128]{2,1,0:T(8,128)(2,1)S(1)}, bf16[32,40,128]{2,1,0:T(8,128)(2,1)S(1)}, u32[]{:S(2)}, u32[]{:S(2)}) collective-permute-start(bf16[32,40,128]{2,1,0:T(8,128)(2,1)S(1)} %all_to_all.16.last), channel_id=1, source_target_pairs={{0,1},{1,2},{2,3},{3,0},{4,68},{5,69},{6,70},{7,71},{8,9},{9,10},{... | collective-permute-start | bytes 983048 | tf_op jit(solution)/shard_map/ppermute | solution.py:342

commit v6 on v5

--- a/solution.py
+++ b/solution.py
@@ -15,8 +15,9 @@
 places = 4
 depth = 8
 field = cores * capacity
-tail = 128
+first_rows = 208
 note = 8
+early = 6
 labels = 64
 contract_last = (((1,), (1,)), ((), ()))
 contract_first = (((1,), (0,)), ((), ()))
@@ -102,38 +103,50 @@
     return placed, ids, within
 
 
-def place_kernel(groups, spot_ref, emb_ref, name_ref, main_ref, tail_ref, ids_ref, within_ref):
+def place_kernel(groups, spot_ref, emb_ref, name_ref, half_ref, ids_ref, within_ref):
     placed, ids, within = put_rows(groups, 0, spot_ref, emb_ref, name_ref)
-    width = main_ref.shape[1]
-    for start in range(0, width, wide):
-        size = min(wide, width - start)
-        main_ref[:, start : start + size] = placed(start, size)
-    tail_ref[...] = placed(width, tail)
+    teams, count, _ = half_ref.shape
+    for start in range(0, count // capacity * lanes, wide):
+        values = placed(start, wide)
+        for shift in range(0, wide, lanes):
+            at = (start + shift) // lanes * capacity
+            half_ref[:, at : at + capacity, :] = values[:, shift : shift + lanes].reshape(
+                teams, capacity, lanes
+            )
     ids_ref[...] = ids
     within_ref[...] = within
 
 
-def pair_kernel(
-    groups, spot_ref, emb_ref, name_ref, first_ref, last_ref, ids_ref, main_ref, tail_ref
-):
+def pair_kernel(groups, spot_ref, emb_ref, name_ref, half_ref, ids_ref, main_ref, last_ref):
     placed, ids, _ = put_rows(groups, 1, spot_ref, emb_ref, name_ref)
-    teams, _, width = main_ref.shape
-    main_ref[:, :capacity, :] = first_ref[...].reshape(teams, capacity, width)
-    tail_ref[:, :capacity, :] = last_ref[...].reshape(teams, capacity, tail)
-    for start in range(0, width, wide):
-        size = min(wide, width - start)
-        main_ref[:, capacity:field, start : start + size] = placed(start, size).reshape(
-            teams, capacity, size
-        )
-    tail_ref[:, capacity:field, :] = placed(width, tail).reshape(teams, capacity, tail)
+    teams, count, _ = half_ref.shape
+    border = main_ref.shape[1]
+
+    def store(at, values):
+        if at < border:
+            main_ref[:, at : at + capacity, :] = values
+        else:
+            last_ref[:, at - border : at - border + capacity, :] = values
+
+    for start in range(0, count // capacity * lanes, wide):
+        values = placed(start, wide)
+        for shift in range(0, wide, lanes):
+            block = (start + shift) // lanes
+            store(block * field, half_ref[:, block * capacity : (block + 1) * capacity, :])
+            store(
+                block * field + capacity,
+                values[:, shift : shift + lanes].reshape(teams, capacity, lanes),
+            )
     ids = (ids + ids_ref[...] - 1.0).astype(jnp.bfloat16)
-    tail_ref[:, field:, :] = jnp.broadcast_to(ids[:, None, :], (teams, note, lanes))
+    last_ref[:, last_ref.shape[1] - note :, :] = jnp.broadcast_to(
+        ids[:, None, :], (teams, note, lanes)
+    )
 
 
 def read_ids(ref, hold):
     count = lanes // field
     blocks = ref.shape[0] // count
-    hold[...] = jnp.max(ref[:, field:, :].astype(jnp.float32), axis=1)
+    hold[...] = jnp.max(ref[:, ref.shape[1] - note :, :].astype(jnp.float32), axis=1)
     lane = lax.broadcasted_iota(jnp.int32, (blocks, lanes), 1)
     total = hold[pl.ds(0, blocks, stride=count), :]
     for q in range(1, count):
@@ -142,9 +155,20 @@
     return total
 
 
-def features(main, last, start, count):
-    rest = last[start // field : (start + count) // field, :field, :].reshape(count, tail)
-    return jnp.concatenate([main[start : start + count, :], rest], axis=1)
+def features(main, last, blocks, start, count):
+    teams = slice(start // field, (start + count) // field)
+    border = main.shape[1]
+    found = []
+    for block in blocks:
+        low, high = block * field, (block + 1) * field
+        parts = []
+        if low < border:
+            parts.append(main[teams, low : min(high, border), :])
+        if high > border:
+            parts.append(last[teams, max(low, border) - border : high - border, :])
+        piece = parts[0] if len(parts) == 1 else jnp.concatenate(parts, axis=1)
+        found.append(piece.reshape(count, lanes))
+    return jnp.concatenate(found, axis=1)
 
 
 def to_column(row):
@@ -188,14 +212,15 @@
 def own_kernel(main, last, out_ref, ids_ref, hold):
     ids = read_ids(last, hold)
     ids_ref[...] = ids
-    rows = main.shape[0]
+    rows = ids.shape[0] * lanes
+    blocks = range((main.shape[1] + last.shape[1] - note) // field)
     columns = columns_of(ids)
-    left = features(main, last, 0, rows)
+    left = features(main, last, blocks, 0, rows)
     best = None
     per = wide // lanes
     for at in range(rows // wide):
         best, _ = scan_block(
-            product(left, features(main, last, at * wide, wide)),
+            product(left, features(main, last, blocks, at * wide, wide)),
             columns,
             ids[at * per : (at + 1) * per, :],
             best,
@@ -206,20 +231,27 @@
 
 def start_kernel(spot_ref, main, after, before, near_ref, side_ref):
     low = spot_ref[1] == 1
-    rows = main.shape[0]
-    left = main[...]
-    side_left = jnp.where(low, before[: rows // 2, :], after[rows // 2 :, :])
+    rows = main.shape[0] * field
+    half = rows // 2
+    blocks = range(early)
+    left = features(main, None, blocks, 0, rows)
+    side_left = jnp.where(
+        low, features(before, None, blocks, 0, half), features(after, None, blocks, half, half)
+    )
     for at in range(0, rows, wide):
-        near = after[at : at + wide, :]
+        near = features(after, None, blocks, at, wide)
         near_ref[:, at : at + wide] = product(left, near)
-        right = jnp.where(low, near, before[at : at + wide, :])
+        right = jnp.where(low, near, features(before, None, blocks, at, wide))
         side_ref[:, at : at + wide] = product(side_left, right)
 
 
 def cross_kernel(
     spot_ref,
+    main,
     last,
+    after_main,
     after_last,
+    before_main,
     before_last,
     near_ref,
     side_ref,
@@ -238,16 +270,15 @@
     blocks = ids.shape[0]
     rows = blocks * lanes
     half = rows // 2
+    late = range(early, (main.shape[1] + last.shape[1] - note) // field)
+    left = features(main, last, late, 0, rows)
+    after = features(after_main, after_last, late, 0, rows)
+    before = features(before_main, before_last, late, 0, rows)
+    side_left = jnp.where(low, before[:half, :], after[half:, :])
     columns = columns_of(ids)
     right_ids = jnp.where(low, after_ids, before_ids)
     left_ids = jnp.where(low, before_ids[: blocks // 2, :], after_ids[blocks // 2 :, :])
     left_columns = columns_of(left_ids)
-
-    def final(ref):
-        return ref[:, :field, :].reshape(rows, tail)
-
-    left, after, before = final(last), final(after_last), final(before_last)
-    side_left = jnp.where(low, before[:half, :], after[half:, :])
     per = wide // lanes
     best, far, up, side = None, None, [], []
     for at in range(rows // wide):
@@ -326,14 +357,17 @@
     rows = owner.shape[1]
     team = lax.broadcasted_iota(jnp.int32, (places * depth, rows), 0)
     onehot = (team == owner // cores).astype(jnp.bfloat16)
-    found = jnp.zeros((lanes, rows), jnp.float32)
+    pieces = []
     for _ in range(3):
-        piece = rest.astype(jnp.bfloat16)
-        rest = rest - piece.astype(jnp.float32)
-        found = found + lax.dot_general(
-            piece, onehot, (((0,), (0,)), ((), ())), preferred_element_type=jnp.float32
-        )
-    lane = lax.broadcasted_iota(jnp.int32, (lanes, rows), 0)
+        pieces.append(rest.astype(jnp.bfloat16))
+        rest = rest - pieces[-1].astype(jnp.float32)
+    found = lax.dot_general(
+        jnp.concatenate(pieces, axis=0),
+        jnp.concatenate([onehot] * 3, axis=0),
+        (((0,), (0,)), ((), ())),
+        preferred_element_type=jnp.float32,
+    )[:field, :]
+    lane = lax.broadcasted_iota(jnp.int32, (field, rows), 0)
     within = within_ref[...] + owner % cores * capacity
     out_ref[...] = jnp.sum(jnp.where(lane == within, found, 0.0), axis=0, keepdims=True)
 
@@ -379,11 +413,11 @@
     names = (owner * labels + cluster).reshape(1, rows)
     other_rows = send(embeddings, swap)
     other_names = send(names, swap)
-    first, last, ids, within = call(
+    total = width // lanes * field
+    half, ids, within = call(
         functools.partial(place_kernel, groups),
         [
-            array(spots // cores, width - tail),
-            array(spots // cores, tail),
+            array(each, total // cores, lanes),
             array(each, lanes, dtype=f32),
             array(1, rows, dtype=jnp.int32),
         ],
@@ -394,21 +428,18 @@
     )
     parts = call(
         functools.partial(pair_kernel, groups),
-        [array(each, field, width - tail), array(each, field + note, tail)],
+        [array(each, first_rows, lanes), array(each, total - first_rows + note, lanes)],
         "pair",
         spot,
         other_rows,
         other_names,
-        first,
-        last,
+        half,
         ids,
     )
     teams = plane_teams()
     own, after, before = [], [], []
     for part in parts:
         got = trade(part, teams)
-        if not own:
-            got = got.reshape(spots, width - tail)
         own.append(got)
         before.append(send(got, beside(1)))
         after.append(send(got, beside(-1)))
@@ -434,9 +465,9 @@
         array(count, lanes, dtype=f32),
         "cross",
         spot,
-        own[1],
-        after[1],
-        before[1],
+        *own,
+        *after,
+        *before,
         near,
         side,
         inside,

time: 120 us -> 118 us (0.983)
  transfers between devices with their start and end apart: 6 -> 6, of which waited for: 1 -> 1; matrix products, arithmetic and copies ran while one was open for 1% -> 1% of each run, Pallas kernels for 7% -> 6%
where the time goes in v6:
time: 118 us
  blocking collectives  93.7 us (79%)
  Pallas kernels  13 us (11%)
  starting transfers between devices  8.61 us (7%)
  local copies, waits for them, and re-layouts  1.23 us (1%)
    all_to_all x2, blocking collectives, trade(): lax.all_to_all(values, everyone, split_axis=0, concat_axis=0, axis_index_...  69.1 us
    all_to_all x1, blocking collectives, shards(): lax.all_to_all(best.reshape(count, 1, 1, lanes), everyone, split_axis=0,...  24.6 us
    pallas_call x6, Pallas kernels, call(): pl.pallas_call(kernel, out_shape=out_shape, in_specs=[smem if a is spot e...  13 us
    ppermute x6, starting transfers between devices, send(): return lax.ppermute(values, everyone, route)  8.61 us
  transfers between devices with their start and end apart: 6, of which 1 were waited for; matrix products, arithmetic and copies ran while one was open for 1% of the time, Pallas kernels for 6%

profile of v6, /device:TPU:1, one launch (start us, length us, event | category | flops | bytes accessed | tf_op | source)
XLA Modules:
  0.0 117.9 jit_solution(14901957149851605320)
XLA Ops:
  0.0 3.2 %collective-permute-start = (bf16[512,1024]{1,0:T(8,128)(2,1)}, bf16[512,1024]{1,0:T(8,128)(2,1)S(1)}, u32[]{:S(2)}, u32[]{:S(2)}) collective-permute-start(bf16[512,1024]{1,0:T(8,128)(2,1)} %emb_ref.1), channel_id=1, source_target_pairs={{0,4},{1,5},{2,6},{3,7},{4,0},{5,1},{6,2},{7,3},{8,12},{9,13},{10,... | collective-permute-start | bytes 3145736 | tf_op jit(solution)/shard_map/ppermute | solution.py:376
  3.2 0.7 add_bitcast_fusion.name_ref
  3.9 0.0 collective-permute-start.1
  4.0 0.1 pad_add_fusion.spot_ref
  4.0 0.0 copy-start
  4.1 1.2 %copy-done = bf16[512,1024]{1,0:T(8,128)(2,1)S(1)} copy-done((bf16[512,1024]{1,0:T(8,128)(2,1)S(1)}, bf16[512,1024]{1,0:T(8,128)(2,1)}, u32[]{:S(2)}) %copy-start) | copy-done | bytes 1048600
  5.3 1.6 %place.1 = (bf16[32,128,128]{2,1,0:T(8,128)(2,1)S(1)}, f32[32,128]{1,0:T(8,128)S(1)}, s32[1,512]{1,0:T(1,128)S(1)}) custom-call(s32[4]{0:T(128)S(1)} %pad_add_fusion.spot_ref, bf16[512,1024]{1,0:T(8,128)(2,1)S(1)} %copy-done, s32[1,512]{1,0:T(1,128)S(1)} %add_bitcast_fusion.name_ref), custom_call_target="tpu_custom_call" | custom-call | tf_op jit(solution)/shard_map/place/pallas_call | solution.py:399
  6.9 0.0 collective-permute-done.1.name_ref
  6.9 0.0 collective-permute-done.emb_ref
  6.9 1.6 %pair.1 = (bf16[32,208,128]{2,1,0:T(8,128)(2,1)S(1)}, bf16[32,56,128]{2,1,0:T(8,128)(2,1)S(1)}) custom-call(s32[4]{0:T(128)S(1)} %pad_add_fusion.spot_ref, bf16[512,1024]{1,0:T(8,128)(2,1)S(1)} %collective-permute-done.emb_ref, s32[1,512]{1,0:T(1,128)S(1)} %collective-permute-done.1.name_ref, bf16[32,128,128]{2,1,0:T(8,128)(2,1)S(1)} %get-tuple-element.14.half_ref, ...), custom_call_target="tpu_custom_call" | custom-call | tf_op jit(solution)/shard_map/pair/pallas_call | solution.py:399
  8.5 48.1 %all_to_all.15.main = bf16[32,208,128]{2,1,0:T(8,128)(2,1)S(1)} all-to-all(bf16[32,208,128]{2,1,0:T(8,128)(2,1)S(1)} %get-tuple-element.16), channel_id=1, replica_groups={{0,8,16,24,32,40,48,56,64,72,80,88,96,104,112,120,128,136,144,152,160,1..., dimensions={0} | all-to-all | bytes 3407872 | tf_op jit(solution)/shard_map/all_to_all | solution.py:380
  56.6 1.0 collective-permute-start.4
  57.6 1.7 %collective-permute-start.2 = (bf16[32,208,128]{2,1,0:T(8,128)(2,1)S(1)}, bf16[32,208,128]{2,1,0:T(8,128)(2,1)S(1)}, u32[]{:S(2)}, u32[]{:S(2)}) collective-permute-start(bf16[32,208,128]{2,1,0:T(8,128)(2,1)S(1)} %all_to_all.15.main), channel_id=1, source_target_pairs={{0,3},{1,0},{2,1},{3,2},{4,196},{5,197},{6,198},{7,199},{8,11},{9,... | collective-permute-start | bytes 5111816 | tf_op jit(solution)/shard_map/ppermute | solution.py:376
  59.3 21.1 %all_to_all.16.last = bf16[32,56,128]{2,1,0:T(8,128)(2,1)S(1)} all-to-all(bf16[32,56,128]{2,1,0:T(8,128)(2,1)S(1)} %get-tuple-element.17), channel_id=1, replica_groups={{0,8,16,24,32,40,48,56,64,72,80,88,96,104,112,120,128,136,144,152,160,1..., dimensions={0} | all-to-all | bytes 917504 | tf_op jit(solution)/shard_map/all_to_all | solution.py:380
  80.4 0.0 collective-permute-start.5
  80.4 2.7 %collective-permute-start.3 = (bf16[32,56,128]{2,1,0:T(8,128)(2,1)S(1)}, bf16[32,56,128]{2,1,0:T(8,128)(2,1)S(1)}, u32[]{:S(2)}, u32[]{:S(2)}) collective-permute-start(bf16[32,56,128]{2,1,0:T(8,128)(2,1)S(1)} %all_to_all.16.last), channel_id=1, source_target_pairs={{0,3},{1,0},{2,1},{3,2},{4,196},{5,197},{6,198},{7,199},{8,11},{9,... | collective-permute-start | bytes 1376264 | tf_op jit(solution)/shard_map/ppermute | solution.py:376
  83.0 2.5 %own.1 = (f32[8,128]{1,0:T(8,128)S(1)}, f32[8,128]{1,0:T(8,128)S(1)}) custom-call(bf16[32,208,128]{2,1,0:T(8,128)(2,1)S(1)} %all_to_all.15.main, bf16[32,56,128]{2,1,0:T(8,128)(2,1)S(1)} %all_to_all.16.last), custom_call_target="tpu_custom_call" | custom-call | tf_op jit(solution)/shard_map/own/pallas_call | solution.py:399
  85.5 0.0 collective-permute-done.4.before.before_main
  85.5 0.0 collective-permute-done.2.after.after_main
  85.5 3.2 %start.1 = (f32[1024,1024]{1,0:T(8,128)S(1)}, f32[512,1024]{1,0:T(8,128)S(1)}) custom-call(s32[4]{0:T(128)S(1)} %pad_add_fusion.spot_ref, bf16[32,208,128]{2,1,0:T(8,128)(2,1)S(1)} %all_to_all.15.main, bf16[32,208,128]{2,1,0:T(8,128)(2,1)S(1)} %collective-permute-done.2.after.after_main, bf16[32,208,128]{2,1,0:T(8,128)(2,1)S(1)} %collective-permute-done.4.before.before_main), custom_call_target="tpu_custom_call" | custom-call | tf_op jit(solution)/shard_map/start/pallas_call | solution.py:399
  88.7 0.4 collective-permute-done.5.before_last
  89.2 0.0 collective-permute-done.3.after_last
  89.2 2.7 %cross.1 = f32[256,128]{1,0:T(8,128)S(1)} custom-call(s32[4]{0:T(128)S(1)} %pad_add_fusion.spot_ref, bf16[32,208,128]{2,1,0:T(8,128)(2,1)S(1)} %all_to_all.15.main, bf16[32,56,128]{2,1,0:T(8,128)(2,1)S(1)} %all_to_all.16.last, bf16[32,208,128]{2,1,0:T(8,128)(2,1)S(1)} %collective-permute-done.2.after.after_main, ...), custom_call_target="tpu_custom_call" | custom-call | tf_op jit(solution)/shard_map/cross/pallas_call | solution.py:399
  91.9 24.6 %all_to_all.17 = f32[256,1,1,128]{3,2,1,0:T(1,128)S(1)} all-to-all(f32[256,1,1,128]{3,2,1,0:T(1,128)S(1)} %bitcast.12), channel_id=1, replica_groups=mesh['ingest'=64,'span'=4] {'ingest','span'}, dimensions={0} | all-to-all | bytes 262144 | tf_op jit(solution)/shard_map/all_to_all | solution.py:477
  116.5 1.4 %fetch.1 = f32[1,512]{1,0:T(1,128)} custom-call(s32[4]{0:T(128)S(1)} %pad_add_fusion.spot_ref, f32[256,128]{1,0:T(8,128)S(1)} %bitcast.13, s32[1,512]{1,0:T(1,128)S(1)} %add_bitcast_fusion.name_ref, s32[1,512]{1,0:T(1,128)S(1)} %get-tuple-element.22.within_ref), custom_call_target="tpu_custom_call" | custom-call | tf_op jit(solution)/shard_map/fetch/pallas_call | solution.py:399
Async XLA Ops:
  0.0 6.9 %collective-permute-start = (bf16[512,1024]{1,0:T(8,128)(2,1)}, bf16[512,1024]{1,0:T(8,128)(2,1)S(1)}, u32[]{:S(2)}, u32[]{:S(2)}) collective-permute-start(bf16[512,1024]{1,0:T(8,128)(2,1)} %emb_ref.1), channel_id=1, source_target_pairs={{0,4},{1,5},{2,6},{3,7},{4,0},{5,1},{6,2},{7,3},{8,12},{9,13},{10,... | collective-permute-start | bytes 3145736 | tf_op jit(solution)/shard_map/ppermute | solution.py:376
  3.9 2.9 %collective-permute-start.1 = (s32[1,512]{1,0:T(1,128)S(1)}, s32[1,512]{1,0:T(1,128)S(1)}, u32[]{:S(2)}, u32[]{:S(2)}) collective-permute-start(s32[1,512]{1,0:T(1,128)S(1)} %add_bitcast_fusion.name_ref), channel_id=1, source_target_pairs={{0,4},{1,5},{2,6},{3,7},{4,0},{5,1},{6,2},{7,3},{8,12},{9,13},{10,... | collective-permute-start | bytes 6152 | tf_op jit(solution)/shard_map/ppermute | solution.py:376
  4.0 1.2 %copy-start = (bf16[512,1024]{1,0:T(8,128)(2,1)S(1)}, bf16[512,1024]{1,0:T(8,128)(2,1)}, u32[]{:S(2)}) copy-start(bf16[512,1024]{1,0:T(8,128)(2,1)} %emb_ref.1) | copy-start | bytes 3145732
  56.6 28.9 %collective-permute-start.4 = (bf16[32,208,128]{2,1,0:T(8,128)(2,1)S(1)}, bf16[32,208,128]{2,1,0:T(8,128)(2,1)S(1)}, u32[]{:S(2)}, u32[]{:S(2)}) collective-permute-start(bf16[32,208,128]{2,1,0:T(8,128)(2,1)S(1)} %all_to_all.15.main), channel_id=1, source_target_pairs={{0,1},{1,2},{2,3},{3,0},{4,68},{5,69},{6,70},{7,71},{8,9},{9,10},{... | collective-permute-start | bytes 5111816 | tf_op jit(solution)/shard_map/ppermute | solution.py:376
  57.6 28.0 %collective-permute-start.2 = (bf16[32,208,128]{2,1,0:T(8,128)(2,1)S(1)}, bf16[32,208,128]{2,1,0:T(8,128)(2,1)S(1)}, u32[]{:S(2)}, u32[]{:S(2)}) collective-permute-start(bf16[32,208,128]{2,1,0:T(8,128)(2,1)S(1)} %all_to_all.15.main), channel_id=1, source_target_pairs={{0,3},{1,0},{2,1},{3,2},{4,196},{5,197},{6,198},{7,199},{8,11},{9,... | collective-permute-start | bytes 5111816 | tf_op jit(solution)/shard_map/ppermute | solution.py:376
  80.4 8.8 %collective-permute-start.5 = (bf16[32,56,128]{2,1,0:T(8,128)(2,1)S(1)}, bf16[32,56,128]{2,1,0:T(8,128)(2,1)S(1)}, u32[]{:S(2)}, u32[]{:S(2)}) collective-permute-start(bf16[32,56,128]{2,1,0:T(8,128)(2,1)S(1)} %all_to_all.16.last), channel_id=1, source_target_pairs={{0,1},{1,2},{2,3},{3,0},{4,68},{5,69},{6,70},{7,71},{8,9},{9,10},{... | collective-permute-start | bytes 1376264 | tf_op jit(solution)/shard_map/ppermute | solution.py:376
  80.4 8.8 %collective-permute-start.3 = (bf16[32,56,128]{2,1,0:T(8,128)(2,1)S(1)}, bf16[32,56,128]{2,1,0:T(8,128)(2,1)S(1)}, u32[]{:S(2)}, u32[]{:S(2)}) collective-permute-start(bf16[32,56,128]{2,1,0:T(8,128)(2,1)S(1)} %all_to_all.16.last), channel_id=1, source_target_pairs={{0,3},{1,0},{2,1},{3,2},{4,196},{5,197},{6,198},{7,199},{8,11},{9,... | collective-permute-start | bytes 1376264 | tf_op jit(solution)/shard_map/ppermute | solution.py:376

commit v7 on v6

--- a/solution.py
+++ b/solution.py
@@ -15,10 +15,12 @@
 places = 4
 depth = 8
 field = cores * capacity
-first_rows = 208
 note = 8
 early = 6
+first_rows = 208
+nowhere = -4.0
 labels = 64
+label_bits, core_bits, field_bits = 6, 1, 5
 contract_last = (((1,), (1,)), ((), ()))
 contract_first = (((1,), (0,)), ((), ()))
 everyone = ("ingest", "span")
@@ -76,10 +78,10 @@
 
 def put_rows(groups, side, spot_ref, emb_ref, name_ref):
     core = spot_ref[0]
-    owner = name_ref[...] // labels
+    owner = name_ref[...] >> label_bits
     rows = owner.shape[1]
     within = rank_rows(owner, groups)
-    slot = jnp.where(owner % cores == core, owner // cores * capacity + within, -1)
+    slot = jnp.where((owner & (cores - 1)) == core, (owner >> core_bits) * capacity + within, -1)
     room = groups // cores * capacity
     put = (lax.broadcasted_iota(jnp.int32, (room, rows), 0) == slot).astype(jnp.bfloat16)
     values = emb_ref[...].astype(jnp.float32)
@@ -95,8 +97,8 @@
         ).astype(jnp.bfloat16)
 
     team = lax.broadcasted_iota(jnp.int32, (groups // cores, rows), 0)
-    here = (team == owner // cores) & (owner % cores == core)
-    named = here.astype(jnp.bfloat16) * (name_ref[...] % labels + 1).astype(jnp.bfloat16)
+    here = (team == (owner >> core_bits)) & ((owner & (cores - 1)) == core)
+    named = here.astype(jnp.bfloat16) * ((name_ref[...] & (labels - 1)) + 1).astype(jnp.bfloat16)
     lane = lax.broadcasted_iota(jnp.int32, (lanes, rows), 0)
     into = (lane == within + side * capacity).astype(jnp.bfloat16)
     ids = lax.dot_general(named, into, contract_last, preferred_element_type=jnp.float32)
@@ -120,7 +122,7 @@
 def pair_kernel(groups, spot_ref, emb_ref, name_ref, half_ref, ids_ref, main_ref, last_ref):
     placed, ids, _ = put_rows(groups, 1, spot_ref, emb_ref, name_ref)
     teams, count, _ = half_ref.shape
-    border = main_ref.shape[1]
+    border = main_ref.shape[1] - note
 
     def store(at, values):
         if at < border:
@@ -138,7 +140,7 @@
                 values[:, shift : shift + lanes].reshape(teams, capacity, lanes),
             )
     ids = (ids + ids_ref[...] - 1.0).astype(jnp.bfloat16)
-    last_ref[:, last_ref.shape[1] - note :, :] = jnp.broadcast_to(
+    main_ref[:, border:, :] = jnp.broadcast_to(
         ids[:, None, :], (teams, note, lanes)
     )
 
@@ -151,21 +153,20 @@
     total = hold[pl.ds(0, blocks, stride=count), :]
     for q in range(1, count):
         piece = pltpu.roll(hold[pl.ds(q, blocks, stride=count), :], field * q, 1)
-        total = jnp.where(lane // field == q, piece, total)
+        total = jnp.where(lane >> field_bits == q, piece, total)
     return total
 
 
-def features(main, last, blocks, start, count):
+def features(refs, blocks, start, count):
     teams = slice(start // field, (start + count) // field)
-    border = main.shape[1]
     found = []
     for block in blocks:
         low, high = block * field, (block + 1) * field
         parts = []
-        if low < border:
-            parts.append(main[teams, low : min(high, border), :])
-        if high > border:
-            parts.append(last[teams, max(low, border) - border : high - border, :])
+        if low < first_rows:
+            parts.append(refs[0][teams, low : min(high, first_rows), :])
+        if high > first_rows:
+            parts.append(refs[1][teams, max(low, first_rows) - first_rows : high - first_rows, :])
         piece = parts[0] if len(parts) == 1 else jnp.concatenate(parts, axis=1)
         found.append(piece.reshape(count, lanes))
     return jnp.concatenate(found, axis=1)
@@ -193,56 +194,82 @@
     return lax.dot_general(left, right, contract_last, preferred_element_type=jnp.float32)
 
 
-def scan_block(total, left_ids, right_ids, best, skip):
-    tops = []
-    for half in range(wide // lanes):
-        scores = total[:, half * lanes : (half + 1) * lanes]
-        ids = right_ids[half : half + 1, :]
-        same = left_ids == jnp.where(ids < 0, -2.0, ids)
-        if skip is not None:
+def own_kernel(main, last, out_ref, hold):
+    ids = read_ids(main, hold)
+    rows = ids.shape[0] * lanes
+    blocks = range((first_rows + last.shape[1]) // field)
+    columns = columns_of(ids)
+    left = features((main, last), blocks, 0, rows)
+    steps, per = rows // wide, wide // lanes
+    best, tops = [None] * steps, []
+    for at in range(steps):
+        begin = at * wide
+        masked = []
+        total = product(left[begin:, :], left[begin : begin + wide, :])
+        for h in range(per):
+            scores = total[:, h * lanes : (h + 1) * lanes]
+            row_ids = ids[at * per + h : at * per + h + 1, :]
             row = lax.broadcasted_iota(jnp.int32, scores.shape, 0)
             column = lax.broadcasted_iota(jnp.int32, scores.shape, 1)
-            same = same & (row - column != skip + half * lanes)
-        masked = jnp.where(same, scores, -1.0)
-        best = masked if best is None else jnp.maximum(best, masked)
-        tops.append(jnp.max(masked, axis=0, keepdims=True))
-    return best, tops
-
-
-def own_kernel(main, last, out_ref, ids_ref, hold):
-    ids = read_ids(last, hold)
-    ids_ref[...] = ids
-    rows = ids.shape[0] * lanes
-    blocks = range((main.shape[1] + last.shape[1] - note) // field)
+            same = columns[begin:, :] == jnp.where(row_ids < 0, -2.0, row_ids)
+            masked.append(jnp.where(same & (row - column != h * lanes), scores, -1.0))
+            tops.append(jnp.max(masked[-1], axis=0, keepdims=True))
+        both = jnp.maximum(masked[0], masked[1])
+        for i in range(at, steps):
+            part = both[i * wide - begin : (i + 1) * wide - begin, :]
+            best[i] = part if best[i] is None else jnp.maximum(best[i], part)
+    out_ref[...] = jnp.maximum(
+        to_rows(jnp.concatenate(best, axis=0)), jnp.concatenate(tops, axis=0)
+    )
+
+
+def masked_sums(sums, left_ids, right_ids):
+    return jnp.concatenate(
+        [
+            jnp.where(
+                left_ids == jnp.where(right_ids[h : h + 1, :] < 0, -2.0, right_ids[h : h + 1, :]),
+                sums[:, h * lanes : (h + 1) * lanes],
+                nowhere,
+            )
+            for h in range(wide // lanes)
+        ],
+        axis=1,
+    )
+
+
+def start_kernel(spot_ref, main, after, before, near_ref, side_ref, hold):
+    low = spot_ref[1] == 1
+    ids, after_ids, before_ids = [
+        read_ids(ref, hold.at[i]) for i, ref in enumerate((main, after, before))
+    ]
+    count = ids.shape[0]
+    rows = count * lanes
+    half = rows // 2
     columns = columns_of(ids)
-    left = features(main, last, blocks, 0, rows)
-    best = None
+    right_ids = jnp.where(low, after_ids, before_ids)
+    left_ids = jnp.where(low, before_ids[: count // 2, :], after_ids[count // 2 :, :])
+    left_columns = columns_of(left_ids)
+    blocks = range(early)
+    left = features((main,), blocks, 0, rows)
+    side_left = jnp.where(
+        low, features((before,), blocks, 0, half), features((after,), blocks, half, half)
+    )
     per = wide // lanes
     for at in range(rows // wide):
-        best, _ = scan_block(
-            product(left, features(main, last, blocks, at * wide, wide)),
-            columns,
-            ids[at * per : (at + 1) * per, :],
-            best,
-            at * wide,
+        span, cut = slice(at * wide, (at + 1) * wide), slice(at * per, (at + 1) * per)
+        near = features((after,), blocks, at * wide, wide)
+        near_ref[:, span] = masked_sums(product(left, near), columns, after_ids[cut, :])
+        right = jnp.where(low, near, features((before,), blocks, at * wide, wide))
+        side_ref[:, span] = masked_sums(
+            product(side_left, right), left_columns, right_ids[cut, :]
         )
-    out_ref[...] = to_rows(best)
-
-
-def start_kernel(spot_ref, main, after, before, near_ref, side_ref):
-    low = spot_ref[1] == 1
-    rows = main.shape[0] * field
-    half = rows // 2
-    blocks = range(early)
-    left = features(main, None, blocks, 0, rows)
-    side_left = jnp.where(
-        low, features(before, None, blocks, 0, half), features(after, None, blocks, half, half)
-    )
-    for at in range(0, rows, wide):
-        near = features(after, None, blocks, at, wide)
-        near_ref[:, at : at + wide] = product(left, near)
-        right = jnp.where(low, near, features(before, None, blocks, at, wide))
-        side_ref[:, at : at + wide] = product(side_left, right)
+
+
+def add_block(total, best):
+    halves = [total[:, h * lanes : (h + 1) * lanes] for h in range(wide // lanes)]
+    for part in halves:
+        best = part if best is None else jnp.maximum(best, part)
+    return best, [jnp.max(part, axis=0, keepdims=True) for part in halves]
 
 
 def cross_kernel(
@@ -256,41 +283,27 @@
     near_ref,
     side_ref,
     inside_ref,
-    ids_ref,
     out_ref,
-    hold,
     table,
 ):
     low = spot_ref[1] == 1
-    ids, after_ids, before_ids = (
-        ids_ref[...],
-        read_ids(after_last, hold.at[0]),
-        read_ids(before_last, hold.at[1]),
-    )
-    blocks = ids.shape[0]
+    blocks = inside_ref.shape[0]
     rows = blocks * lanes
     half = rows // 2
-    late = range(early, (main.shape[1] + last.shape[1] - note) // field)
-    left = features(main, last, late, 0, rows)
-    after = features(after_main, after_last, late, 0, rows)
-    before = features(before_main, before_last, late, 0, rows)
+    late = range(early, (first_rows + last.shape[1]) // field)
+    left, after, before = [
+        features(refs, late, 0, rows)
+        for refs in ((main, last), (after_main, after_last), (before_main, before_last))
+    ]
     side_left = jnp.where(low, before[:half, :], after[half:, :])
-    columns = columns_of(ids)
-    right_ids = jnp.where(low, after_ids, before_ids)
-    left_ids = jnp.where(low, before_ids[: blocks // 2, :], after_ids[blocks // 2 :, :])
-    left_columns = columns_of(left_ids)
-    per = wide // lanes
     best, far, up, side = None, None, [], []
     for at in range(rows // wide):
         span = slice(at * wide, (at + 1) * wide)
         near = after[span, :]
         right = jnp.where(low, near, before[span, :])
-        cut = slice(at * per, (at + 1) * per)
-        best, tops = scan_block(
-            near_ref[:, span] + product(left, near), columns, after_ids[cut, :], best, None)
+        best, tops = add_block(near_ref[:, span] + product(left, near), best)
         up += tops
-        far, tops = scan_block(
-            side_ref[:, span] + product(side_left, right), left_columns, right_ids[cut, :], far, None)
+        far, tops = add_block(side_ref[:, span] + product(side_left, right), far)
         side += tops
     up, side = jnp.concatenate(up, axis=0), jnp.concatenate(side, axis=0)
     mine = jnp.maximum(to_rows(best), inside_ref[...])
@@ -353,10 +366,10 @@
     odd = pltpu.roll(jnp.concatenate(odd, axis=0), capacity, 1)
     rest = jnp.where(lax.broadcasted_iota(jnp.int32, even.shape, 1) < capacity, even, odd)
     rest = jnp.where(lax.broadcasted_iota(jnp.int32, even.shape, 1) < field, rest, 0.0)
-    owner = name_ref[...] // labels
+    owner = name_ref[...] >> label_bits
     rows = owner.shape[1]
     team = lax.broadcasted_iota(jnp.int32, (places * depth, rows), 0)
-    onehot = (team == owner // cores).astype(jnp.bfloat16)
+    onehot = (team == (owner >> core_bits)).astype(jnp.bfloat16)
     pieces = []
     for _ in range(3):
         pieces.append(rest.astype(jnp.bfloat16))
@@ -368,7 +381,7 @@
         preferred_element_type=jnp.float32,
     )[:field, :]
     lane = lax.broadcasted_iota(jnp.int32, (field, rows), 0)
-    within = within_ref[...] + owner % cores * capacity
+    within = within_ref[...] + (owner & (cores - 1)) * capacity
     out_ref[...] = jnp.sum(jnp.where(lane == within, found, 0.0), axis=0, keepdims=True)
 
 
@@ -428,7 +441,7 @@
     )
     parts = call(
         functools.partial(pair_kernel, groups),
-        [array(each, first_rows, lanes), array(each, total - first_rows + note, lanes)],
+        [array(each, first_rows + note, lanes), array(each, total - first_rows, lanes)],
         "pair",
         spot,
         other_rows,
@@ -443,14 +456,8 @@
         own.append(got)
         before.append(send(got, beside(1)))
         after.append(send(got, beside(-1)))
-    inside, ids = call(
-        own_kernel,
-        [array(blocks, lanes, dtype=f32)] * 2,
-        "own",
-        *own,
-        scratch=[pltpu.VMEM((each, lanes), f32)],
-    )
-    count = groups * places
+    held = pltpu.VMEM((each, lanes), f32)
+    inside = call(own_kernel, array(blocks, lanes, dtype=f32), "own", *own, scratch=[held])
     near, side = call(
         start_kernel,
         [array(spots, spots, dtype=f32), array(spots // 2, spots, dtype=f32)],
@@ -459,7 +466,9 @@
         own[0],
         after[0],
         before[0],
-    )
+        scratch=[pltpu.VMEM((3, each, lanes), f32)],
+    )
+    count = groups * places
     best = call(
         cross_kernel,
         array(count, lanes, dtype=f32),
@@ -471,8 +480,7 @@
         near,
         side,
         inside,
-        ids,
-        scratch=[pltpu.VMEM((2, each, lanes), f32), pltpu.VMEM((3, each, lanes), f32)],
+        scratch=[pltpu.VMEM((3, each, lanes), f32)],
     )
     back = lax.all_to_all(
         best.reshape(count, 1, 1, lanes), everyone, split_axis=0, concat_axis=0, tiled=True

time: 118 us -> 117 us (level)
  Pallas kernels: 13 us -> 11.7 us
    pallas_call x6, Pallas kernels: 13 us -> 11.7 us  [call(): pl.pallas_call(kernel, out_shape=out_shape, in_specs=[smem if a is spot e...]
where the time goes in v7:
time: 117 us
  blocking collectives  94.1 us (80%)
  Pallas kernels  11.7 us (10%)
  starting transfers between devices  8.63 us (7%)
  local copies, waits for them, and re-layouts  1.23 us (1%)
    all_to_all x2, blocking collectives, trade(): lax.all_to_all(values, everyone, split_axis=0, concat_axis=0, axis_index_...  69.3 us
    all_to_all x1, blocking collectives, shards(): lax.all_to_all(best.reshape(count, 1, 1, lanes), everyone, split_axis=0,...  24.8 us
    pallas_call x6, Pallas kernels, call(): pl.pallas_call(kernel, out_shape=out_shape, in_specs=[smem if a is spot e...  11.7 us
    ppermute x6, starting transfers between devices, send(): return lax.ppermute(values, everyone, route)  8.63 us
  transfers between devices with their start and end apart: 6, of which 1 were waited for; matrix products, arithmetic and copies ran while one was open for 1% of the time, Pallas kernels for 6%

profile of v7, /device:TPU:1, one launch (start us, length us, event | category | flops | bytes accessed | tf_op | source)
XLA Modules:
  0.0 117.0 jit_solution(9389081731743637449)
XLA Ops:
  0.0 3.2 %collective-permute-start = (bf16[512,1024]{1,0:T(8,128)(2,1)}, bf16[512,1024]{1,0:T(8,128)(2,1)S(1)}, u32[]{:S(2)}, u32[]{:S(2)}) collective-permute-start(bf16[512,1024]{1,0:T(8,128)(2,1)} %emb_ref.1), channel_id=1, source_target_pairs={{0,4},{1,5},{2,6},{3,7},{4,0},{5,1},{6,2},{7,3},{8,12},{9,13},{10,... | collective-permute-start | bytes 3145736 | tf_op jit(solution)/shard_map/ppermute | solution.py:389
  3.2 0.7 add_bitcast_fusion.name_ref
  3.9 0.0 collective-permute-start.1
  4.0 0.1 pad_add_fusion.spot_ref
  4.0 0.0 copy-start
  4.1 1.2 %copy-done = bf16[512,1024]{1,0:T(8,128)(2,1)S(1)} copy-done((bf16[512,1024]{1,0:T(8,128)(2,1)S(1)}, bf16[512,1024]{1,0:T(8,128)(2,1)}, u32[]{:S(2)}) %copy-start) | copy-done | bytes 1048600
  5.3 1.6 %place.1 = (bf16[32,128,128]{2,1,0:T(8,128)(2,1)S(1)}, f32[32,128]{1,0:T(8,128)S(1)}, s32[1,512]{1,0:T(1,128)S(1)}) custom-call(s32[4]{0:T(128)S(1)} %pad_add_fusion.spot_ref, bf16[512,1024]{1,0:T(8,128)(2,1)S(1)} %copy-done, s32[1,512]{1,0:T(1,128)S(1)} %add_bitcast_fusion.name_ref), custom_call_target="tpu_custom_call" | custom-call | tf_op jit(solution)/shard_map/place/pallas_call | solution.py:412
  6.8 0.0 collective-permute-done.1.name_ref
  6.9 0.0 collective-permute-done.emb_ref
  6.9 1.6 %pair.1 = (bf16[32,216,128]{2,1,0:T(8,128)(2,1)S(1)}, bf16[32,48,128]{2,1,0:T(8,128)(2,1)S(1)}) custom-call(s32[4]{0:T(128)S(1)} %pad_add_fusion.spot_ref, bf16[512,1024]{1,0:T(8,128)(2,1)S(1)} %collective-permute-done.emb_ref, s32[1,512]{1,0:T(1,128)S(1)} %collective-permute-done.1.name_ref, bf16[32,128,128]{2,1,0:T(8,128)(2,1)S(1)} %get-tuple-element.12.half_ref, ...), custom_call_target="tpu_custom_call" | custom-call | tf_op jit(solution)/shard_map/pair/pallas_call | solution.py:412
  8.5 49.2 %all_to_all.15.main = bf16[32,216,128]{2,1,0:T(8,128)(2,1)S(1)} all-to-all(bf16[32,216,128]{2,1,0:T(8,128)(2,1)S(1)} %get-tuple-element.14), channel_id=1, replica_groups={{0,8,16,24,32,40,48,56,64,72,80,88,96,104,112,120,128,136,144,152,160,1..., dimensions={0} | all-to-all | bytes 3538944 | tf_op jit(solution)/shard_map/all_to_all | solution.py:393
  57.7 1.5 %collective-permute-start.4 = (bf16[32,216,128]{2,1,0:T(8,128)(2,1)S(1)}, bf16[32,216,128]{2,1,0:T(8,128)(2,1)S(1)}, u32[]{:S(2)}, u32[]{:S(2)}) collective-permute-start(bf16[32,216,128]{2,1,0:T(8,128)(2,1)S(1)} %all_to_all.15.main), channel_id=1, source_target_pairs={{0,1},{1,2},{2,3},{3,0},{4,68},{5,69},{6,70},{7,71},{8,9},{9,10},{... | collective-permute-start | bytes 5308424 | tf_op jit(solution)/shard_map/ppermute | solution.py:389
  59.2 1.3 %collective-permute-start.2 = (bf16[32,216,128]{2,1,0:T(8,128)(2,1)S(1)}, bf16[32,216,128]{2,1,0:T(8,128)(2,1)S(1)}, u32[]{:S(2)}, u32[]{:S(2)}) collective-permute-start(bf16[32,216,128]{2,1,0:T(8,128)(2,1)S(1)} %all_to_all.15.main), channel_id=1, source_target_pairs={{0,3},{1,0},{2,1},{3,2},{4,196},{5,197},{6,198},{7,199},{8,11},{9,... | collective-permute-start | bytes 5308424 | tf_op jit(solution)/shard_map/ppermute | solution.py:389
  60.4 20.1 %all_to_all.16.last = bf16[32,48,128]{2,1,0:T(8,128)(2,1)S(1)} all-to-all(bf16[32,48,128]{2,1,0:T(8,128)(2,1)S(1)} %get-tuple-element.15), channel_id=1, replica_groups={{0,8,16,24,32,40,48,56,64,72,80,88,96,104,112,120,128,136,144,152,160,1..., dimensions={0} | all-to-all | bytes 786432 | tf_op jit(solution)/shard_map/all_to_all | solution.py:393
  80.6 0.0 collective-permute-start.5
  80.6 2.7 %collective-permute-start.3 = (bf16[32,48,128]{2,1,0:T(8,128)(2,1)S(1)}, bf16[32,48,128]{2,1,0:T(8,128)(2,1)S(1)}, u32[]{:S(2)}, u32[]{:S(2)}) collective-permute-start(bf16[32,48,128]{2,1,0:T(8,128)(2,1)S(1)} %all_to_all.16.last), channel_id=1, source_target_pairs={{0,3},{1,0},{2,1},{3,2},{4,196},{5,197},{6,198},{7,199},{8,11},{9,... | collective-permute-start | bytes 1179656 | tf_op jit(solution)/shard_map/ppermute | solution.py:389
  83.2 1.7 %own.1.inside_ref = f32[8,128]{1,0:T(8,128)S(1)} custom-call(bf16[32,216,128]{2,1,0:T(8,128)(2,1)S(1)} %all_to_all.15.main, bf16[32,48,128]{2,1,0:T(8,128)(2,1)S(1)} %all_to_all.16.last), custom_call_target="tpu_custom_call" | custom-call | tf_op jit(solution)/shard_map/own/pallas_call | solution.py:412
  84.9 0.0 collective-permute-done.4.before.before_main
  84.9 0.0 collective-permute-done.2.after.after_main
  85.0 3.3 %start.1 = (f32[1024,1024]{1,0:T(8,128)S(1)}, f32[512,1024]{1,0:T(8,128)S(1)}) custom-call(s32[4]{0:T(128)S(1)} %pad_add_fusion.spot_ref, bf16[32,216,128]{2,1,0:T(8,128)(2,1)S(1)} %all_to_all.15.main, bf16[32,216,128]{2,1,0:T(8,128)(2,1)S(1)} %collective-permute-done.2.after.after_main, bf16[32,216,128]{2,1,0:T(8,128)(2,1)S(1)} %collective-permute-done.4.before.before_main), custom_call_target="tpu_custom_call" | custom-call | tf_op jit(solution)/shard_map/start/pallas_call | solution.py:412
  88.3 0.4 collective-permute-done.5.before_last
  88.7 0.0 collective-permute-done.3.after_last
  88.7 2.1 %cross.1 = f32[256,128]{1,0:T(8,128)S(1)} custom-call(s32[4]{0:T(128)S(1)} %pad_add_fusion.spot_ref, bf16[32,216,128]{2,1,0:T(8,128)(2,1)S(1)} %all_to_all.15.main, bf16[32,48,128]{2,1,0:T(8,128)(2,1)S(1)} %all_to_all.16.last, bf16[32,216,128]{2,1,0:T(8,128)(2,1)S(1)} %collective-permute-done.2.after.after_main, ...), custom_call_target="tpu_custom_call" | custom-call | tf_op jit(solution)/shard_map/cross/pallas_call | solution.py:412
  90.8 24.8 %all_to_all.17 = f32[256,1,1,128]{3,2,1,0:T(1,128)S(1)} all-to-all(f32[256,1,1,128]{3,2,1,0:T(1,128)S(1)} %bitcast.12), channel_id=1, replica_groups=mesh['ingest'=64,'span'=4] {'ingest','span'}, dimensions={0} | all-to-all | bytes 262144 | tf_op jit(solution)/shard_map/all_to_all | solution.py:485
  115.6 1.4 %fetch.1 = f32[1,512]{1,0:T(1,128)} custom-call(s32[4]{0:T(128)S(1)} %pad_add_fusion.spot_ref, f32[256,128]{1,0:T(8,128)S(1)} %bitcast.13, s32[1,512]{1,0:T(1,128)S(1)} %add_bitcast_fusion.name_ref, s32[1,512]{1,0:T(1,128)S(1)} %get-tuple-element.18.within_ref), custom_call_target="tpu_custom_call" | custom-call | tf_op jit(solution)/shard_map/fetch/pallas_call | solution.py:412
Async XLA Ops:
  0.0 6.9 %collective-permute-start = (bf16[512,1024]{1,0:T(8,128)(2,1)}, bf16[512,1024]{1,0:T(8,128)(2,1)S(1)}, u32[]{:S(2)}, u32[]{:S(2)}) collective-permute-start(bf16[512,1024]{1,0:T(8,128)(2,1)} %emb_ref.1), channel_id=1, source_target_pairs={{0,4},{1,5},{2,6},{3,7},{4,0},{5,1},{6,2},{7,3},{8,12},{9,13},{10,... | collective-permute-start | bytes 3145736 | tf_op jit(solution)/shard_map/ppermute | solution.py:389
  3.9 2.9 %collective-permute-start.1 = (s32[1,512]{1,0:T(1,128)S(1)}, s32[1,512]{1,0:T(1,128)S(1)}, u32[]{:S(2)}, u32[]{:S(2)}) collective-permute-start(s32[1,512]{1,0:T(1,128)S(1)} %add_bitcast_fusion.name_ref), channel_id=1, source_target_pairs={{0,4},{1,5},{2,6},{3,7},{4,0},{5,1},{6,2},{7,3},{8,12},{9,13},{10,... | collective-permute-start | bytes 6152 | tf_op jit(solution)/shard_map/ppermute | solution.py:389
  4.0 1.2 %copy-start = (bf16[512,1024]{1,0:T(8,128)(2,1)S(1)}, bf16[512,1024]{1,0:T(8,128)(2,1)}, u32[]{:S(2)}) copy-start(bf16[512,1024]{1,0:T(8,128)(2,1)} %emb_ref.1) | copy-start | bytes 3145732
  57.7 27.2 %collective-permute-start.4 = (bf16[32,216,128]{2,1,0:T(8,128)(2,1)S(1)}, bf16[32,216,128]{2,1,0:T(8,128)(2,1)S(1)}, u32[]{:S(2)}, u32[]{:S(2)}) collective-permute-start(bf16[32,216,128]{2,1,0:T(8,128)(2,1)S(1)} %all_to_all.15.main), channel_id=1, source_target_pairs={{0,1},{1,2},{2,3},{3,0},{4,68},{5,69},{6,70},{7,71},{8,9},{9,10},{... | collective-permute-start | bytes 5308424 | tf_op jit(solution)/shard_map/ppermute | solution.py:389
  59.2 25.8 %collective-permute-start.2 = (bf16[32,216,128]{2,1,0:T(8,128)(2,1)S(1)}, bf16[32,216,128]{2,1,0:T(8,128)(2,1)S(1)}, u32[]{:S(2)}, u32[]{:S(2)}) collective-permute-start(bf16[32,216,128]{2,1,0:T(8,128)(2,1)S(1)} %all_to_all.15.main), channel_id=1, source_target_pairs={{0,3},{1,0},{2,1},{3,2},{4,196},{5,197},{6,198},{7,199},{8,11},{9,... | collective-permute-start | bytes 5308424 | tf_op jit(solution)/shard_map/ppermute | solution.py:389
  80.6 8.1 %collective-permute-start.5 = (bf16[32,48,128]{2,1,0:T(8,128)(2,1)S(1)}, bf16[32,48,128]{2,1,0:T(8,128)(2,1)S(1)}, u32[]{:S(2)}, u32[]{:S(2)}) collective-permute-start(bf16[32,48,128]{2,1,0:T(8,128)(2,1)S(1)} %all_to_all.16.last), channel_id=1, source_target_pairs={{0,1},{1,2},{2,3},{3,0},{4,68},{5,69},{6,70},{7,71},{8,9},{9,10},{... | collective-permute-start | bytes 1179656 | tf_op jit(solution)/shard_map/ppermute | solution.py:389
  80.6 8.1 %collective-permute-start.3 = (bf16[32,48,128]{2,1,0:T(8,128)(2,1)S(1)}, bf16[32,48,128]{2,1,0:T(8,128)(2,1)S(1)}, u32[]{:S(2)}, u32[]{:S(2)}) collective-permute-start(bf16[32,48,128]{2,1,0:T(8,128)(2,1)S(1)} %all_to_all.16.last), channel_id=1, source_target_pairs={{0,3},{1,0},{2,1},{3,2},{4,196},{5,197},{6,198},{7,199},{8,11},{9,... | collective-permute-start | bytes 1179656 | tf_op jit(solution)/shard_map/ppermute | solution.py:389

commit v8 on v7

--- a/solution.py
+++ b/solution.py
@@ -19,8 +19,7 @@
 early = 6
 first_rows = 208
 nowhere = -4.0
-labels = 64
-label_bits, core_bits, field_bits = 6, 1, 5
+core_bits, field_bits = 1, 5
 contract_last = (((1,), (1,)), ((), ()))
 contract_first = (((1,), (0,)), ((), ()))
 everyone = ("ingest", "span")
@@ -76,9 +75,9 @@
     return jnp.sum(jnp.where(belongs, before, 0.0), axis=0, keepdims=True).astype(jnp.int32)
 
 
-def put_rows(groups, side, spot_ref, emb_ref, name_ref):
+def put_rows(groups, side, spot_ref, emb_ref, owner_ref, cluster_ref):
     core = spot_ref[0]
-    owner = name_ref[...] >> label_bits
+    owner = owner_ref[...]
     rows = owner.shape[1]
     within = rank_rows(owner, groups)
     slot = jnp.where((owner & (cores - 1)) == core, (owner >> core_bits) * capacity + within, -1)
@@ -98,15 +97,24 @@
 
     team = lax.broadcasted_iota(jnp.int32, (groups // cores, rows), 0)
     here = (team == (owner >> core_bits)) & ((owner & (cores - 1)) == core)
-    named = here.astype(jnp.bfloat16) * ((name_ref[...] & (labels - 1)) + 1).astype(jnp.bfloat16)
+    named = here.astype(jnp.bfloat16) * (cluster_ref[...] + 1).astype(jnp.bfloat16)
     lane = lax.broadcasted_iota(jnp.int32, (lanes, rows), 0)
     into = (lane == within + side * capacity).astype(jnp.bfloat16)
     ids = lax.dot_general(named, into, contract_last, preferred_element_type=jnp.float32)
     return placed, ids, within
 
 
-def place_kernel(groups, spot_ref, emb_ref, name_ref, half_ref, ids_ref, within_ref):
-    placed, ids, within = put_rows(groups, 0, spot_ref, emb_ref, name_ref)
+def place_kernel(groups, spot_ref, *refs):
+    sources, (half_ref, ids_ref, plan_ref), held, done = refs[:3], refs[3:6], refs[6:9], refs[9]
+    copies = [
+        pltpu.make_async_copy(source, kept, done.at[i])
+        for i, (source, kept) in enumerate(zip(sources, held))
+    ]
+    for copy in copies[::-1]:
+        copy.start()
+    for copy in copies[::-1]:
+        copy.wait()
+    placed, ids, within = put_rows(groups, 0, spot_ref, *held)
     teams, count, _ = half_ref.shape
     for start in range(0, count // capacity * lanes, wide):
         values = placed(start, wide)
@@ -116,11 +124,15 @@
                 teams, capacity, lanes
             )
     ids_ref[...] = ids
-    within_ref[...] = within
-
-
-def pair_kernel(groups, spot_ref, emb_ref, name_ref, half_ref, ids_ref, main_ref, last_ref):
-    placed, ids, _ = put_rows(groups, 1, spot_ref, emb_ref, name_ref)
+    owner = held[1][...]
+    plan_ref[0:1, :] = owner >> core_bits
+    plan_ref[1:2, :] = within + (owner & (cores - 1)) * capacity
+
+
+def pair_kernel(
+    groups, spot_ref, emb_ref, owner_ref, cluster_ref, half_ref, ids_ref, main_ref, last_ref
+):
+    placed, ids, _ = put_rows(groups, 1, spot_ref, emb_ref, owner_ref, cluster_ref)
     teams, count, _ = half_ref.shape
     border = main_ref.shape[1] - note
 
@@ -348,7 +360,7 @@
                     ]
 
 
-def fetch_kernel(spot_ref, back_ref, name_ref, within_ref, out_ref):
+def fetch_kernel(spot_ref, back_ref, plan_ref, out_ref):
     x, y = spot_ref[2], spot_ref[3]
     each = places * depth
     across = cores * places
@@ -366,10 +378,9 @@
     odd = pltpu.roll(jnp.concatenate(odd, axis=0), capacity, 1)
     rest = jnp.where(lax.broadcasted_iota(jnp.int32, even.shape, 1) < capacity, even, odd)
     rest = jnp.where(lax.broadcasted_iota(jnp.int32, even.shape, 1) < field, rest, 0.0)
-    owner = name_ref[...] >> label_bits
-    rows = owner.shape[1]
+    rows = plan_ref.shape[1]
     team = lax.broadcasted_iota(jnp.int32, (places * depth, rows), 0)
-    onehot = (team == (owner >> core_bits)).astype(jnp.bfloat16)
+    onehot = (team == plan_ref[0:1, :]).astype(jnp.bfloat16)
     pieces = []
     for _ in range(3):
         pieces.append(rest.astype(jnp.bfloat16))
@@ -381,8 +392,7 @@
         preferred_element_type=jnp.float32,
     )[:field, :]
     lane = lax.broadcasted_iota(jnp.int32, (field, rows), 0)
-    within = within_ref[...] + (owner & (cores - 1)) * capacity
-    out_ref[...] = jnp.sum(jnp.where(lane == within, found, 0.0), axis=0, keepdims=True)
+    out_ref[...] = jnp.sum(jnp.where(lane == plan_ref[1:2, :], found, 0.0), axis=0, keepdims=True)
 
 
 def send(values, route):
@@ -422,30 +432,28 @@
         return jax.ShapeDtypeStruct(shape, dtype)
 
     swap = other_core()
-    cluster = lax.optimization_barrier(cluster.reshape(rows, 1))
-    names = (owner * labels + cluster).reshape(1, rows)
-    other_rows = send(embeddings, swap)
-    other_names = send(names, swap)
+    sources = embeddings, owner.reshape(1, rows), cluster.reshape(1, rows)
+    others = [send(values, swap) for values in sources]
     total = width // lanes * field
-    half, ids, within = call(
+    half, ids, plan = pl.pallas_call(
         functools.partial(place_kernel, groups),
-        [
+        out_shape=[
             array(each, total // cores, lanes),
             array(each, lanes, dtype=f32),
-            array(1, rows, dtype=jnp.int32),
+            array(2, rows, dtype=jnp.int32),
         ],
-        "place",
-        spot,
-        embeddings,
-        names,
-    )
+        in_specs=[smem] + [pl.BlockSpec(memory_space=pltpu.HBM)] * 3,
+        scratch_shapes=[pltpu.VMEM(values.shape, values.dtype) for values in sources]
+        + [pltpu.SemaphoreType.DMA((3,))],
+        compiler_params=params(),
+        name="place",
+    )(spot, *[pltpu.with_memory_space_constraint(values, pltpu.HBM) for values in sources])
     parts = call(
         functools.partial(pair_kernel, groups),
         [array(each, first_rows + note, lanes), array(each, total - first_rows, lanes)],
         "pair",
         spot,
-        other_rows,
-        other_names,
+        *others,
         half,
         ids,
     )
@@ -485,7 +493,7 @@
     back = lax.all_to_all(
         best.reshape(count, 1, 1, lanes), everyone, split_axis=0, concat_axis=0, tiled=True
     ).reshape(count, lanes)
-    result = call(fetch_kernel, array(1, rows, dtype=f32), "fetch", spot, back, names, within)
+    result = call(fetch_kernel, array(1, rows, dtype=f32), "fetch", spot, back, plan)
     return result.reshape(rows)
 
 

time: 117 us -> 117 us (level)
  starting transfers between devices: 8.63 us -> 10.5 us
  blocking collectives: 94.1 us -> 92.7 us
  Pallas kernels: 11.7 us -> 13 us
  local copies, waits for them, and re-layouts: 1.23 us -> 0 us
    pallas_call x0 -> x1, Pallas kernels: none -> 2.85 us  [shards(): pl.pallas_call(functools.partial(place_kernel, groups), out_shape=[array(...]
    ppermute x6 -> x7, starting transfers between devices: 8.63 us -> 10.5 us  [send(): return lax.ppermute(values, everyone, route)]
    pallas_call x6 -> x5, Pallas kernels: 11.7 us -> 10.2 us  [call(): pl.pallas_call(kernel, out_shape=out_shape, in_specs=[smem if a is spot e...]
    unnamed x2 -> x0, local copies, waits for them, and re-layouts: 1.23 us -> none
  transfers between devices with their start and end apart: 6 -> 7, of which waited for: 1 -> 1; matrix products, arithmetic and copies ran while one was open for 1% -> 0% of each run, Pallas kernels for 6% -> 7%
where the time goes in v8:
time: 117 us
  blocking collectives  92.7 us (79%)
  Pallas kernels  13 us (11%)
  starting transfers between devices  10.5 us (9%)
    all_to_all x2, blocking collectives, trade(): lax.all_to_all(values, everyone, split_axis=0, concat_axis=0, axis_index_...  68.4 us
    all_to_all x1, blocking collectives, shards(): lax.all_to_all(best.reshape(count, 1, 1, lanes), everyone, split_axis=0,...  24.3 us
    ppermute x7, starting transfers between devices, send(): return lax.ppermute(values, everyone, route)  10.5 us
    pallas_call x5, Pallas kernels, call(): pl.pallas_call(kernel, out_shape=out_shape, in_specs=[smem if a is spot e...  10.2 us
    pallas_call x1, Pallas kernels, shards(): pl.pallas_call(functools.partial(place_kernel, groups), out_shape=[array(...  2.85 us
  transfers between devices with their start and end apart: 7, of which 1 were waited for; matrix products, arithmetic and copies ran while one was open for 0% of the time, Pallas kernels for 7%

profile of v8, /device:TPU:1, one launch (start us, length us, event | category | flops | bytes accessed | tf_op | source)
XLA Modules:
  0.0 116.8 jit_solution(13815251890456483548)
XLA Ops:
  0.0 3.2 %collective-permute-start = (bf16[512,1024]{1,0:T(8,128)(2,1)}, bf16[512,1024]{1,0:T(8,128)(2,1)S(1)}, u32[]{:S(2)}, u32[]{:S(2)}) collective-permute-start(bf16[512,1024]{1,0:T(8,128)(2,1)} %refs_0_.1), channel_id=1, source_target_pairs={{0,4},{1,5},{2,6},{3,7},{4,0},{5,1},{6,2},{7,3},{8,12},{9,13},{10,... | collective-permute-start | bytes 3145736 | tf_op jit(solution)/shard_map/ppermute | solution.py:399
  3.2 0.0 collective-permute-start.1
  3.2 0.5 collective-permute-start.2
  3.8 0.1 pad_add_fusion.spot_ref
  3.8 2.9 %place.1 = (bf16[32,128,128]{2,1,0:T(8,128)(2,1)S(1)}, f32[32,128]{1,0:T(8,128)S(1)}, s32[2,512]{1,0:T(2,128)S(1)}) custom-call(s32[4]{0:T(128)S(1)} %pad_add_fusion.spot_ref, bf16[512,1024]{1,0:T(8,128)(2,1)} %refs_0_.1, s32[1,512]{1,0:T(1,128)} %bitcast.14, s32[1,512]{1,0:T(1,128)} %bitcast.16), custom_call_target="tpu_custom_call" | custom-call | tf_op jit(solution)/shard_map/place/pallas_call | solution.py:438
  6.7 0.0 collective-permute-done.1.owner_ref
  6.7 0.0 collective-permute-done.2.cluster_ref
  6.7 0.0 collective-permute-done.emb_ref
  6.7 1.6 %pair.1 = (bf16[32,216,128]{2,1,0:T(8,128)(2,1)S(1)}, bf16[32,48,128]{2,1,0:T(8,128)(2,1)S(1)}) custom-call(s32[4]{0:T(128)S(1)} %pad_add_fusion.spot_ref, bf16[512,1024]{1,0:T(8,128)(2,1)S(1)} %collective-permute-done.emb_ref, s32[1,512]{1,0:T(1,128)S(1)} %collective-permute-done.1.owner_ref, s32[1,512]{1,0:T(1,128)S(1)} %collective-permute-done.2.cluster_ref, ...), custom_call_target="tpu_custom_call" | custom-call | tf_op jit(solution)/shard_map/pair/pallas_call | solution.py:422
  8.4 49.6 %all_to_all.15.main = bf16[32,216,128]{2,1,0:T(8,128)(2,1)S(1)} all-to-all(bf16[32,216,128]{2,1,0:T(8,128)(2,1)S(1)} %get-tuple-element.14), channel_id=1, replica_groups={{0,8,16,24,32,40,48,56,64,72,80,88,96,104,112,120,128,136,144,152,160,1..., dimensions={0} | all-to-all | bytes 3538944 | tf_op jit(solution)/shard_map/all_to_all | solution.py:403
  57.9 2.1 %collective-permute-start.5 = (bf16[32,216,128]{2,1,0:T(8,128)(2,1)S(1)}, bf16[32,216,128]{2,1,0:T(8,128)(2,1)S(1)}, u32[]{:S(2)}, u32[]{:S(2)}) collective-permute-start(bf16[32,216,128]{2,1,0:T(8,128)(2,1)S(1)} %all_to_all.15.main), channel_id=1, source_target_pairs={{0,1},{1,2},{2,3},{3,0},{4,68},{5,69},{6,70},{7,71},{8,9},{9,10},{... | collective-permute-start | bytes 5308424 | tf_op jit(solution)/shard_map/ppermute | solution.py:399
  60.0 2.0 %collective-permute-start.3 = (bf16[32,216,128]{2,1,0:T(8,128)(2,1)S(1)}, bf16[32,216,128]{2,1,0:T(8,128)(2,1)S(1)}, u32[]{:S(2)}, u32[]{:S(2)}) collective-permute-start(bf16[32,216,128]{2,1,0:T(8,128)(2,1)S(1)} %all_to_all.15.main), channel_id=1, source_target_pairs={{0,3},{1,0},{2,1},{3,2},{4,196},{5,197},{6,198},{7,199},{8,11},{9,... | collective-permute-start | bytes 5308424 | tf_op jit(solution)/shard_map/ppermute | solution.py:399
  62.0 18.9 %all_to_all.16.last = bf16[32,48,128]{2,1,0:T(8,128)(2,1)S(1)} all-to-all(bf16[32,48,128]{2,1,0:T(8,128)(2,1)S(1)} %get-tuple-element.15), channel_id=1, replica_groups={{0,8,16,24,32,40,48,56,64,72,80,88,96,104,112,120,128,136,144,152,160,1..., dimensions={0} | all-to-all | bytes 786432 | tf_op jit(solution)/shard_map/all_to_all | solution.py:403
  80.9 0.0 collective-permute-start.6
  80.9 2.7 %collective-permute-start.4 = (bf16[32,48,128]{2,1,0:T(8,128)(2,1)S(1)}, bf16[32,48,128]{2,1,0:T(8,128)(2,1)S(1)}, u32[]{:S(2)}, u32[]{:S(2)}) collective-permute-start(bf16[32,48,128]{2,1,0:T(8,128)(2,1)S(1)} %all_to_all.16.last), channel_id=1, source_target_pairs={{0,3},{1,0},{2,1},{3,2},{4,196},{5,197},{6,198},{7,199},{8,11},{9,... | collective-permute-start | bytes 1179656 | tf_op jit(solution)/shard_map/ppermute | solution.py:399
  83.6 1.7 %own.1.inside_ref = f32[8,128]{1,0:T(8,128)S(1)} custom-call(bf16[32,216,128]{2,1,0:T(8,128)(2,1)S(1)} %all_to_all.15.main, bf16[32,48,128]{2,1,0:T(8,128)(2,1)S(1)} %all_to_all.16.last), custom_call_target="tpu_custom_call" | custom-call | tf_op jit(solution)/shard_map/own/pallas_call | solution.py:422
  85.3 0.0 collective-permute-done.5.before.before_main
  85.3 0.0 collective-permute-done.3.after.after_main
  85.3 3.3 %start.1 = (f32[1024,1024]{1,0:T(8,128)S(1)}, f32[512,1024]{1,0:T(8,128)S(1)}) custom-call(s32[4]{0:T(128)S(1)} %pad_add_fusion.spot_ref, bf16[32,216,128]{2,1,0:T(8,128)(2,1)S(1)} %all_to_all.15.main, bf16[32,216,128]{2,1,0:T(8,128)(2,1)S(1)} %collective-permute-done.3.after.after_main, bf16[32,216,128]{2,1,0:T(8,128)(2,1)S(1)} %collective-permute-done.5.before.before_main), custom_call_target="tpu_custom_call" | custom-call | tf_op jit(solution)/shard_map/start/pallas_call | solution.py:422
  88.6 0.4 collective-permute-done.6.before_last
  89.0 0.0 collective-permute-done.4.after_last
  89.0 2.1 %cross.1 = f32[256,128]{1,0:T(8,128)S(1)} custom-call(s32[4]{0:T(128)S(1)} %pad_add_fusion.spot_ref, bf16[32,216,128]{2,1,0:T(8,128)(2,1)S(1)} %all_to_all.15.main, bf16[32,48,128]{2,1,0:T(8,128)(2,1)S(1)} %all_to_all.16.last, bf16[32,216,128]{2,1,0:T(8,128)(2,1)S(1)} %collective-permute-done.3.after.after_main, ...), custom_call_target="tpu_custom_call" | custom-call | tf_op jit(solution)/shard_map/cross/pallas_call | solution.py:422
  91.1 24.3 %all_to_all.17 = f32[256,1,1,128]{3,2,1,0:T(1,128)S(1)} all-to-all(f32[256,1,1,128]{3,2,1,0:T(1,128)S(1)} %bitcast.11), channel_id=1, replica_groups=mesh['ingest'=64,'span'=4] {'ingest','span'}, dimensions={0} | all-to-all | bytes 262144 | tf_op jit(solution)/shard_map/all_to_all | solution.py:493
  115.4 1.4 %fetch.1 = f32[1,512]{1,0:T(1,128)} custom-call(s32[4]{0:T(128)S(1)} %pad_add_fusion.spot_ref, f32[256,128]{1,0:T(8,128)S(1)} %bitcast.12, s32[2,512]{1,0:T(2,128)S(1)} %get-tuple-element.18.plan_ref), custom_call_target="tpu_custom_call" | custom-call | tf_op jit(solution)/shard_map/fetch/pallas_call | solution.py:422
Async XLA Ops:
  0.0 6.7 %collective-permute-start = (bf16[512,1024]{1,0:T(8,128)(2,1)}, bf16[512,1024]{1,0:T(8,128)(2,1)S(1)}, u32[]{:S(2)}, u32[]{:S(2)}) collective-permute-start(bf16[512,1024]{1,0:T(8,128)(2,1)} %refs_0_.1), channel_id=1, source_target_pairs={{0,4},{1,5},{2,6},{3,7},{4,0},{5,1},{6,2},{7,3},{8,12},{9,13},{10,... | collective-permute-start | bytes 3145736 | tf_op jit(solution)/shard_map/ppermute | solution.py:399
  3.2 3.5 %collective-permute-start.1 = (s32[1,512]{1,0:T(1,128)}, s32[1,512]{1,0:T(1,128)S(1)}, u32[]{:S(2)}, u32[]{:S(2)}) collective-permute-start(s32[1,512]{1,0:T(1,128)} %bitcast.13), channel_id=1, source_target_pairs={{0,4},{1,5},{2,6},{3,7},{4,0},{5,1},{6,2},{7,3},{8,12},{9,13},{10,... | collective-permute-start | bytes 6152 | tf_op jit(solution)/shard_map/ppermute | solution.py:399
  3.2 3.5 %collective-permute-start.2 = (s32[1,512]{1,0:T(1,128)}, s32[1,512]{1,0:T(1,128)S(1)}, u32[]{:S(2)}, u32[]{:S(2)}) collective-permute-start(s32[1,512]{1,0:T(1,128)} %bitcast.15), channel_id=1, source_target_pairs={{0,4},{1,5},{2,6},{3,7},{4,0},{5,1},{6,2},{7,3},{8,12},{9,13},{10,... | collective-permute-start | bytes 6152 | tf_op jit(solution)/shard_map/ppermute | solution.py:399
  57.9 27.4 %collective-permute-start.5 = (bf16[32,216,128]{2,1,0:T(8,128)(2,1)S(1)}, bf16[32,216,128]{2,1,0:T(8,128)(2,1)S(1)}, u32[]{:S(2)}, u32[]{:S(2)}) collective-permute-start(bf16[32,216,128]{2,1,0:T(8,128)(2,1)S(1)} %all_to_all.15.main), channel_id=1, source_target_pairs={{0,1},{1,2},{2,3},{3,0},{4,68},{5,69},{6,70},{7,71},{8,9},{9,10},{... | collective-permute-start | bytes 5308424 | tf_op jit(solution)/shard_map/ppermute | solution.py:399
  60.0 25.3 %collective-permute-start.3 = (bf16[32,216,128]{2,1,0:T(8,128)(2,1)S(1)}, bf16[32,216,128]{2,1,0:T(8,128)(2,1)S(1)}, u32[]{:S(2)}, u32[]{:S(2)}) collective-permute-start(bf16[32,216,128]{2,1,0:T(8,128)(2,1)S(1)} %all_to_all.15.main), channel_id=1, source_target_pairs={{0,3},{1,0},{2,1},{3,2},{4,196},{5,197},{6,198},{7,199},{8,11},{9,... | collective-permute-start | bytes 5308424 | tf_op jit(solution)/shard_map/ppermute | solution.py:399
  80.9 8.1 %collective-permute-start.6 = (bf16[32,48,128]{2,1,0:T(8,128)(2,1)S(1)}, bf16[32,48,128]{2,1,0:T(8,128)(2,1)S(1)}, u32[]{:S(2)}, u32[]{:S(2)}) collective-permute-start(bf16[32,48,128]{2,1,0:T(8,128)(2,1)S(1)} %all_to_all.16.last), channel_id=1, source_target_pairs={{0,1},{1,2},{2,3},{3,0},{4,68},{5,69},{6,70},{7,71},{8,9},{9,10},{... | collective-permute-start | bytes 1179656 | tf_op jit(solution)/shard_map/ppermute | solution.py:399
  80.9 8.1 %collective-permute-start.4 = (bf16[32,48,128]{2,1,0:T(8,128)(2,1)S(1)}, bf16[32,48,128]{2,1,0:T(8,128)(2,1)S(1)}, u32[]{:S(2)}, u32[]{:S(2)}) collective-permute-start(bf16[32,48,128]{2,1,0:T(8,128)(2,1)S(1)} %all_to_all.16.last), channel_id=1, source_target_pairs={{0,3},{1,0},{2,1},{3,2},{4,196},{5,197},{6,198},{7,199},{8,11},{9,... | collective-permute-start | bytes 1179656 | tf_op jit(solution)/shard_map/ppermute | solution.py:399

commit v9 on v8

--- a/solution.py
+++ b/solution.py
@@ -116,9 +116,9 @@
         copy.wait()
     placed, ids, within = put_rows(groups, 0, spot_ref, *held)
     teams, count, _ = half_ref.shape
-    for start in range(0, count // capacity * lanes, wide):
-        values = placed(start, wide)
-        for shift in range(0, wide, lanes):
+    for start in range(0, count // capacity * lanes, 4 * wide):
+        values = placed(start, 4 * wide)
+        for shift in range(0, 4 * wide, lanes):
             at = (start + shift) // lanes * capacity
             half_ref[:, at : at + capacity, :] = values[:, shift : shift + lanes].reshape(
                 teams, capacity, lanes
@@ -142,9 +142,9 @@
         else:
             last_ref[:, at - border : at - border + capacity, :] = values
 
-    for start in range(0, count // capacity * lanes, wide):
-        values = placed(start, wide)
-        for shift in range(0, wide, lanes):
+    for start in range(0, count // capacity * lanes, 4 * wide):
+        values = placed(start, 4 * wide)
+        for shift in range(0, 4 * wide, lanes):
             block = (start + shift) // lanes
             store(block * field, half_ref[:, block * capacity : (block + 1) * capacity, :])
             store(
@@ -206,7 +206,11 @@
     return lax.dot_general(left, right, contract_last, preferred_element_type=jnp.float32)
 
 
-def own_kernel(main, last, out_ref, hold):
+def own_kernel(main, last, plan_ref, out_ref, onehot_ref, pick_ref, hold):
+    team = lax.broadcasted_iota(jnp.int32, pick_ref.shape, 0)
+    onehot = (team == plan_ref[0:1, :]).astype(jnp.bfloat16)
+    onehot_ref[...] = jnp.concatenate([onehot] * 3, axis=0)
+    pick_ref[...] = jnp.where(team == plan_ref[1:2, :], 1.0, 0.0)
     ids = read_ids(main, hold)
     rows = ids.shape[0] * lanes
     blocks = range((first_rows + last.shape[1]) // field)
@@ -360,7 +364,7 @@
                     ]
 
 
-def fetch_kernel(spot_ref, back_ref, plan_ref, out_ref):
+def fetch_kernel(spot_ref, back_ref, onehot_ref, pick_ref, out_ref):
     x, y = spot_ref[2], spot_ref[3]
     each = places * depth
     across = cores * places
@@ -378,21 +382,17 @@
     odd = pltpu.roll(jnp.concatenate(odd, axis=0), capacity, 1)
     rest = jnp.where(lax.broadcasted_iota(jnp.int32, even.shape, 1) < capacity, even, odd)
     rest = jnp.where(lax.broadcasted_iota(jnp.int32, even.shape, 1) < field, rest, 0.0)
-    rows = plan_ref.shape[1]
-    team = lax.broadcasted_iota(jnp.int32, (places * depth, rows), 0)
-    onehot = (team == plan_ref[0:1, :]).astype(jnp.bfloat16)
     pieces = []
     for _ in range(3):
         pieces.append(rest.astype(jnp.bfloat16))
         rest = rest - pieces[-1].astype(jnp.float32)
     found = lax.dot_general(
         jnp.concatenate(pieces, axis=0),
-        jnp.concatenate([onehot] * 3, axis=0),
+        onehot_ref[...],
         (((0,), (0,)), ((), ())),
         preferred_element_type=jnp.float32,
     )[:field, :]
-    lane = lax.broadcasted_iota(jnp.int32, (field, rows), 0)
-    out_ref[...] = jnp.sum(jnp.where(lane == plan_ref[1:2, :], found, 0.0), axis=0, keepdims=True)
+    out_ref[...] = jnp.sum(jnp.where(pick_ref[...] > 0, found, 0.0), axis=0, keepdims=True)
 
 
 def send(values, route):
@@ -465,7 +465,14 @@
         before.append(send(got, beside(1)))
         after.append(send(got, beside(-1)))
     held = pltpu.VMEM((each, lanes), f32)
-    inside = call(own_kernel, array(blocks, lanes, dtype=f32), "own", *own, scratch=[held])
+    inside, onehot, pick = call(
+        own_kernel,
+        [array(blocks, lanes, dtype=f32), array(3 * each, rows), array(each, rows, dtype=f32)],
+        "own",
+        *own,
+        plan,
+        scratch=[held],
+    )
     near, side = call(
         start_kernel,
         [array(spots, spots, dtype=f32), array(spots // 2, spots, dtype=f32)],
@@ -493,7 +500,7 @@
     back = lax.all_to_all(
         best.reshape(count, 1, 1, lanes), everyone, split_axis=0, concat_axis=0, tiled=True
     ).reshape(count, lanes)
-    result = call(fetch_kernel, array(1, rows, dtype=f32), "fetch", spot, back, plan)
+    result = call(fetch_kernel, array(1, rows, dtype=f32), "fetch", spot, back, onehot, pick)
     return result.reshape(rows)
 
 

time: 117 us -> 117 us (level)
  no operation moved by 1% of the time
where the time goes in v9:
time: 117 us
  blocking collectives  92.7 us (79%)
  Pallas kernels  13 us (11%)
  starting transfers between devices  10.6 us (9%)
    all_to_all x2, blocking collectives, trade(): lax.all_to_all(values, everyone, split_axis=0, concat_axis=0, axis_index_...  68.4 us
    all_to_all x1, blocking collectives, shards(): lax.all_to_all(best.reshape(count, 1, 1, lanes), everyone, split_axis=0,...  24.3 us
    ppermute x7, starting transfers between devices, send(): return lax.ppermute(values, everyone, route)  10.6 us
    pallas_call x5, Pallas kernels, call(): pl.pallas_call(kernel, out_shape=out_shape, in_specs=[smem if a is spot e...  10.2 us
    pallas_call x1, Pallas kernels, shards(): pl.pallas_call(functools.partial(place_kernel, groups), out_shape=[array(...  2.85 us
  transfers between devices with their start and end apart: 7, of which 1 were waited for; matrix products, arithmetic and copies ran while one was open for 0% of the time, Pallas kernels for 7%

profile of v9, /device:TPU:1, one launch (start us, length us, event | category | flops | bytes accessed | tf_op | source)
XLA Modules:
  0.0 116.9 jit_solution(6617314894481815369)
XLA Ops:
  0.0 3.2 %collective-permute-start = (bf16[512,1024]{1,0:T(8,128)(2,1)}, bf16[512,1024]{1,0:T(8,128)(2,1)S(1)}, u32[]{:S(2)}, u32[]{:S(2)}) collective-permute-start(bf16[512,1024]{1,0:T(8,128)(2,1)} %refs_0_.1), channel_id=1, source_target_pairs={{0,4},{1,5},{2,6},{3,7},{4,0},{5,1},{6,2},{7,3},{8,12},{9,13},{10,... | collective-permute-start | bytes 3145736 | tf_op jit(solution)/shard_map/ppermute | solution.py:399
  3.2 0.0 collective-permute-start.1
  3.2 0.5 collective-permute-start.2
  3.8 0.1 pad_add_fusion.spot_ref
  3.8 2.9 %place.1 = (bf16[32,128,128]{2,1,0:T(8,128)(2,1)S(1)}, f32[32,128]{1,0:T(8,128)S(1)}, s32[2,512]{1,0:T(2,128)S(1)}) custom-call(s32[4]{0:T(128)S(1)} %pad_add_fusion.spot_ref, bf16[512,1024]{1,0:T(8,128)(2,1)} %refs_0_.1, s32[1,512]{1,0:T(1,128)} %bitcast.14, s32[1,512]{1,0:T(1,128)} %bitcast.16), custom_call_target="tpu_custom_call" | custom-call | tf_op jit(solution)/shard_map/place/pallas_call | solution.py:438
  6.7 0.0 collective-permute-done.1.owner_ref
  6.7 0.0 collective-permute-done.2.cluster_ref
  6.7 0.0 collective-permute-done.emb_ref
  6.7 1.6 %pair.1 = (bf16[32,216,128]{2,1,0:T(8,128)(2,1)S(1)}, bf16[32,48,128]{2,1,0:T(8,128)(2,1)S(1)}) custom-call(s32[4]{0:T(128)S(1)} %pad_add_fusion.spot_ref, bf16[512,1024]{1,0:T(8,128)(2,1)S(1)} %collective-permute-done.emb_ref, s32[1,512]{1,0:T(1,128)S(1)} %collective-permute-done.1.owner_ref, s32[1,512]{1,0:T(1,128)S(1)} %collective-permute-done.2.cluster_ref, ...), custom_call_target="tpu_custom_call" | custom-call | tf_op jit(solution)/shard_map/pair/pallas_call | solution.py:422
  8.4 49.5 %all_to_all.15.main = bf16[32,216,128]{2,1,0:T(8,128)(2,1)S(1)} all-to-all(bf16[32,216,128]{2,1,0:T(8,128)(2,1)S(1)} %get-tuple-element.17), channel_id=1, replica_groups={{0,8,16,24,32,40,48,56,64,72,80,88,96,104,112,120,128,136,144,152,160,1..., dimensions={0} | all-to-all | bytes 3538944 | tf_op jit(solution)/shard_map/all_to_all | solution.py:403
  57.9 2.1 %collective-permute-start.5 = (bf16[32,216,128]{2,1,0:T(8,128)(2,1)S(1)}, bf16[32,216,128]{2,1,0:T(8,128)(2,1)S(1)}, u32[]{:S(2)}, u32[]{:S(2)}) collective-permute-start(bf16[32,216,128]{2,1,0:T(8,128)(2,1)S(1)} %all_to_all.15.main), channel_id=1, source_target_pairs={{0,1},{1,2},{2,3},{3,0},{4,68},{5,69},{6,70},{7,71},{8,9},{9,10},{... | collective-permute-start | bytes 5308424 | tf_op jit(solution)/shard_map/ppermute | solution.py:399
  60.1 2.0 %collective-permute-start.3 = (bf16[32,216,128]{2,1,0:T(8,128)(2,1)S(1)}, bf16[32,216,128]{2,1,0:T(8,128)(2,1)S(1)}, u32[]{:S(2)}, u32[]{:S(2)}) collective-permute-start(bf16[32,216,128]{2,1,0:T(8,128)(2,1)S(1)} %all_to_all.15.main), channel_id=1, source_target_pairs={{0,3},{1,0},{2,1},{3,2},{4,196},{5,197},{6,198},{7,199},{8,11},{9,... | collective-permute-start | bytes 5308424 | tf_op jit(solution)/shard_map/ppermute | solution.py:399
  62.1 18.8 %all_to_all.16.last = bf16[32,48,128]{2,1,0:T(8,128)(2,1)S(1)} all-to-all(bf16[32,48,128]{2,1,0:T(8,128)(2,1)S(1)} %get-tuple-element.18), channel_id=1, replica_groups={{0,8,16,24,32,40,48,56,64,72,80,88,96,104,112,120,128,136,144,152,160,1..., dimensions={0} | all-to-all | bytes 786432 | tf_op jit(solution)/shard_map/all_to_all | solution.py:403
  80.9 0.0 collective-permute-start.6
  80.9 2.7 %collective-permute-start.4 = (bf16[32,48,128]{2,1,0:T(8,128)(2,1)S(1)}, bf16[32,48,128]{2,1,0:T(8,128)(2,1)S(1)}, u32[]{:S(2)}, u32[]{:S(2)}) collective-permute-start(bf16[32,48,128]{2,1,0:T(8,128)(2,1)S(1)} %all_to_all.16.last), channel_id=1, source_target_pairs={{0,3},{1,0},{2,1},{3,2},{4,196},{5,197},{6,198},{7,199},{8,11},{9,... | collective-permute-start | bytes 1179656 | tf_op jit(solution)/shard_map/ppermute | solution.py:399
  83.6 1.7 %own.1 = (f32[8,128]{1,0:T(8,128)S(1)}, bf16[96,512]{1,0:T(8,128)(2,1)S(1)}, f32[32,512]{1,0:T(8,128)S(1)}) custom-call(bf16[32,216,128]{2,1,0:T(8,128)(2,1)S(1)} %all_to_all.15.main, bf16[32,48,128]{2,1,0:T(8,128)(2,1)S(1)} %all_to_all.16.last, s32[2,512]{1,0:T(2,128)S(1)} %get-tuple-element.21.plan_ref), custom_call_target="tpu_custom_call" | custom-call | tf_op jit(solution)/shard_map/own/pallas_call | solution.py:422
  85.3 0.0 collective-permute-done.5.before.before_main
  85.3 0.0 collective-permute-done.3.after.after_main
  85.3 3.3 %start.1 = (f32[1024,1024]{1,0:T(8,128)S(1)}, f32[512,1024]{1,0:T(8,128)S(1)}) custom-call(s32[4]{0:T(128)S(1)} %pad_add_fusion.spot_ref, bf16[32,216,128]{2,1,0:T(8,128)(2,1)S(1)} %all_to_all.15.main, bf16[32,216,128]{2,1,0:T(8,128)(2,1)S(1)} %collective-permute-done.3.after.after_main, bf16[32,216,128]{2,1,0:T(8,128)(2,1)S(1)} %collective-permute-done.5.before.before_main), custom_call_target="tpu_custom_call" | custom-call | tf_op jit(solution)/shard_map/start/pallas_call | solution.py:422
  88.6 0.4 collective-permute-done.6.before_last
  89.0 0.0 collective-permute-done.4.after_last
  89.0 2.1 %cross.1 = f32[256,128]{1,0:T(8,128)S(1)} custom-call(s32[4]{0:T(128)S(1)} %pad_add_fusion.spot_ref, bf16[32,216,128]{2,1,0:T(8,128)(2,1)S(1)} %all_to_all.15.main, bf16[32,48,128]{2,1,0:T(8,128)(2,1)S(1)} %all_to_all.16.last, bf16[32,216,128]{2,1,0:T(8,128)(2,1)S(1)} %collective-permute-done.3.after.after_main, ...), custom_call_target="tpu_custom_call" | custom-call | tf_op jit(solution)/shard_map/cross/pallas_call | solution.py:422
  91.2 24.3 %all_to_all.17 = f32[256,1,1,128]{3,2,1,0:T(1,128)S(1)} all-to-all(f32[256,1,1,128]{3,2,1,0:T(1,128)S(1)} %bitcast.11), channel_id=1, replica_groups=mesh['ingest'=64,'span'=4] {'ingest','span'}, dimensions={0} | all-to-all | bytes 262144 | tf_op jit(solution)/shard_map/all_to_all | solution.py:500
  115.5 1.4 %fetch.1 = f32[1,512]{1,0:T(1,128)} custom-call(s32[4]{0:T(128)S(1)} %pad_add_fusion.spot_ref, f32[256,128]{1,0:T(8,128)S(1)} %bitcast.12, bf16[96,512]{1,0:T(8,128)(2,1)S(1)} %get-tuple-element.23.onehot_ref, f32[32,512]{1,0:T(8,128)S(1)} %get-tuple-element.24.pick_ref), custom_call_target="tpu_custom_call" | custom-call | tf_op jit(solution)/shard_map/fetch/pallas_call | solution.py:422
Async XLA Ops:
  0.0 6.7 %collective-permute-start = (bf16[512,1024]{1,0:T(8,128)(2,1)}, bf16[512,1024]{1,0:T(8,128)(2,1)S(1)}, u32[]{:S(2)}, u32[]{:S(2)}) collective-permute-start(bf16[512,1024]{1,0:T(8,128)(2,1)} %refs_0_.1), channel_id=1, source_target_pairs={{0,4},{1,5},{2,6},{3,7},{4,0},{5,1},{6,2},{7,3},{8,12},{9,13},{10,... | collective-permute-start | bytes 3145736 | tf_op jit(solution)/shard_map/ppermute | solution.py:399
  3.2 3.5 %collective-permute-start.1 = (s32[1,512]{1,0:T(1,128)}, s32[1,512]{1,0:T(1,128)S(1)}, u32[]{:S(2)}, u32[]{:S(2)}) collective-permute-start(s32[1,512]{1,0:T(1,128)} %bitcast.13), channel_id=1, source_target_pairs={{0,4},{1,5},{2,6},{3,7},{4,0},{5,1},{6,2},{7,3},{8,12},{9,13},{10,... | collective-permute-start | bytes 6152 | tf_op jit(solution)/shard_map/ppermute | solution.py:399
  3.2 3.5 %collective-permute-start.2 = (s32[1,512]{1,0:T(1,128)}, s32[1,512]{1,0:T(1,128)S(1)}, u32[]{:S(2)}, u32[]{:S(2)}) collective-permute-start(s32[1,512]{1,0:T(1,128)} %bitcast.15), channel_id=1, source_target_pairs={{0,4},{1,5},{2,6},{3,7},{4,0},{5,1},{6,2},{7,3},{8,12},{9,13},{10,... | collective-permute-start | bytes 6152 | tf_op jit(solution)/shard_map/ppermute | solution.py:399
  57.9 27.3 %collective-permute-start.5 = (bf16[32,216,128]{2,1,0:T(8,128)(2,1)S(1)}, bf16[32,216,128]{2,1,0:T(8,128)(2,1)S(1)}, u32[]{:S(2)}, u32[]{:S(2)}) collective-permute-start(bf16[32,216,128]{2,1,0:T(8,128)(2,1)S(1)} %all_to_all.15.main), channel_id=1, source_target_pairs={{0,1},{1,2},{2,3},{3,0},{4,68},{5,69},{6,70},{7,71},{8,9},{9,10},{... | collective-permute-start | bytes 5308424 | tf_op jit(solution)/shard_map/ppermute | solution.py:399
  60.1 25.2 %collective-permute-start.3 = (bf16[32,216,128]{2,1,0:T(8,128)(2,1)S(1)}, bf16[32,216,128]{2,1,0:T(8,128)(2,1)S(1)}, u32[]{:S(2)}, u32[]{:S(2)}) collective-permute-start(bf16[32,216,128]{2,1,0:T(8,128)(2,1)S(1)} %all_to_all.15.main), channel_id=1, source_target_pairs={{0,3},{1,0},{2,1},{3,2},{4,196},{5,197},{6,198},{7,199},{8,11},{9,... | collective-permute-start | bytes 5308424 | tf_op jit(solution)/shard_map/ppermute | solution.py:399
  80.9 8.1 %collective-permute-start.6 = (bf16[32,48,128]{2,1,0:T(8,128)(2,1)S(1)}, bf16[32,48,128]{2,1,0:T(8,128)(2,1)S(1)}, u32[]{:S(2)}, u32[]{:S(2)}) collective-permute-start(bf16[32,48,128]{2,1,0:T(8,128)(2,1)S(1)} %all_to_all.16.last), channel_id=1, source_target_pairs={{0,1},{1,2},{2,3},{3,0},{4,68},{5,69},{6,70},{7,71},{8,9},{9,10},{... | collective-permute-start | bytes 1179656 | tf_op jit(solution)/shard_map/ppermute | solution.py:399
  80.9 8.1 %collective-permute-start.4 = (bf16[32,48,128]{2,1,0:T(8,128)(2,1)S(1)}, bf16[32,48,128]{2,1,0:T(8,128)(2,1)S(1)}, u32[]{:S(2)}, u32[]{:S(2)}) collective-permute-start(bf16[32,48,128]{2,1,0:T(8,128)(2,1)S(1)} %all_to_all.16.last), channel_id=1, source_target_pairs={{0,3},{1,0},{2,1},{3,2},{4,196},{5,197},{6,198},{7,199},{8,11},{9,... | collective-permute-start | bytes 1179656 | tf_op jit(solution)/shard_map/ppermute | solution.py:399

commit v10 on v9

--- a/solution.py
+++ b/solution.py
@@ -10,7 +10,7 @@
 epsilon = 1e-06
 capacity = 16
 lanes = 128
-wide = 256
+wide = 512
 cores = 2
 places = 4
 depth = 8
@@ -116,9 +116,9 @@
         copy.wait()
     placed, ids, within = put_rows(groups, 0, spot_ref, *held)
     teams, count, _ = half_ref.shape
-    for start in range(0, count // capacity * lanes, 4 * wide):
-        values = placed(start, 4 * wide)
-        for shift in range(0, 4 * wide, lanes):
+    for start in range(0, count // capacity * lanes, 2 * wide):
+        values = placed(start, 2 * wide)
+        for shift in range(0, 2 * wide, lanes):
             at = (start + shift) // lanes * capacity
             half_ref[:, at : at + capacity, :] = values[:, shift : shift + lanes].reshape(
                 teams, capacity, lanes
@@ -142,9 +142,9 @@
         else:
             last_ref[:, at - border : at - border + capacity, :] = values
 
-    for start in range(0, count // capacity * lanes, 4 * wide):
-        values = placed(start, 4 * wide)
-        for shift in range(0, 4 * wide, lanes):
+    for start in range(0, count // capacity * lanes, 2 * wide):
+        values = placed(start, 2 * wide)
+        for shift in range(0, 2 * wide, lanes):
             block = (start + shift) // lanes
             store(block * field, half_ref[:, block * capacity : (block + 1) * capacity, :])
             store(
@@ -230,7 +230,7 @@
             same = columns[begin:, :] == jnp.where(row_ids < 0, -2.0, row_ids)
             masked.append(jnp.where(same & (row - column != h * lanes), scores, -1.0))
             tops.append(jnp.max(masked[-1], axis=0, keepdims=True))
-        both = jnp.maximum(masked[0], masked[1])
+        both = functools.reduce(jnp.maximum, masked)
         for i in range(at, steps):
             part = both[i * wide - begin : (i + 1) * wide - begin, :]
             best[i] = part if best[i] is None else jnp.maximum(best[i], part)

time: 117 us -> 117 us (level)
  no operation moved by 1% of the time
where the time goes in v10:
time: 117 us
  blocking collectives  92.7 us (79%)
  Pallas kernels  12.9 us (11%)
  starting transfers between devices  10.6 us (9%)
    all_to_all x2, blocking collectives, trade(): lax.all_to_all(values, everyone, split_axis=0, concat_axis=0, axis_index_...  68.4 us
    all_to_all x1, blocking collectives, shards(): lax.all_to_all(best.reshape(count, 1, 1, lanes), everyone, split_axis=0,...  24.3 us
    ppermute x7, starting transfers between devices, send(): return lax.ppermute(values, everyone, route)  10.6 us
    pallas_call x5, Pallas kernels, call(): pl.pallas_call(kernel, out_shape=out_shape, in_specs=[smem if a is spot e...  10.1 us
    pallas_call x1, Pallas kernels, shards(): pl.pallas_call(functools.partial(place_kernel, groups), out_shape=[array(...  2.85 us
  transfers between devices with their start and end apart: 7, of which 1 were waited for; matrix products, arithmetic and copies ran while one was open for 0% of the time, Pallas kernels for 7%

profile of v10, /device:TPU:1, one launch (start us, length us, event | category | flops | bytes accessed | tf_op | source)
XLA Modules:
  0.0 116.6 jit_solution(11401224743268541346)
XLA Ops:
  0.0 3.2 %collective-permute-start = (bf16[512,1024]{1,0:T(8,128)(2,1)}, bf16[512,1024]{1,0:T(8,128)(2,1)S(1)}, u32[]{:S(2)}, u32[]{:S(2)}) collective-permute-start(bf16[512,1024]{1,0:T(8,128)(2,1)} %refs_0_.1), channel_id=1, source_target_pairs={{0,4},{1,5},{2,6},{3,7},{4,0},{5,1},{6,2},{7,3},{8,12},{9,13},{10,... | collective-permute-start | bytes 3145736 | tf_op jit(solution)/shard_map/ppermute | solution.py:399
  3.2 0.0 collective-permute-start.1
  3.2 0.5 collective-permute-start.2
  3.8 0.1 pad_add_fusion.spot_ref
  3.8 2.9 %place.1 = (bf16[32,128,128]{2,1,0:T(8,128)(2,1)S(1)}, f32[32,128]{1,0:T(8,128)S(1)}, s32[2,512]{1,0:T(2,128)S(1)}) custom-call(s32[4]{0:T(128)S(1)} %pad_add_fusion.spot_ref, bf16[512,1024]{1,0:T(8,128)(2,1)} %refs_0_.1, s32[1,512]{1,0:T(1,128)} %bitcast.14, s32[1,512]{1,0:T(1,128)} %bitcast.16), custom_call_target="tpu_custom_call" | custom-call | tf_op jit(solution)/shard_map/place/pallas_call | solution.py:438
  6.7 0.0 collective-permute-done.1.owner_ref
  6.7 0.0 collective-permute-done.2.cluster_ref
  6.7 0.0 collective-permute-done.emb_ref
  6.7 1.6 %pair.1 = (bf16[32,216,128]{2,1,0:T(8,128)(2,1)S(1)}, bf16[32,48,128]{2,1,0:T(8,128)(2,1)S(1)}) custom-call(s32[4]{0:T(128)S(1)} %pad_add_fusion.spot_ref, bf16[512,1024]{1,0:T(8,128)(2,1)S(1)} %collective-permute-done.emb_ref, s32[1,512]{1,0:T(1,128)S(1)} %collective-permute-done.1.owner_ref, s32[1,512]{1,0:T(1,128)S(1)} %collective-permute-done.2.cluster_ref, ...), custom_call_target="tpu_custom_call" | custom-call | tf_op jit(solution)/shard_map/pair/pallas_call | solution.py:422
  8.4 49.5 %all_to_all.15.main = bf16[32,216,128]{2,1,0:T(8,128)(2,1)S(1)} all-to-all(bf16[32,216,128]{2,1,0:T(8,128)(2,1)S(1)} %get-tuple-element.17), channel_id=1, replica_groups={{0,8,16,24,32,40,48,56,64,72,80,88,96,104,112,120,128,136,144,152,160,1..., dimensions={0} | all-to-all | bytes 3538944 | tf_op jit(solution)/shard_map/all_to_all | solution.py:403
  57.9 2.1 %collective-permute-start.5 = (bf16[32,216,128]{2,1,0:T(8,128)(2,1)S(1)}, bf16[32,216,128]{2,1,0:T(8,128)(2,1)S(1)}, u32[]{:S(2)}, u32[]{:S(2)}) collective-permute-start(bf16[32,216,128]{2,1,0:T(8,128)(2,1)S(1)} %all_to_all.15.main), channel_id=1, source_target_pairs={{0,1},{1,2},{2,3},{3,0},{4,68},{5,69},{6,70},{7,71},{8,9},{9,10},{... | collective-permute-start | bytes 5308424 | tf_op jit(solution)/shard_map/ppermute | solution.py:399
  60.1 2.0 %collective-permute-start.3 = (bf16[32,216,128]{2,1,0:T(8,128)(2,1)S(1)}, bf16[32,216,128]{2,1,0:T(8,128)(2,1)S(1)}, u32[]{:S(2)}, u32[]{:S(2)}) collective-permute-start(bf16[32,216,128]{2,1,0:T(8,128)(2,1)S(1)} %all_to_all.15.main), channel_id=1, source_target_pairs={{0,3},{1,0},{2,1},{3,2},{4,196},{5,197},{6,198},{7,199},{8,11},{9,... | collective-permute-start | bytes 5308424 | tf_op jit(solution)/shard_map/ppermute | solution.py:399
  62.1 18.8 %all_to_all.16.last = bf16[32,48,128]{2,1,0:T(8,128)(2,1)S(1)} all-to-all(bf16[32,48,128]{2,1,0:T(8,128)(2,1)S(1)} %get-tuple-element.18), channel_id=1, replica_groups={{0,8,16,24,32,40,48,56,64,72,80,88,96,104,112,120,128,136,144,152,160,1..., dimensions={0} | all-to-all | bytes 786432 | tf_op jit(solution)/shard_map/all_to_all | solution.py:403
  80.9 0.0 collective-permute-start.6
  80.9 2.7 %collective-permute-start.4 = (bf16[32,48,128]{2,1,0:T(8,128)(2,1)S(1)}, bf16[32,48,128]{2,1,0:T(8,128)(2,1)S(1)}, u32[]{:S(2)}, u32[]{:S(2)}) collective-permute-start(bf16[32,48,128]{2,1,0:T(8,128)(2,1)S(1)} %all_to_all.16.last), channel_id=1, source_target_pairs={{0,3},{1,0},{2,1},{3,2},{4,196},{5,197},{6,198},{7,199},{8,11},{9,... | collective-permute-start | bytes 1179656 | tf_op jit(solution)/shard_map/ppermute | solution.py:399
  83.6 2.0 %own.1 = (f32[8,128]{1,0:T(8,128)S(1)}, bf16[96,512]{1,0:T(8,128)(2,1)S(1)}, f32[32,512]{1,0:T(8,128)S(1)}) custom-call(bf16[32,216,128]{2,1,0:T(8,128)(2,1)S(1)} %all_to_all.15.main, bf16[32,48,128]{2,1,0:T(8,128)(2,1)S(1)} %all_to_all.16.last, s32[2,512]{1,0:T(2,128)S(1)} %get-tuple-element.21.plan_ref), custom_call_target="tpu_custom_call" | custom-call | tf_op jit(solution)/shard_map/own/pallas_call | solution.py:422
  85.5 0.0 collective-permute-done.5.before.before_main
  85.6 0.0 collective-permute-done.3.after.after_main
  85.6 3.2 %start.1 = (f32[1024,1024]{1,0:T(8,128)S(1)}, f32[512,1024]{1,0:T(8,128)S(1)}) custom-call(s32[4]{0:T(128)S(1)} %pad_add_fusion.spot_ref, bf16[32,216,128]{2,1,0:T(8,128)(2,1)S(1)} %all_to_all.15.main, bf16[32,216,128]{2,1,0:T(8,128)(2,1)S(1)} %collective-permute-done.3.after.after_main, bf16[32,216,128]{2,1,0:T(8,128)(2,1)S(1)} %collective-permute-done.5.before.before_main), custom_call_target="tpu_custom_call" | custom-call | tf_op jit(solution)/shard_map/start/pallas_call | solution.py:422
  88.8 0.3 collective-permute-done.6.before_last
  89.0 0.0 collective-permute-done.4.after_last
  89.1 1.9 %cross.1 = f32[256,128]{1,0:T(8,128)S(1)} custom-call(s32[4]{0:T(128)S(1)} %pad_add_fusion.spot_ref, bf16[32,216,128]{2,1,0:T(8,128)(2,1)S(1)} %all_to_all.15.main, bf16[32,48,128]{2,1,0:T(8,128)(2,1)S(1)} %all_to_all.16.last, bf16[32,216,128]{2,1,0:T(8,128)(2,1)S(1)} %collective-permute-done.3.after.after_main, ...), custom_call_target="tpu_custom_call" | custom-call | tf_op jit(solution)/shard_map/cross/pallas_call | solution.py:422
  90.9 24.3 %all_to_all.17 = f32[256,1,1,128]{3,2,1,0:T(1,128)S(1)} all-to-all(f32[256,1,1,128]{3,2,1,0:T(1,128)S(1)} %bitcast.11), channel_id=1, replica_groups=mesh['ingest'=64,'span'=4] {'ingest','span'}, dimensions={0} | all-to-all | bytes 262144 | tf_op jit(solution)/shard_map/all_to_all | solution.py:500
  115.2 1.4 %fetch.1 = f32[1,512]{1,0:T(1,128)} custom-call(s32[4]{0:T(128)S(1)} %pad_add_fusion.spot_ref, f32[256,128]{1,0:T(8,128)S(1)} %bitcast.12, bf16[96,512]{1,0:T(8,128)(2,1)S(1)} %get-tuple-element.23.onehot_ref, f32[32,512]{1,0:T(8,128)S(1)} %get-tuple-element.24.pick_ref), custom_call_target="tpu_custom_call" | custom-call | tf_op jit(solution)/shard_map/fetch/pallas_call | solution.py:422
Async XLA Ops:
  0.0 6.7 %collective-permute-start = (bf16[512,1024]{1,0:T(8,128)(2,1)}, bf16[512,1024]{1,0:T(8,128)(2,1)S(1)}, u32[]{:S(2)}, u32[]{:S(2)}) collective-permute-start(bf16[512,1024]{1,0:T(8,128)(2,1)} %refs_0_.1), channel_id=1, source_target_pairs={{0,4},{1,5},{2,6},{3,7},{4,0},{5,1},{6,2},{7,3},{8,12},{9,13},{10,... | collective-permute-start | bytes 3145736 | tf_op jit(solution)/shard_map/ppermute | solution.py:399
  3.2 3.5 %collective-permute-start.1 = (s32[1,512]{1,0:T(1,128)}, s32[1,512]{1,0:T(1,128)S(1)}, u32[]{:S(2)}, u32[]{:S(2)}) collective-permute-start(s32[1,512]{1,0:T(1,128)} %bitcast.13), channel_id=1, source_target_pairs={{0,4},{1,5},{2,6},{3,7},{4,0},{5,1},{6,2},{7,3},{8,12},{9,13},{10,... | collective-permute-start | bytes 6152 | tf_op jit(solution)/shard_map/ppermute | solution.py:399
  3.2 3.5 %collective-permute-start.2 = (s32[1,512]{1,0:T(1,128)}, s32[1,512]{1,0:T(1,128)S(1)}, u32[]{:S(2)}, u32[]{:S(2)}) collective-permute-start(s32[1,512]{1,0:T(1,128)} %bitcast.15), channel_id=1, source_target_pairs={{0,4},{1,5},{2,6},{3,7},{4,0},{5,1},{6,2},{7,3},{8,12},{9,13},{10,... | collective-permute-start | bytes 6152 | tf_op jit(solution)/shard_map/ppermute | solution.py:399
  57.9 27.6 %collective-permute-start.5 = (bf16[32,216,128]{2,1,0:T(8,128)(2,1)S(1)}, bf16[32,216,128]{2,1,0:T(8,128)(2,1)S(1)}, u32[]{:S(2)}, u32[]{:S(2)}) collective-permute-start(bf16[32,216,128]{2,1,0:T(8,128)(2,1)S(1)} %all_to_all.15.main), channel_id=1, source_target_pairs={{0,1},{1,2},{2,3},{3,0},{4,68},{5,69},{6,70},{7,71},{8,9},{9,10},{... | collective-permute-start | bytes 5308424 | tf_op jit(solution)/shard_map/ppermute | solution.py:399
  60.1 25.5 %collective-permute-start.3 = (bf16[32,216,128]{2,1,0:T(8,128)(2,1)S(1)}, bf16[32,216,128]{2,1,0:T(8,128)(2,1)S(1)}, u32[]{:S(2)}, u32[]{:S(2)}) collective-permute-start(bf16[32,216,128]{2,1,0:T(8,128)(2,1)S(1)} %all_to_all.15.main), channel_id=1, source_target_pairs={{0,3},{1,0},{2,1},{3,2},{4,196},{5,197},{6,198},{7,199},{8,11},{9,... | collective-permute-start | bytes 5308424 | tf_op jit(solution)/shard_map/ppermute | solution.py:399
  80.9 8.1 %collective-permute-start.6 = (bf16[32,48,128]{2,1,0:T(8,128)(2,1)S(1)}, bf16[32,48,128]{2,1,0:T(8,128)(2,1)S(1)}, u32[]{:S(2)}, u32[]{:S(2)}) collective-permute-start(bf16[32,48,128]{2,1,0:T(8,128)(2,1)S(1)} %all_to_all.16.last), channel_id=1, source_target_pairs={{0,1},{1,2},{2,3},{3,0},{4,68},{5,69},{6,70},{7,71},{8,9},{9,10},{... | collective-permute-start | bytes 1179656 | tf_op jit(solution)/shard_map/ppermute | solution.py:399
  80.9 8.1 %collective-permute-start.4 = (bf16[32,48,128]{2,1,0:T(8,128)(2,1)S(1)}, bf16[32,48,128]{2,1,0:T(8,128)(2,1)S(1)}, u32[]{:S(2)}, u32[]{:S(2)}) collective-permute-start(bf16[32,48,128]{2,1,0:T(8,128)(2,1)S(1)} %all_to_all.16.last), channel_id=1, source_target_pairs={{0,3},{1,0},{2,1},{3,2},{4,196},{5,197},{6,198},{7,199},{8,11},{9,... | collective-permute-start | bytes 1179656 | tf_op jit(solution)/shard_map/ppermute | solution.py:399

commit v11 on v9

--- a/solution.py
+++ b/solution.py
@@ -462,8 +462,8 @@
     for part in parts:
         got = trade(part, teams)
         own.append(got)
+        after.append(send(got, beside(-1)))
         before.append(send(got, beside(1)))
-        after.append(send(got, beside(-1)))
     held = pltpu.VMEM((each, lanes), f32)
     inside, onehot, pick = call(
         own_kernel,

time: 117 us -> 117 us (level)
  no operation moved by 1% of the time
where the time goes in v11:
time: 117 us
  blocking collectives  92.7 us (79%)
  Pallas kernels  13 us (11%)
  starting transfers between devices  10.6 us (9%)
    all_to_all x2, blocking collectives, trade(): lax.all_to_all(values, everyone, split_axis=0, concat_axis=0, axis_index_...  68.4 us
    all_to_all x1, blocking collectives, shards(): lax.all_to_all(best.reshape(count, 1, 1, lanes), everyone, split_axis=0,...  24.3 us
    ppermute x7, starting transfers between devices, send(): return lax.ppermute(values, everyone, route)  10.6 us
    pallas_call x5, Pallas kernels, call(): pl.pallas_call(kernel, out_shape=out_shape, in_specs=[smem if a is spot e...  10.2 us
    pallas_call x1, Pallas kernels, shards(): pl.pallas_call(functools.partial(place_kernel, groups), out_shape=[array(...  2.85 us
  transfers between devices with their start and end apart: 7, of which 1 were waited for; matrix products, arithmetic and copies ran while one was open for 0% of the time, Pallas kernels for 7%

profile of v11, /device:TPU:1, one launch (start us, length us, event | category | flops | bytes accessed | tf_op | source)
XLA Modules:
  0.0 116.9 jit_solution(6617314894481815369)
XLA Ops:
  0.0 3.2 %collective-permute-start = (bf16[512,1024]{1,0:T(8,128)(2,1)}, bf16[512,1024]{1,0:T(8,128)(2,1)S(1)}, u32[]{:S(2)}, u32[]{:S(2)}) collective-permute-start(bf16[512,1024]{1,0:T(8,128)(2,1)} %refs_0_.1), channel_id=1, source_target_pairs={{0,4},{1,5},{2,6},{3,7},{4,0},{5,1},{6,2},{7,3},{8,12},{9,13},{10,... | collective-permute-start | bytes 3145736 | tf_op jit(solution)/shard_map/ppermute | solution.py:399
  3.2 0.0 collective-permute-start.1
  3.2 0.5 collective-permute-start.2
  3.8 0.1 pad_add_fusion.spot_ref
  3.8 2.9 %place.1 = (bf16[32,128,128]{2,1,0:T(8,128)(2,1)S(1)}, f32[32,128]{1,0:T(8,128)S(1)}, s32[2,512]{1,0:T(2,128)S(1)}) custom-call(s32[4]{0:T(128)S(1)} %pad_add_fusion.spot_ref, bf16[512,1024]{1,0:T(8,128)(2,1)} %refs_0_.1, s32[1,512]{1,0:T(1,128)} %bitcast.14, s32[1,512]{1,0:T(1,128)} %bitcast.16), custom_call_target="tpu_custom_call" | custom-call | tf_op jit(solution)/shard_map/place/pallas_call | solution.py:438
  6.7 0.0 collective-permute-done.1.owner_ref
  6.7 0.0 collective-permute-done.2.cluster_ref
  6.7 0.0 collective-permute-done.emb_ref
  6.7 1.6 %pair.1 = (bf16[32,216,128]{2,1,0:T(8,128)(2,1)S(1)}, bf16[32,48,128]{2,1,0:T(8,128)(2,1)S(1)}) custom-call(s32[4]{0:T(128)S(1)} %pad_add_fusion.spot_ref, bf16[512,1024]{1,0:T(8,128)(2,1)S(1)} %collective-permute-done.emb_ref, s32[1,512]{1,0:T(1,128)S(1)} %collective-permute-done.1.owner_ref, s32[1,512]{1,0:T(1,128)S(1)} %collective-permute-done.2.cluster_ref, ...), custom_call_target="tpu_custom_call" | custom-call | tf_op jit(solution)/shard_map/pair/pallas_call | solution.py:422
  8.4 49.5 %all_to_all.15.main = bf16[32,216,128]{2,1,0:T(8,128)(2,1)S(1)} all-to-all(bf16[32,216,128]{2,1,0:T(8,128)(2,1)S(1)} %get-tuple-element.17), channel_id=1, replica_groups={{0,8,16,24,32,40,48,56,64,72,80,88,96,104,112,120,128,136,144,152,160,1..., dimensions={0} | all-to-all | bytes 3538944 | tf_op jit(solution)/shard_map/all_to_all | solution.py:403
  57.9 2.1 %collective-permute-start.5 = (bf16[32,216,128]{2,1,0:T(8,128)(2,1)S(1)}, bf16[32,216,128]{2,1,0:T(8,128)(2,1)S(1)}, u32[]{:S(2)}, u32[]{:S(2)}) collective-permute-start(bf16[32,216,128]{2,1,0:T(8,128)(2,1)S(1)} %all_to_all.15.main), channel_id=1, source_target_pairs={{0,1},{1,2},{2,3},{3,0},{4,68},{5,69},{6,70},{7,71},{8,9},{9,10},{... | collective-permute-start | bytes 5308424 | tf_op jit(solution)/shard_map/ppermute | solution.py:399
  60.1 2.0 %collective-permute-start.3 = (bf16[32,216,128]{2,1,0:T(8,128)(2,1)S(1)}, bf16[32,216,128]{2,1,0:T(8,128)(2,1)S(1)}, u32[]{:S(2)}, u32[]{:S(2)}) collective-permute-start(bf16[32,216,128]{2,1,0:T(8,128)(2,1)S(1)} %all_to_all.15.main), channel_id=1, source_target_pairs={{0,3},{1,0},{2,1},{3,2},{4,196},{5,197},{6,198},{7,199},{8,11},{9,... | collective-permute-start | bytes 5308424 | tf_op jit(solution)/shard_map/ppermute | solution.py:399
  62.1 18.8 %all_to_all.16.last = bf16[32,48,128]{2,1,0:T(8,128)(2,1)S(1)} all-to-all(bf16[32,48,128]{2,1,0:T(8,128)(2,1)S(1)} %get-tuple-element.18), channel_id=1, replica_groups={{0,8,16,24,32,40,48,56,64,72,80,88,96,104,112,120,128,136,144,152,160,1..., dimensions={0} | all-to-all | bytes 786432 | tf_op jit(solution)/shard_map/all_to_all | solution.py:403
  80.9 0.0 collective-permute-start.6
  80.9 2.7 %collective-permute-start.4 = (bf16[32,48,128]{2,1,0:T(8,128)(2,1)S(1)}, bf16[32,48,128]{2,1,0:T(8,128)(2,1)S(1)}, u32[]{:S(2)}, u32[]{:S(2)}) collective-permute-start(bf16[32,48,128]{2,1,0:T(8,128)(2,1)S(1)} %all_to_all.16.last), channel_id=1, source_target_pairs={{0,3},{1,0},{2,1},{3,2},{4,196},{5,197},{6,198},{7,199},{8,11},{9,... | collective-permute-start | bytes 1179656 | tf_op jit(solution)/shard_map/ppermute | solution.py:399
  83.6 1.7 %own.1 = (f32[8,128]{1,0:T(8,128)S(1)}, bf16[96,512]{1,0:T(8,128)(2,1)S(1)}, f32[32,512]{1,0:T(8,128)S(1)}) custom-call(bf16[32,216,128]{2,1,0:T(8,128)(2,1)S(1)} %all_to_all.15.main, bf16[32,48,128]{2,1,0:T(8,128)(2,1)S(1)} %all_to_all.16.last, s32[2,512]{1,0:T(2,128)S(1)} %get-tuple-element.21.plan_ref), custom_call_target="tpu_custom_call" | custom-call | tf_op jit(solution)/shard_map/own/pallas_call | solution.py:422
  85.3 0.0 collective-permute-done.5.before.before_main
  85.3 0.0 collective-permute-done.3.after.after_main
  85.3 3.3 %start.1 = (f32[1024,1024]{1,0:T(8,128)S(1)}, f32[512,1024]{1,0:T(8,128)S(1)}) custom-call(s32[4]{0:T(128)S(1)} %pad_add_fusion.spot_ref, bf16[32,216,128]{2,1,0:T(8,128)(2,1)S(1)} %all_to_all.15.main, bf16[32,216,128]{2,1,0:T(8,128)(2,1)S(1)} %collective-permute-done.3.after.after_main, bf16[32,216,128]{2,1,0:T(8,128)(2,1)S(1)} %collective-permute-done.5.before.before_main), custom_call_target="tpu_custom_call" | custom-call | tf_op jit(solution)/shard_map/start/pallas_call | solution.py:422
  88.6 0.4 collective-permute-done.6.before_last
  89.0 0.0 collective-permute-done.4.after_last
  89.0 2.1 %cross.1 = f32[256,128]{1,0:T(8,128)S(1)} custom-call(s32[4]{0:T(128)S(1)} %pad_add_fusion.spot_ref, bf16[32,216,128]{2,1,0:T(8,128)(2,1)S(1)} %all_to_all.15.main, bf16[32,48,128]{2,1,0:T(8,128)(2,1)S(1)} %all_to_all.16.last, bf16[32,216,128]{2,1,0:T(8,128)(2,1)S(1)} %collective-permute-done.3.after.after_main, ...), custom_call_target="tpu_custom_call" | custom-call | tf_op jit(solution)/shard_map/cross/pallas_call | solution.py:422
  91.2 24.3 %all_to_all.17 = f32[256,1,1,128]{3,2,1,0:T(1,128)S(1)} all-to-all(f32[256,1,1,128]{3,2,1,0:T(1,128)S(1)} %bitcast.11), channel_id=1, replica_groups=mesh['ingest'=64,'span'=4] {'ingest','span'}, dimensions={0} | all-to-all | bytes 262144 | tf_op jit(solution)/shard_map/all_to_all | solution.py:500
  115.5 1.4 %fetch.1 = f32[1,512]{1,0:T(1,128)} custom-call(s32[4]{0:T(128)S(1)} %pad_add_fusion.spot_ref, f32[256,128]{1,0:T(8,128)S(1)} %bitcast.12, bf16[96,512]{1,0:T(8,128)(2,1)S(1)} %get-tuple-element.23.onehot_ref, f32[32,512]{1,0:T(8,128)S(1)} %get-tuple-element.24.pick_ref), custom_call_target="tpu_custom_call" | custom-call | tf_op jit(solution)/shard_map/fetch/pallas_call | solution.py:422
Async XLA Ops:
  0.0 6.7 %collective-permute-start = (bf16[512,1024]{1,0:T(8,128)(2,1)}, bf16[512,1024]{1,0:T(8,128)(2,1)S(1)}, u32[]{:S(2)}, u32[]{:S(2)}) collective-permute-start(bf16[512,1024]{1,0:T(8,128)(2,1)} %refs_0_.1), channel_id=1, source_target_pairs={{0,4},{1,5},{2,6},{3,7},{4,0},{5,1},{6,2},{7,3},{8,12},{9,13},{10,... | collective-permute-start | bytes 3145736 | tf_op jit(solution)/shard_map/ppermute | solution.py:399
  3.2 3.5 %collective-permute-start.1 = (s32[1,512]{1,0:T(1,128)}, s32[1,512]{1,0:T(1,128)S(1)}, u32[]{:S(2)}, u32[]{:S(2)}) collective-permute-start(s32[1,512]{1,0:T(1,128)} %bitcast.13), channel_id=1, source_target_pairs={{0,4},{1,5},{2,6},{3,7},{4,0},{5,1},{6,2},{7,3},{8,12},{9,13},{10,... | collective-permute-start | bytes 6152 | tf_op jit(solution)/shard_map/ppermute | solution.py:399
  3.2 3.5 %collective-permute-start.2 = (s32[1,512]{1,0:T(1,128)}, s32[1,512]{1,0:T(1,128)S(1)}, u32[]{:S(2)}, u32[]{:S(2)}) collective-permute-start(s32[1,512]{1,0:T(1,128)} %bitcast.15), channel_id=1, source_target_pairs={{0,4},{1,5},{2,6},{3,7},{4,0},{5,1},{6,2},{7,3},{8,12},{9,13},{10,... | collective-permute-start | bytes 6152 | tf_op jit(solution)/shard_map/ppermute | solution.py:399
  57.9 27.3 %collective-permute-start.5 = (bf16[32,216,128]{2,1,0:T(8,128)(2,1)S(1)}, bf16[32,216,128]{2,1,0:T(8,128)(2,1)S(1)}, u32[]{:S(2)}, u32[]{:S(2)}) collective-permute-start(bf16[32,216,128]{2,1,0:T(8,128)(2,1)S(1)} %all_to_all.15.main), channel_id=1, source_target_pairs={{0,1},{1,2},{2,3},{3,0},{4,68},{5,69},{6,70},{7,71},{8,9},{9,10},{... | collective-permute-start | bytes 5308424 | tf_op jit(solution)/shard_map/ppermute | solution.py:399
  60.1 25.2 %collective-permute-start.3 = (bf16[32,216,128]{2,1,0:T(8,128)(2,1)S(1)}, bf16[32,216,128]{2,1,0:T(8,128)(2,1)S(1)}, u32[]{:S(2)}, u32[]{:S(2)}) collective-permute-start(bf16[32,216,128]{2,1,0:T(8,128)(2,1)S(1)} %all_to_all.15.main), channel_id=1, source_target_pairs={{0,3},{1,0},{2,1},{3,2},{4,196},{5,197},{6,198},{7,199},{8,11},{9,... | collective-permute-start | bytes 5308424 | tf_op jit(solution)/shard_map/ppermute | solution.py:399
  80.9 8.1 %collective-permute-start.6 = (bf16[32,48,128]{2,1,0:T(8,128)(2,1)S(1)}, bf16[32,48,128]{2,1,0:T(8,128)(2,1)S(1)}, u32[]{:S(2)}, u32[]{:S(2)}) collective-permute-start(bf16[32,48,128]{2,1,0:T(8,128)(2,1)S(1)} %all_to_all.16.last), channel_id=1, source_target_pairs={{0,1},{1,2},{2,3},{3,0},{4,68},{5,69},{6,70},{7,71},{8,9},{9,10},{... | collective-permute-start | bytes 1179656 | tf_op jit(solution)/shard_map/ppermute | solution.py:399
  80.9 8.1 %collective-permute-start.4 = (bf16[32,48,128]{2,1,0:T(8,128)(2,1)S(1)}, bf16[32,48,128]{2,1,0:T(8,128)(2,1)S(1)}, u32[]{:S(2)}, u32[]{:S(2)}) collective-permute-start(bf16[32,48,128]{2,1,0:T(8,128)(2,1)S(1)} %all_to_all.16.last), channel_id=1, source_target_pairs={{0,3},{1,0},{2,1},{3,2},{4,196},{5,197},{6,198},{7,199},{8,11},{9,... | collective-permute-start | bytes 1179656 | tf_op jit(solution)/shard_map/ppermute | solution.py:399
